TPU v7x, 32 devices: a whole 2x2x4 slice. The times are simulated.
32 devices in a mesh: expert: 8 (over z, y), dp: 4 (over x, core).
Axes of the slice: x: 2, y: 2, z: 4, core: 2. Of those that a mesh axis runs over, the one named last changes fastest.
Arguments:
- grad_rows: bfloat16 [4, 4096, 2048], P('dp', 'expert'), may hold values from -6 to 6
- counts: int32 [4, 8, 8], P('dp', 'expert'), may hold values from 0 to 80, as said below
- order: int32 [4, 4096], P('dp', 'expert'), may hold values from 0 to 511, as said below
- hidden: bfloat16 [4, 8, 640, 768], P('dp', 'expert'), may hold values from -0.29882812 to 0.29882812
- down_weight: bfloat16 [8, 768, 2048], P('expert'), may hold values from -0.21875 to 0.21875
- error_in: bfloat16 [4, 8, 768, 2048], P('dp', 'expert'), may hold values from -6 to 6
- q_init: bfloat16 [8, 2048, 64], P('expert'), may hold values from -6 to 6
Outputs:
- input_grad: bfloat16 [4, 4096, 768], P('dp', 'expert')
- p_basis: float32 [8, 768, 64], P('expert')
- q_factor: float32 [8, 2048, 64], P('expert')
- error_out: bfloat16 [4, 8, 768, 2048], P('dp', 'expert')
Inputs may be any that keep to these rules, and one draw needn't show every extreme that they name: On each device (r, s) the 8 counts sum to 512; in every draw one expert receives exactly 80 rows from every device. `order`: each device's 512 entries are a permutation of 0 to 511.
All inputs are finite; a program needn't handle non-finite values.
Results may differ from a plain program's by a relative error of at most 0.001.
Values may be sent and summed in bfloat16 or wider, within the bound.
No kernel may reach another device: no remote copies, remote signals or barrier semaphores. Data moves between devices by JAX's collectives and lax.ppermute only.
A program may use at most 128 MiB of HBM per device.

v0:
```python
import jax
import jax.numpy as jnp
from jax import lax
from jax.sharding import PartitionSpec as P


def orthonormal_rows(p_rows, gram):
    lower = jnp.linalg.cholesky(gram)
    return lax.linalg.triangular_solve(lower, p_rows, left_side=False, lower=True, transpose_a=True)


def shards(grad_rows, counts, order, hidden, down_weight, error_in, q_init):
    local_rows = grad_rows[0]
    route_count = counts[0, 0]
    order_local = order[0]
    experts = route_count.shape[0]
    total_rows = local_rows.shape[0]
    width = local_rows.shape[1]
    saved_hidden = hidden[0, 0]
    hidden_units = saved_hidden.shape[1]
    capacity = saved_hidden.shape[0] // experts
    expert_weight = down_weight[0]
    route_ends = jnp.cumsum(route_count)
    route_starts = route_ends - route_count
    slot_ids = jnp.arange(capacity, dtype=jnp.int32)
    pick_index = jnp.minimum(route_starts[:, None] + slot_ids[None, :], total_rows - 1)
    slot_valid = slot_ids[None, :] < route_count[:, None]
    outgoing = local_rows[pick_index.reshape(-1)].reshape(experts, capacity, width)
    outgoing = jnp.where(slot_valid[:, :, None], outgoing, jnp.zeros((), jnp.bfloat16))
    arrived = lax.all_to_all(outgoing, "expert", split_axis=0, concat_axis=0, tiled=True)
    returned = lax.all_to_all(
        jnp.einsum(
            "ncd,fd->ncf", arrived, expert_weight, preferred_element_type=jnp.float32
        ).astype(jnp.bfloat16),
        "expert",
        split_axis=0,
        concat_axis=0,
        tiled=True,
    )
    arrived_flat = arrived.reshape(experts * capacity, width)
    grad_w = lax.dot_general(
        saved_hidden, arrived_flat, (((0,), (0,)), ((), ())), preferred_element_type=jnp.float32
    )
    moment = grad_w + error_in[0, 0].astype(jnp.float32)
    q_start = q_init[0].astype(jnp.float32)
    partial_p = jnp.dot(moment, q_start, precision=lax.Precision.HIGHEST)
    p_total = lax.psum(partial_p, "dp")
    p_basis = orthonormal_rows(
        p_total, jnp.dot(p_total.T, p_total, precision=lax.Precision.HIGHEST)
    )
    partial_q = lax.dot_general(
        moment, p_basis, (((0,), (0,)), ((), ())), precision=lax.Precision.HIGHEST
    )
    replicas = lax.axis_size("dp")
    q_factor = lax.psum(partial_q, "dp") / replicas
    approximation = jnp.dot(p_basis, q_factor.T, precision=lax.Precision.HIGHEST)
    error_new = (moment - approximation).astype(jnp.bfloat16)
    returned_flat = returned.reshape(experts * capacity, hidden_units)
    expert_of = jnp.sum((route_ends[None, :] <= order_local[:, None]).astype(jnp.int32), axis=1)
    expert_ids = jnp.arange(experts, dtype=jnp.int32)
    onehot = (expert_of[:, None] == expert_ids[None, :]).astype(jnp.int32)
    row_base = jnp.sum(onehot * (expert_ids * capacity - route_starts)[None, :], axis=1)
    position = row_base + order_local
    input_grad = returned_flat[position]
    return (input_grad[None], p_basis[None], q_factor[None], error_new[None, None])


def solution(mesh):
    placed = (
        P("dp", "expert", None),
        P("dp", "expert", None),
        P("dp", "expert"),
        P("dp", "expert", None, None),
        P("expert", None, None),
        P("dp", "expert", None, None),
        P("expert", None, None),
    )
    return jax.shard_map(
        shards,
        mesh=mesh,
        in_specs=placed,
        out_specs=(
            P("dp", "expert", None),
            P("expert", None, None),
            P("expert", None, None),
            P("dp", "expert", None, None),
        ),
        check_vma=False,
    )
```

profile of v0, /device:TPU:0, one launch (start us, length us, event | category | flops | bytes accessed | tf_op | source)
XLA Modules:
  0.0 215.6 jit_solution(2620371014982569518)
XLA Ops:
  7.2 1.0 reduce-window.7
  8.2 0.7 multiply_subtract_fusion
  9.0 0.7 iota_compare_fusion.3
  9.7 8.8 %gather_fusion = bf16[640,2048]{1,0:T(8,128)(2,1)} fusion(bf16[512,2048]{1,0:T(8,128)(2,1)} %bitcast.59, s32[1024]{0:T(1024)S(1)} %pad_clamp_fusion.1), kind=kCustom, calls=%fused_computation | custom fusion | bytes 5245440 | tf_op jit(solution)/shard_map/gather | solution.py:28
  18.5 3.5 %broadcast_select_fusion = bf16[8,80,2048]{2,1,0:T(8,128)(2,1)} fusion(bf16[8,80,2048]{2,1,0:T(8,128)(2,1)} %bitcast.60, pred[8,80]{1,0:T(8,128)(4,1)S(1)} %iota_compare_fusion.3), kind=kLoop, calls=%fused_computation.7 | loop fusion | flops 1310720 | bytes 5243520 | tf_op jit(solution)/shard_map/jit(_where)/select_n | solution.py:29
  22.0 7.3 %all-to-all-start = ((bf16[8,80,2048]{2,1,0:T(8,128)(2,1)}), bf16[8,80,2048]{2,1,0:T(8,128)(2,1)}, u32[]{:S(2)}, u32[]{:S(2)}) async-start(bf16[8,80,2048]{2,1,0:T(8,128)(2,1)} %broadcast_select_fusion), calls=%async_computation | async-start | bytes 5242880 | tf_op jit(solution)/shard_map/all_to_all | solution.py:30
  29.3 4.6 %copy.19 = bf16[1,1,768,2048]{2,3,1,0:T(8,128)(2,1)} copy(bf16[1,1,768,2048]{3,2,1,0:T(8,128)(2,1)} %param.12) | data formatting | bytes 6291456 | tf_op args[5]
  34.2 54.7 %all-to-all-done = bf16[8,80,2048]{2,1,0:T(8,128)(2,1)} async-done(((bf16[8,80,2048]{2,1,0:T(8,128)(2,1)}), bf16[8,80,2048]{2,1,0:T(8,128)(2,1)}, u32[]{:S(2)}, u32[]{:S(2)}) %all-to-all-start) | async-done | bytes 2621472 | tf_op jit(solution)/shard_map/all_to_all | solution.py:30
  88.9 5.8 %convert_add_fusion = f32[768,2048]{0,1:T(8,128)S(1)} fusion(bf16[640,2048]{1,0:T(8,128)(2,1)} %bitcast.13, bf16[1,1,768,2048]{2,3,1,0:T(8,128)(2,1)} %copy.19, bf16[1,1,640,768]{3,2,1,0:T(8,128)(2,1)} %param.10), kind=kOutput, calls=%fused_computation.2 | convolution fusion | flops 2016411648 | bytes 13041664 | tf_op jit(solution)/shard_map/dot_general | solution.py:41
  94.7 2.7 %copy-done.1 = f32[768,2048]{0,1:T(8,128)} copy-done((f32[768,2048]{0,1:T(8,128)}, f32[768,2048]{0,1:T(8,128)S(1)}, u32[]{:S(2)}) %copy-start.1) | copy-done | bytes 6291480
  97.3 3.2 %fusion.8 = f32[768,64]{0,1:T(8,128)} fusion(f32[768,2048]{0,1:T(8,128)S(1)} %convert_add_fusion, bf16[1,2048,64]{1,2,0:T(8,128)(2,1)S(1)} %copy-done.3), kind=kOutput, calls=%fused_computation.12 | convolution fusion | flops 1207959552 | bytes 6750208 | tf_op jit(solution)/shard_map/dot_general | solution.py:46
  100.5 4.9 %fusion.3 = bf16[8,80,768]{2,1,0:T(8,128)(2,1)} fusion(bf16[8,80,2048]{2,1,0:T(8,128)(2,1)} %all-to-all-done, bf16[1,768,2048]{2,1,0:T(8,128)(2,1)S(1)} %copy-done), kind=kOutput, calls=%fused_computation.8 | convolution fusion | flops 2013757440 | bytes 6750208 | tf_op jit(solution)/shard_map/ncd,fd->ncf/dot_general | solution.py:32
  105.5 4.2 %all-to-all-start.1 = ((bf16[8,80,768]{2,1,0:T(8,128)(2,1)}), bf16[8,80,768]{2,1,0:T(8,128)(2,1)}, u32[]{:S(2)}, u32[]{:S(2)}) async-start(bf16[8,80,768]{2,1,0:T(8,128)(2,1)} %fusion.3), calls=%async_computation.1 | async-start | bytes 1966080 | tf_op jit(solution)/shard_map/all_to_all | solution.py:31
  109.9 21.5 %all-reduce.3.cloned.1.call-done = f32[768,64]{0,1:T(8,128)} async-done(((f32[768,64]{0,1:T(8,128)}), f32[768,64]{0,1:T(8,128)}) %all-reduce.3.cloned.1.call-update) | async-done | bytes 196624 | tf_op jit(solution)/shard_map/psum | solution.py:47
  131.4 1.3 fusion.17
  132.8 5.8 %cholesky.16 = f32[64,64]{1,0:T(8,128)S(1)} custom-call(f32[64,64]{1,0:T(8,128)S(1)} %fusion.14), custom_call_target="Cholesky" | custom-call | tf_op jit(solution)/shard_map/jit(cholesky)/cholesky | solution.py:8
  140.0 4.9 %custom-call.6 = f32[1,64,64]{1,2,0:T(8,128)S(1)} custom-call(f32[1,64,64]{2,1,0:T(8,128)S(1)} %fusion.11), custom_call_target="InvertDiagBlocksLowerTriangular" | custom-call | tf_op jit(solution)/shard_map/triangular_solve | solution.py:9
  144.9 1.3 fusion.12
  146.2 9.8 %fusion.18 = f32[2048,64]{0,1:T(8,128)} fusion(f32[768,2048]{0,1:T(8,128)} %copy-done.1, f32[768,64]{0,1:T(8,128)S(1)} %fusion.12), kind=kOutput, calls=%fused_computation.40 | convolution fusion | flops 1207959552 | bytes 7012352 | tf_op jit(solution)/shard_map/dot_general | solution.py:51
  156.1 33.3 %all-reduce.5.cloned.1.call-done = f32[2048,64]{0,1:T(8,128)} async-done(((f32[2048,64]{0,1:T(8,128)}), f32[2048,64]{0,1:T(8,128)}) %all-reduce.5.cloned.1.call-update) | async-done | bytes 524304 | tf_op jit(solution)/shard_map/psum | solution.py:55
  189.4 8.5 %fusion.2 = bf16[1,1,768,2048]{2,3,1,0:T(8,128)(2,1)} fusion(f32[768,2048]{0,1:T(8,128)} %copy-done.1, f32[768,64]{0,1:T(8,128)S(1)} %fusion.12, f32[2048,64]{0,1:T(8,128)} %all-reduce.5.cloned.1.call-done), kind=kOutput, calls=%fused_computation.6 | convolution fusion | flops 1211236352 | bytes 10158080 | tf_op jit(solution)/shard_map/dot_general | solution.py:56
  197.9 4.6 %copy.22 = bf16[1,1,768,2048]{3,2,1,0:T(8,128)(2,1)} copy(bf16[1,1,768,2048]{2,3,1,0:T(8,128)(2,1)} %fusion.2) | data formatting | bytes 6291456
  202.5 1.9 multiply_bitcast_fusion
  204.4 4.4 %gather_fusion.1 = bf16[512,768]{1,0:T(8,128)(2,1)} fusion(bf16[640,768]{1,0:T(8,128)(2,1)} %bitcast.7, s32[1024]{0:T(1024)S(1)} %pad_clamp_fusion), kind=kCustom, calls=%fused_computation.1 | custom fusion | bytes 1574912 | tf_op jit(solution)/shard_map/gather | solution.py:64
  (27 shorter events, 2.1 us)
Async XLA Ops:
  7.2 93.4 %copy-start = (bf16[1,768,2048]{2,1,0:T(8,128)(2,1)S(1)}, bf16[1,768,2048]{2,1,0:T(8,128)(2,1)}, u32[]{:S(2)}) copy-start(bf16[1,768,2048]{2,1,0:T(8,128)(2,1)} %param.11) | copy-start | bytes 9437188
  22.0 66.9 %all-to-all-start = ((bf16[8,80,2048]{2,1,0:T(8,128)(2,1)}), bf16[8,80,2048]{2,1,0:T(8,128)(2,1)}, u32[]{:S(2)}, u32[]{:S(2)}) async-start(bf16[8,80,2048]{2,1,0:T(8,128)(2,1)} %broadcast_select_fusion), calls=%async_computation | async-start | bytes 5242880 | tf_op jit(solution)/shard_map/all_to_all | solution.py:30
  29.3 4.7 %copy-start.4 = (s32[1,512]{1,0:T(1,128)S(1)}, s32[1,512]{1,0:T(1,128)}, u32[]{:S(2)}) copy-start(s32[1,512]{1,0:T(1,128)} %param.9) | copy-start | bytes 6148
  29.3 102.1 %all-reduce.3.cloned.1.call-start = ((), (), s32[]{:S(2)}) async-start(), calls=%async_computation.2 | async-start | bytes 393216 | tf_op jit(solution)/shard_map/psum | solution.py:47
  88.9 8.5 %copy-start.3 = (bf16[1,2048,64]{1,2,0:T(8,128)(2,1)S(1)}, bf16[1,2048,64]{1,2,0:T(8,128)(2,1)}, u32[]{:S(2)}) copy-start(bf16[1,2048,64]{1,2,0:T(8,128)(2,1)} %param.13) | copy-start | bytes 786436
  94.7 2.7 %copy-start.1 = (f32[768,2048]{0,1:T(8,128)}, f32[768,2048]{0,1:T(8,128)S(1)}, u32[]{:S(2)}) copy-start(f32[768,2048]{0,1:T(8,128)S(1)} %convert_add_fusion) | copy-start | bytes 18874372
  105.5 98.9 %all-to-all-start.1 = ((bf16[8,80,768]{2,1,0:T(8,128)(2,1)}), bf16[8,80,768]{2,1,0:T(8,128)(2,1)}, u32[]{:S(2)}, u32[]{:S(2)}) async-start(bf16[8,80,768]{2,1,0:T(8,128)(2,1)} %fusion.3), calls=%async_computation.1 | async-start | bytes 1966080 | tf_op jit(solution)/shard_map/all_to_all | solution.py:31
  109.7 79.7 %all-reduce.5.cloned.1.call-start = ((), (), s32[]{:S(2)}) async-start(), calls=%async_computation.3 | async-start | bytes 1048576 | tf_op jit(solution)/shard_map/psum | solution.py:55
  146.2 43.2 %copy-start.2 = (f32[768,64]{0,1:T(8,128)}, f32[768,64]{0,1:T(8,128)S(1)}, u32[]{:S(2)}) copy-start(f32[768,64]{0,1:T(8,128)S(1)} %fusion.12) | copy-start | bytes 589828
Sparse Core Ops, SparseCore 0:
  100.6 30.7 all-reduce.2
  156.2 33.1 all-reduce.4
where the time goes:
time: 216 us
  waiting for transfers between devices  110 us (51%)
  matrix products  34.8 us (16%)
  local copies, waits for them, and re-layouts  25.3 us (12%)
  other arithmetic  20.1 us (9%)
  between operations  14.2 us (7%)
  starting transfers between devices  11.8 us (5%)
    all_to_all x1, waiting for transfers between devices, shards(): lax.all_to_all(outgoing, 'expert', split_axis=0, concat_axis=0, tiled=True)  54.7 us
    psum x1, waiting for transfers between devices, shards(): q_factor = lax.psum(partial_q, 'dp') / replicas  33.3 us
    psum x1, waiting for transfers between devices, shards(): p_total = lax.psum(partial_p, 'dp')  21.5 us
    unnamed x12, local copies, waits for them, and re-layouts  11.9 us
    dot_general x1, matrix products, shards(): lax.dot_general(moment, p_basis, (((0,), (0,)), ((), ())), precision=lax....  9.81 us
    gather x1, local copies, waits for them, and re-layouts, shards(): local_rows[pick_index.reshape(-1)].reshape(experts, capacity, width)  8.78 us
    dot_general x1, matrix products, shards(): jnp.dot(p_basis, q_factor.T, precision=lax.Precision.HIGHEST)  8.46 us
    all_to_all x1, starting transfers between devices, shards(): lax.all_to_all(outgoing, 'expert', split_axis=0, concat_axis=0, tiled=True)  7.28 us
  transfers between devices with their start and end apart: 4, of which 3 were waited for; matrix products, arithmetic and copies ran while one was open for 23% of the time, Pallas kernels for 0%

commit v1 on v0

v1 whole, which is shorter than its diff:
```python
import functools

import jax
import jax.numpy as jnp
from jax import lax
from jax.experimental import pallas as pl
from jax.experimental.pallas import tpu as pltpu
from jax.sharding import PartitionSpec as P

F32 = jnp.float32
BF16 = jnp.bfloat16
ROW_TILE = 16
COLS = 512
MIB = 1024 * 1024
FULL = 58


def whole_vmem():
    return pl.BlockSpec(memory_space=pltpu.VMEM)


def split3(x):
    hi = x.astype(BF16)
    rest = x - hi.astype(F32)
    mid = rest.astype(BF16)
    lo = (rest - mid.astype(F32)).astype(BF16)
    return hi, mid, lo


def stack3(x):
    return jnp.concatenate(split3(x), axis=0)


def fold3(x):
    n = x.shape[0] // 3
    return x[:n] + (x[n : 2 * n] + x[2 * n :])


def dot_nt(a, b):
    return lax.dot_general(a, b, (((1,), (1,)), ((), ())), preferred_element_type=F32)


def dot_nn(a, b):
    return jnp.dot(a, b, preferred_element_type=F32)


def full_dot(a, b):
    return jnp.dot(a, b, precision=lax.Precision.HIGHEST, preferred_element_type=F32)

def in_hbm():
    return pl.BlockSpec(memory_space=pltpu.HBM)


TOKEN = ((8, 128), F32)


def set_token(ref):
    ref[...] = jnp.zeros(ref.shape, ref.dtype)


def cost(flops, nbytes):
    return pl.CostEstimate(flops=flops, bytes_accessed=nbytes, transcendentals=0)


def call(kernel, name, scalars, operands, outs, scratch=(), limit=12, flops=10**9, nbytes=10**6, specs=None, out_specs=None):
    outs = [jax.ShapeDtypeStruct(shape, dtype) for shape, dtype in outs]
    return pl.pallas_call(
        kernel,
        grid_spec=pltpu.PrefetchScalarGridSpec(
            num_scalar_prefetch=len(scalars),
            grid=(),
            in_specs=specs or [whole_vmem()] * len(operands),
            out_specs=out_specs or [whole_vmem()] * len(outs),
            scratch_shapes=list(scratch),
        ),
        out_shape=outs,
        compiler_params=pltpu.CompilerParams(vmem_limit_bytes=limit * MIB),
        cost_estimate=cost(flops, nbytes),
        name=name,
    )(*scalars, *operands)


def pack_kernel(n, cap, masks, me_ref, core_ref, counts_hbm, rows_hbm, *rest):
    outs = rest[: len(masks)]
    counts_ref, rows_ref, held, sems, out_sems = rest[len(masks) :]
    total = rows_ref.shape[0]
    window = -(-(cap + ROW_TILE - 1) // ROW_TILE) * ROW_TILE
    copy_counts = pltpu.make_async_copy(counts_hbm, counts_ref, sems.at[0])
    copy_rows = pltpu.make_async_copy(rows_hbm, rows_ref, sems.at[1])
    copy_counts.start()
    copy_rows.start()
    copy_counts.wait()
    j = lax.broadcasted_iota(jnp.int32, (cap, window), 0)
    w = lax.broadcasted_iota(jnp.int32, (cap, window), 1)
    bases, picks = [], []
    for mask in masks:
        dest = me_ref[0] ^ mask
        start = jnp.int32(0)
        for e in range(n):
            start = start + jnp.where(e < dest, counts_ref[0, e], 0)
        base = jnp.minimum((start // ROW_TILE) * ROW_TILE, total - window)
        bases.append(pl.multiple_of(base, ROW_TILE))
        hit = (w == j + (start - base)) & (j < counts_ref[0, dest])
        picks.append(jnp.where(hit, 1.0, 0.0).astype(BF16))
    copy_rows.wait()
    if len(masks) == 1:
        outs[0][...] = dot_nn(picks[0], rows_ref[pl.ds(bases[0], window), :]).astype(BF16)
        return
    copies = []
    for k, (base, pick) in enumerate(zip(bases, picks)):
        held[k] = dot_nn(pick, rows_ref[pl.ds(base, window), :]).astype(BF16)
        copies.append(pltpu.make_async_copy(held.at[k], outs[k], out_sems.at[k]))
        copies[k].start()
    for copy in copies:
        copy.wait()


def pack(me, core, counts, rows, n, cap, masks, nbytes, out_spec, limit):
    count, width = len(masks), rows.shape[1]
    return call(
        functools.partial(pack_kernel, n, cap, masks),
        "pack_rows",
        (me, core),
        (counts, rows),
        [((cap, width), BF16)] * count,
        [
            pltpu.SMEM(counts.shape, jnp.int32),
            pltpu.VMEM(rows.shape, BF16),
            pltpu.VMEM((count, cap, width), BF16),
            pltpu.SemaphoreType.DMA((2,)),
            pltpu.SemaphoreType.DMA((count,)),
        ],
        specs=[in_hbm()] * 2,
        out_specs=[out_spec] * count,
        limit=limit,
        flops=10**6,
        nbytes=nbytes,
    )


def source_at(me_ref, slot, cap):
    if slot is None:
        return 0
    return pl.multiple_of((me_ref[0] ^ slot) * cap, ROW_TILE)


def place(chunks, slots, me_ref, hidden_ref, both_ref, at):
    cap, width = chunks[0].shape
    for k, slot in enumerate(slots):
        rows = pl.ds(at + k * cap, cap)
        both_ref[rows, :width] = chunks[k][...]
        both_ref[rows, width:] = hidden_ref[pl.ds(source_at(me_ref, slot, cap), cap), :]


def p_term(q, rows, hidden):
    return fold3(dot_nn(stack3(dot_nt(q, rows)), hidden))


def early_kernel(slots, me_ref, q_ref, hidden_ref, error_ref, weight_ref, *rest):
    chunks = rest[: len(slots)]
    p_ref, both_ref, moment_ref, *slot_refs = rest[len(slots) :]
    cap = chunks[0].shape[0]
    width = error_ref.shape[1]
    place(chunks, slots, me_ref, hidden_ref, both_ref, 0)
    q = q_ref[...]
    p_ref[...] = dot_nt(q, error_ref[...]) + p_term(q, both_ref[:, :width], both_ref[:, width:])
    hidden_t = both_ref[:, width:].T
    for j in range(0, width, COLS):
        block = dot_nn(hidden_t, both_ref[:, j : j + COLS])
        moment_ref[:, j : j + COLS] = error_ref[:, j : j + COLS].astype(F32) + block
    res = dot_nt(both_ref[:, :width], weight_ref[...]).astype(BF16)
    for k, ref in enumerate(slot_refs):
        ref[...] = res[k * cap : (k + 1) * cap]


def early_part(me, q, hidden, error, weight, chunks, slots):
    cap, width = chunks[0].shape
    ff = hidden.shape[1]
    rows = cap * len(slots)
    return call(
        functools.partial(early_kernel, slots),
        "early_rows",
        (me,),
        (q, hidden, error, weight, *chunks),
        [((q.shape[0], ff), F32), ((rows, width + ff), BF16), ((ff, width), F32)]
        + [((cap, ff), BF16)] * len(slots),
        flops=2 * 10**9,
        nbytes=10**7,
    )


def late_kernel(slots, me_ref, q_ref, hidden_ref, base_ref, *rest):
    chunks, (p_ref, both_ref) = rest[: len(slots)], rest[len(slots) :]
    width = chunks[0].shape[1]
    place(chunks, slots, me_ref, hidden_ref, both_ref, 0)
    p_ref[...] = base_ref[...] + p_term(q_ref[...], both_ref[:, :width], both_ref[:, width:])


def late_part(me, q, hidden, base, chunks, slots):
    cap, width = chunks[0].shape
    ff = hidden.shape[1]
    return call(
        functools.partial(late_kernel, slots),
        "late_rows",
        (me,),
        (q, hidden, base, *chunks),
        [((q.shape[0], ff), F32), ((cap * len(slots), width + ff), BF16)],
        flops=10**6,
        nbytes=10**4,
    )


def slot_kernel(at, count, both_ref, weight_ref, *rest):
    outs = rest[len(rest) - count :]
    cap, width = outs[0].shape[0], weight_ref.shape[1]
    res = dot_nt(both_ref[at : at + cap * count, :width], weight_ref[...]).astype(BF16)
    for k, out in enumerate(outs):
        out[...] = res[k * cap : (k + 1) * cap]


def slot_grads(both, weight, before, at, cap, count, flops):
    return call(
        functools.partial(slot_kernel, at, count),
        "slot_grads",
        (),
        (both, weight, *before),
        [((cap, weight.shape[0]), BF16)] * count,
        flops=flops,
        nbytes=10**4,
    )


def s_kernel(core_ref, pa_ref, pb_ref, error_ref, *rest):
    *groups, p_out, send_ref, keep_ref, token_ref = rest
    set_token(token_ref)
    total = pa_ref[...] + pb_ref[...]
    p_out[...] = total
    p3 = stack3(total)
    width = error_ref.shape[1]
    half = width // 2
    ys = [stack3(fold3(dot_nt(p3, group[:, width:]))) for group in groups]
    for out, part in ((send_ref, 1 - core_ref[0]), (keep_ref, core_ref[0])):
        for j in range(0, half, COLS):
            cols = pl.ds(pl.multiple_of(part * half + j, COLS), COLS)
            res = dot_nn(p3, error_ref[:, cols])
            for y, group in zip(ys, groups):
                res = res + dot_nn(y, group[:, cols])
            out[:, j : j + COLS] = fold3(res)


def s_partial(core, pa, pb, error, groups):
    rank, ff = pa.shape
    width = error.shape[1]
    return call(
        s_kernel,
        "s_partial",
        (core,),
        (pa, pb, error, *groups),
        [((rank, ff), F32), ((rank, width // 2), F32), ((rank, width // 2), F32), TOKEN],
        nbytes=7 * 10**6,
    )


def basis_kernel(p_ref, before_ref, basis_ref, linv_ref, left_ref):
    p = p_ref[...]
    rank = p.shape[0]
    p3 = stack3(p)
    gram_rows = fold3(dot_nt(p3, p3))
    gram = gram_rows[:, :rank] + (gram_rows[:, rank : 2 * rank] + gram_rows[:, 2 * rank :])
    row = lax.broadcasted_iota(jnp.int32, (rank, rank), 0)
    col = lax.broadcasted_iota(jnp.int32, (rank, rank), 1)
    eye = jnp.where(row == col, 1.0, 0.0)
    aug = jnp.concatenate([gram, eye], axis=1)
    sub, group = 8, 4
    shape = (sub, 2 * rank)
    blocks = [aug[b * sub : (b + 1) * sub] for b in range(rank // sub)]
    sub_id = lax.broadcasted_iota(jnp.int32, shape, 0)
    for k in range(0, rank, group):
        kb, kr = divmod(k, sub)
        spread = {
            (b, i): jnp.broadcast_to(blocks[b][:, k + i : k + i + 1], shape)
            for b in range(kb, rank // sub)
            for i in range(group)
        }
        low, scale, pivots = {}, [], []
        for i in range(group):
            for j in range(i + 1):
                left = jnp.broadcast_to(spread[kb, j][kr + i : kr + i + 1], shape)
                for m in range(j):
                    left = left - low[i, m] * low[j, m]
                low[i, j] = left * scale[j] if j < i else left
            scale.append(lax.rsqrt(low[i, i]))
            pivot = jnp.broadcast_to(blocks[kb][kr + i : kr + i + 1], shape)
            for m in range(i):
                pivot = pivot - low[i, m] * pivots[m]
            pivots.append(pivot * scale[i])
        for b in range(kb, rank // sub):
            updated, factors = blocks[b], []
            for i in range(group):
                factor = spread[b, i]
                for m in range(i):
                    factor = factor - factors[m] * low[i, m]
                factors.append(factor * scale[i])
                updated = updated - factors[i] * pivots[i]
            if b == kb:
                updated = jnp.where(sub_id >= kr + group, updated, blocks[b])
                for i in range(group):
                    updated = jnp.where(sub_id == kr + i, pivots[i], updated)
            blocks[b] = updated
    linv = jnp.concatenate(blocks, axis=0)[:, rank:]
    linv_ref[...] = linv
    basis = full_dot(linv, p)
    basis_ref[...] = basis
    hi, mid, lo = split3(basis)
    left_ref[...] = jnp.concatenate([hi, hi, mid, mid, hi, lo], axis=0).T


def basis_of(p, before):
    rank, ff = p.shape
    return call(
        basis_kernel,
        "basis",
        (),
        (p, before),
        [((rank, ff), F32), ((rank, rank), F32), ((ff, 6 * rank), BF16)],
        flops=10**10,
    )


def moment_kernel(before_ref, moment_ref, both_ref, out_ref):
    width = out_ref.shape[1]
    hidden_t = both_ref[:, width:].T
    for j in range(0, width, COLS):
        cols = slice(j, j + COLS)
        out_ref[:, cols] = moment_ref[:, cols] + dot_nn(hidden_t, both_ref[:, cols])


def moment_add(before, moment, both):
    return call(
        moment_kernel,
        "moment_add",
        (),
        (before, moment, both),
        [(moment.shape, F32)],
        nbytes=10**7,
    )[0]


def q_kernel(replicas, mine_ref, far_ref, linv_ref, out_ref):
    out_ref[...] = full_dot(linv_ref[...], mine_ref[...] + far_ref[...]) * (1.0 / replicas)


def q_half(mine, far, linv, replicas):
    return call(functools.partial(q_kernel, replicas), "q_half", (), (mine, far, linv), [(mine.shape, F32)])[0]


def error_block(part, k, block, q_ref, left_ref, moment_ref, right):
    rank, half = q_ref.shape
    here = pl.ds(k * block, block)
    cols = pl.ds(pl.multiple_of(part * half + k * block, block), block)
    hi, mid, lo = split3(-q_ref[:, here])
    for i, piece in enumerate((hi, mid, hi, mid, lo, hi)):
        right[i * rank : (i + 1) * rank, here] = piece
    return (moment_ref[:, cols] + dot_nn(left_ref[...], right[:, here])).astype(BF16)


def error_first_kernel(block, core_ref, q_ref, left_ref, moment_ref, out_ref, right):
    for k in range(q_ref.shape[1] // block):
        here = pl.ds(k * block, block)
        out_ref[:, here] = error_block(core_ref[0], k, block, q_ref, left_ref, moment_ref, right)


def error_first(core, q, left, moment):
    half = q.shape[1]
    return call(
        functools.partial(error_first_kernel, 256),
        "new_error_first",
        (core,),
        (q, left, moment),
        [((moment.shape[0], half), BF16)],
        [pltpu.VMEM((left.shape[1], half), BF16)],
        flops=10**10,
    )[0]


def error_second_kernel(block, core_ref, mine_ref, other_ref, left_ref, moment_ref, first_ref, *rest):
    q_hbm, out_hbm, token_ref, right, held, sems = rest
    set_token(token_ref)
    half = mine_ref.shape[1]
    part = 1 - core_ref[0]
    at_mine = pl.ds(pl.multiple_of(core_ref[0] * half, half), half)
    at_other = pl.ds(pl.multiple_of(part * half, half), half)
    copies = [
        pltpu.make_async_copy(first_ref, out_hbm.at[:, at_mine], sems.at[0]),
        pltpu.make_async_copy(mine_ref, q_hbm.at[:, at_mine], sems.at[1]),
        pltpu.make_async_copy(other_ref, q_hbm.at[:, at_other], sems.at[2]),
    ]
    for copy in copies:
        copy.start()
    for k in range(half // block):
        here = pl.ds(k * block, block)
        cols = pl.ds(pl.multiple_of(part * half + k * block, block), block)
        held[:, here] = error_block(part, k, block, other_ref, left_ref, moment_ref, right)
        copies.append(pltpu.make_async_copy(held.at[:, here], out_hbm.at[:, cols], sems.at[3 + k]))
        copies[-1].start()
    for copy in copies:
        copy.wait()


def error_second(core, mine, other, left, moment, first):
    ff, width = moment.shape
    rank, half = mine.shape
    block = 256
    return call(
        functools.partial(error_second_kernel, block),
        "new_error_second",
        (core,),
        (mine, other, left, moment, first),
        [((rank, width), F32), ((ff, width), BF16), TOKEN],
        [
            pltpu.VMEM((left.shape[1], half), BF16),
            pltpu.VMEM((ff, half), BF16),
            pltpu.SemaphoreType.DMA((3 + half // block,)),
        ],
        out_specs=[in_hbm(), in_hbm(), whole_vmem()],
        flops=10**10,
    )


def pick_kernel(n, cap, masks, me_ref, counts_ref, order_ref, out_ref, held):
    order = order_ref[...]
    j = lax.broadcasted_iota(jnp.int32, (cap, order.shape[1]), 0)
    for k, mask in enumerate(masks):
        expert = me_ref[0] ^ mask
        start = jnp.int32(0)
        for e in range(n):
            start = start + jnp.where(e < expert, counts_ref[e], 0)
        hit = (order == j + start) & (j < counts_ref[expert])
        held[k * cap : (k + 1) * cap, :] = jnp.where(hit, 1.0, 0.0)
    out_ref[...] = held[...].T.astype(BF16)


def pick_of(me, counts, order, n, cap, masks):
    tokens = order.shape[1]
    slots = len(masks) * cap
    return call(
        functools.partial(pick_kernel, n, cap, masks),
        "pick_rows",
        (me, counts),
        (order,),
        [((tokens, slots), BF16)],
        [pltpu.VMEM((slots, tokens), F32)],
        flops=10**6,
        nbytes=10**4,
    )[0]


def unpack_first_kernel(count, before_ref, pick_ref, *rest):
    chunks, (out_ref, token_ref, cat) = rest[:count], rest[count:]
    cap = chunks[0].shape[0]
    for k in range(count):
        cat[k * cap : (k + 1) * cap, :] = chunks[k][...]
    out_ref[...] = dot_nn(pick_ref[...], cat[...]).astype(BF16)
    set_token(token_ref)


def unpack_first(before, pick, chunks):
    cap, ff = chunks[0].shape
    return call(
        functools.partial(unpack_first_kernel, len(chunks)),
        "unpack_first",
        (),
        (before, pick, *chunks),
        [((pick.shape[0], ff), BF16), TOKEN],
        [pltpu.VMEM((len(chunks) * cap, ff), BF16)],
        flops=10**10,
    )


def unpack_kernel(count, parts, token_ref, pick_ref, first_ref, *rest):
    chunks, (out_hbm, cat, out_ref, sems) = rest[:count], rest[count:]
    cap = chunks[0].shape[0]
    for k in range(count):
        cat[k * cap : (k + 1) * cap, :] = chunks[k][...]
    rows = out_ref.shape[0] // parts
    copies = []
    for k in range(parts):
        at = pl.ds(k * rows, rows)
        out_ref[at, :] = first_ref[at, :] + dot_nn(pick_ref[at, :], cat[...]).astype(BF16)
        copies.append(pltpu.make_async_copy(out_ref.at[at, :], out_hbm.at[at, :], sems.at[k]))
        copies[k].start()
    for copy in copies:
        copy.wait()


def unpack(token, pick, first, chunks):
    cap, ff = chunks[0].shape
    tokens, slots = pick.shape
    parts = 2
    return pl.pallas_call(
        functools.partial(unpack_kernel, len(chunks), parts),
        in_specs=[whole_vmem()] * (3 + len(chunks)),
        out_specs=in_hbm(),
        out_shape=jax.ShapeDtypeStruct((tokens, ff), BF16),
        scratch_shapes=[
            pltpu.VMEM((slots, ff), BF16),
            pltpu.VMEM((tokens, ff), BF16),
            pltpu.SemaphoreType.DMA((parts,)),
        ],
        compiler_params=pltpu.CompilerParams(vmem_limit_bytes=8 * MIB),
        cost_estimate=cost(10**6, 10**4),
        name="unpack_rows",
    )(token, pick, first, *chunks)


def pack_plain(route_count, local_rows, experts, capacity):
    total_rows, width = local_rows.shape
    route_starts = jnp.cumsum(route_count) - route_count
    slot_ids = jnp.arange(capacity, dtype=jnp.int32)
    pick_index = jnp.minimum(route_starts[:, None] + slot_ids[None, :], total_rows - 1)
    slot_valid = slot_ids[None, :] < route_count[:, None]
    outgoing = local_rows[pick_index.reshape(-1)].reshape(experts, capacity, width)
    return jnp.where(slot_valid[:, :, None], outgoing, jnp.zeros((), BF16))


def unpack_plain(route_count, order_local, returned, experts, capacity):
    route_ends = jnp.cumsum(route_count)
    route_starts = route_ends - route_count
    expert_of = jnp.sum((route_ends[None, :] <= order_local[:, None]).astype(jnp.int32), axis=1)
    row_base = jnp.arange(experts, dtype=jnp.int32) * capacity - route_starts
    return returned[row_base[expert_of] + order_local]


def add_kernel(a_ref, b_ref, *rest):
    rest[-1][...] = a_ref[...] + b_ref[...]


def add(a, b, *before):
    return call(add_kernel, "add", (), (a, b, *before), [(a.shape, F32)], limit=4, flops=10**6)[0]


def pass_kernel(x_ref, before_ref, out_ref):
    out_ref[...] = x_ref[...]


def pass_on(x, before):
    return call(pass_kernel, "pass_on", (), (x, before), [(x.shape, x.dtype)], limit=4, flops=10**6)[0]


def shards(n_expert, n_dp, grad_rows, counts, order, hidden, down_weight, error_in, q_init):
    rows = grad_rows[0]
    count = counts[0, 0]
    saved = hidden[0, 0]
    weight = down_weight[0]
    error = error_in[0, 0]
    q = q_init[0].T
    ff = saved.shape[1]
    capacity = saved.shape[0] // n_expert
    me = lax.axis_index("expert").astype(jnp.int32)[None]
    core = (lax.axis_index("dp").astype(jnp.int32) & 1)[None]
    core_pairs = [(d, d ^ 1) for d in range(n_dp)]
    chip_pairs = [(d, d ^ 2) for d in range(n_dp)]
    by_pairs = n_expert == 8 and capacity % ROW_TILE == 0

    if by_pairs:
        far = tuple(reversed(range(n_expert // 2, n_expert)))
        near = tuple(reversed(range(0, n_expert // 2)))
        first, last = far[:1] + near, far[1:]

        def swap(x, mask):
            return lax.ppermute(x, "expert", [(e, e ^ mask) for e in range(n_expert)])

        others = far[1:] + near
        packed = {far[0]: pack(me, core, counts[0], rows, n_expert, capacity, far[:1], 4 * 10**6, whole_vmem(), 62)[0]}
        packed.update(zip(others, pack(me, core, counts[0], rows, n_expert, capacity, others, 10**4, in_hbm(), FULL)))
        arrived = {m: swap(packed[m], m) if m else packed[m] for m in far + near}
        pick_near = pick_of(me, count, order, n_expert, capacity, near)
        pick_far = pick_of(me, count, order, n_expert, capacity, far)
        p_first, both_first, moment, *back = early_part(
            me, q, saved, error, weight, [arrived[m] for m in first], first
        )
        back_near = [swap(x, m) if m else x for x, m in zip(back[1:], near)]
        p_mine, both_last = late_part(me, q, saved, p_first, [arrived[m] for m in last], last)
        back_next = slot_grads(
            both_last, weight, (pick_near, pick_far, *back_near), 0, capacity, len(last), 10**10
        )
        before, groups = back_next[:1], [both_first, both_last]
    else:
        outgoing = pack_plain(count, rows, n_expert, capacity)
        arrived = lax.all_to_all(outgoing, "expert", split_axis=0, concat_axis=0, tiled=True)
        arrived = arrived.reshape(n_expert * capacity, rows.shape[1])
        p_mine, both_first, moment, back = early_part(me, q, saved, error, weight, [arrived], (None,))
        before, groups = [], [both_first]
        back = back.reshape(n_expert, capacity, ff)
        returned = lax.all_to_all(back, "expert", split_axis=0, concat_axis=0, tiled=True)
        returned = returned.reshape(n_expert * capacity, ff)
    p_chip = add(p_mine, lax.ppermute(p_mine, "dp", core_pairs), *before)
    p_far = lax.ppermute(p_chip, "dp", chip_pairs)
    p_total, s_send, s_keep, token = s_partial(core, p_chip, p_far, error, groups)
    if by_pairs:
        grad_near, token = unpack_first(token, pick_near, back_near)
    s_half = add(s_keep, lax.ppermute(s_send, "dp", core_pairs), token)
    if by_pairs:
        back_last = pass_on(back_next[-1], s_half)
        back_far = [swap(x, m) for x, m in zip([back[0], *back_next[:-1], back_last], far)]
        moment = moment_add(back_last, moment, both_last)
    basis, linv, left = basis_of(p_total, moment)
    q_mine = q_half(s_half, lax.ppermute(s_half, "dp", chip_pairs), linv, n_dp)
    q_other = lax.ppermute(q_mine, "dp", core_pairs)
    first_half = error_first(core, q_mine, left, moment)
    q_factor, error_out, token = error_second(core, q_mine, q_other, left, moment, first_half)
    if by_pairs:
        input_grad = unpack(token, pick_far, grad_near, back_far)
    else:
        input_grad = unpack_plain(count, order[0], returned, n_expert, capacity)
    return (input_grad[None], basis.T[None], q_factor.T[None], error_out[None, None])


def solution(mesh):
    placed = (
        P("dp", "expert", None),
        P("dp", "expert", None),
        P("dp", "expert"),
        P("dp", "expert", None, None),
        P("expert", None, None),
        P("dp", "expert", None, None),
        P("expert", None, None),
    )
    return jax.shard_map(
        functools.partial(shards, mesh.shape["expert"], mesh.shape["dp"]),
        mesh=mesh,
        in_specs=placed,
        out_specs=(
            P("dp", "expert", None),
            P("expert", None, None),
            P("expert", None, None),
            P("dp", "expert", None, None),
        ),
        check_vma=False,
    )
```

time: 216 us -> 96.2 us (0.45)
  waiting for transfers between devices: 110 us -> 29.5 us
  matrix products: 34.8 us -> 0 us
  Pallas kernels: 0 us -> 26.5 us
  starting transfers between devices: 11.8 us -> 34.3 us
  local copies, waits for them, and re-layouts: 25.3 us -> 4.78 us
  other arithmetic: 20.1 us -> 0 us
  between operations: 14.2 us -> 0.87 us
    psum x2 -> x0, waiting for transfers between devices: 54.8 us -> none  [the longest x1 33.3 us: shards(): q_factor = lax.psum(partial_q, 'dp') / replicas]
    all_to_all x2 -> x0, waiting for transfers between devices: 54.7 us -> none  [the longest x1 54.7 us: shards(): lax.all_to_all(outgoing, 'expert', split_axis=0, concat_axis=0, tiled=True)]
    ppermute x0 -> x19, starting transfers between devices: none -> 34.3 us  [the longest x14 30.9 us: swap(): return lax.ppermute(x, 'expert', [(e, e ^ mask) for e in range(n_expert)])]
    dot_general x6 -> x0, matrix products: 33.5 us -> none  [the longest x1 9.81 us: shards(): lax.dot_general(moment, p_basis, (((0,), (0,)), ((), ())), precision=lax....]
    ppermute x0 -> x19, waiting for transfers between devices: none -> 29.5 us  [the longest x14 25.6 us: swap(): return lax.ppermute(x, 'expert', [(e, e ^ mask) for e in range(n_expert)])]
    pallas_call x0 -> x18, Pallas kernels: none -> 26.5 us  [the longest x17 25.2 us: call(): pl.pallas_call(kernel, grid_spec=pltpu.PrefetchScalarGridSpec(num_scalar_...]
    gather x2 -> x0, local copies, waits for them, and re-layouts: 13.2 us -> none  [the longest x1 8.78 us: shards(): local_rows[pick_index.reshape(-1)].reshape(experts, capacity, width)]
    another operation x6 -> x0, other arithmetic: 13.1 us -> none  [the longest x3 6.52 us: orthonormal_rows(): lower = jnp.linalg.cholesky(gram)]
  transfers between devices with their start and end apart: 4 -> 19, of which waited for: 3 -> 11; matrix products, arithmetic and copies ran while one was open for 23% -> 0% of each run, Pallas kernels for 0% -> 23%
where the time goes in v1:
time: 96.2 us; the launch traced here: 95.9 us
  starting transfers between devices  34.3 us (36%)
  waiting for transfers between devices  29.5 us (31%)
  Pallas kernels  26.5 us (28%)
  local copies, waits for them, and re-layouts  4.78 us (5%)
    ppermute x14, starting transfers between devices, swap(): return lax.ppermute(x, 'expert', [(e, e ^ mask) for e in range(n_expert)])  30.9 us
    ppermute x14, waiting for transfers between devices, swap(): return lax.ppermute(x, 'expert', [(e, e ^ mask) for e in range(n_expert)])  25.6 us
    pallas_call x17, Pallas kernels, call(): pl.pallas_call(kernel, grid_spec=pltpu.PrefetchScalarGridSpec(num_scalar_...  25.2 us
    unnamed x18, local copies, waits for them, and re-layouts  4.78 us
  transfers between devices with their start and end apart: 19, of which 11 were waited for; matrix products, arithmetic and copies ran while one was open for 0% of the time, Pallas kernels for 23%

profile of v1, /device:TPU:0, one launch (start us, length us, event | category | flops | bytes accessed | tf_op | source)
XLA Modules:
  0.0 95.9 jit_solution(4132583241759841796)
XLA Ops:
  0.7 2.7 %pack_rows.2 = bf16[80,2048]{1,0:T(8,128)(2,1)} custom-call(s32[1]{0:T(128)} %bitcast.1.me_ref, s32[1]{0:T(128)} %bitcast.core_ref, s32[1,8]{1,0:T(1,128)} %bitcast.27, bf16[512,2048]{1,0:T(8,128)(2,1)} %bitcast.31), custom_call_target="tpu_custom_call" | custom-call | flops 1000000 | bytes 4000000 | tf_op jit(solution)/shard_map/pack_rows/pallas_call | solution.py:67
  3.3 6.1 %collective-permute-start = (bf16[80,2048]{1,0:T(8,128)(2,1)}, bf16[80,2048]{1,0:T(8,128)(2,1)S(1)}, u32[]{:S(2)}, u32[]{:S(2)}) collective-permute-start(bf16[80,2048]{1,0:T(8,128)(2,1)} %pack_rows.2), channel_id=1, source_target_pairs={{0,28},{4,24},{8,20},{12,16},{16,12},{20,8},{24,4},{28,0},{1,29},{... | collective-permute-start | bytes 983048 | tf_op jit(solution)/shard_map/ppermute | solution.py:571
  9.4 3.3 %pack_rows.3 = (bf16[80,2048]{1,0:T(8,128)(2,1)}, bf16[80,2048]{1,0:T(8,128)(2,1)}, bf16[80,2048]{1,0:T(8,128)(2,1)}, bf16[80,2048]{1,0:T(8,128)(2,1)}, bf16[80,...) custom-call(s32[1]{0:T(128)} %bitcast.1.me_ref, s32[1]{0:T(128)} %bitcast.core_ref, ...), custom_call_target="tpu_custom_call" | custom-call | flops 1000000 | bytes 10000 | tf_op jit(solution)/shard_map/pack_rows/pallas_call | solution.py:67
  12.8 2.0 %collective-permute-start.2 = (bf16[80,2048]{1,0:T(8,128)(2,1)}, bf16[80,2048]{1,0:T(8,128)(2,1)S(1)}, u32[]{:S(2)}, u32[]{:S(2)}) collective-permute-start(bf16[80,2048]{1,0:T(8,128)(2,1)} %get-tuple-element.37), channel_id=1, source_target_pairs={{0,8},{4,12},{8,0},{12,4},{16,24},{20,28},{24,16},{28,20},{1,9},{5... | collective-permute-start | bytes 983048 | tf_op jit(solution)/shard_map/ppermute | solution.py:571
  14.7 1.5 %collective-permute-start.3 = (bf16[80,2048]{1,0:T(8,128)(2,1)}, bf16[80,2048]{1,0:T(8,128)(2,1)S(1)}, u32[]{:S(2)}, u32[]{:S(2)}) collective-permute-start(bf16[80,2048]{1,0:T(8,128)(2,1)} %get-tuple-element.38), channel_id=1, source_target_pairs={{0,4},{4,0},{8,12},{12,8},{16,20},{20,16},{24,28},{28,24},{1,5},{5... | collective-permute-start | bytes 983048 | tf_op jit(solution)/shard_map/ppermute | solution.py:571
  16.5 1.8 %collective-permute-done.rest_0_ = bf16[80,2048]{1,0:T(8,128)(2,1)S(1)} collective-permute-done((bf16[80,2048]{1,0:T(8,128)(2,1)}, bf16[80,2048]{1,0:T(8,128)(2,1)S(1)}, u32[]{:S(2)}, u32[]{:S(2)}) %collective-permute-start) | collective-permute-done | bytes 327712 | tf_op jit(solution)/shard_map/ppermute | solution.py:571
  18.3 12.2 %collective-permute-start.5 = (bf16[80,2048]{1,0:T(8,128)(2,1)}, bf16[80,2048]{1,0:T(8,128)(2,1)S(1)}, u32[]{:S(2)}, u32[]{:S(2)}) collective-permute-start(bf16[80,2048]{1,0:T(8,128)(2,1)} %get-tuple-element.42), channel_id=1, source_target_pairs={{0,20},{4,16},{8,28},{12,24},{16,4},{20,0},{24,12},{28,8},{1,21},{... | collective-permute-start | bytes 983048 | tf_op jit(solution)/shard_map/ppermute | solution.py:571
  30.5 5.7 %collective-permute-done.2.rest_2_ = bf16[80,2048]{1,0:T(8,128)(2,1)S(1)} collective-permute-done((bf16[80,2048]{1,0:T(8,128)(2,1)}, bf16[80,2048]{1,0:T(8,128)(2,1)S(1)}, u32[]{:S(2)}, u32[]{:S(2)}) %collective-permute-start.2) | collective-permute-done | bytes 327712 | tf_op jit(solution)/shard_map/ppermute | solution.py:571
  36.2 1.9 %copy-done = bf16[1,1,768,2048]{3,2,1,0:T(8,128)(2,1)S(1)} copy-done((bf16[1,1,768,2048]{3,2,1,0:T(8,128)(2,1)S(1)}, bf16[1,1,768,2048]{3,2,1,0:T(8,128)(2,1)}, u32[]{:S(2)}) %copy-start) | copy-done | bytes 3145752
  38.1 1.9 %copy-done.3 = bf16[1,768,2048]{2,1,0:T(8,128)(2,1)S(1)} copy-done((bf16[1,768,2048]{2,1,0:T(8,128)(2,1)S(1)}, bf16[1,768,2048]{2,1,0:T(8,128)(2,1)}, u32[]{:S(2)}) %copy-start.3) | copy-done | bytes 3145752
  41.0 5.0 %early_rows.1 = (f32[64,768]{1,0:T(8,128)S(1)}, bf16[400,2816]{1,0:T(8,128)(2,1)S(1)}, f32[768,2048]{1,0:T(8,128)S(1)}, bf16[80,768]{1,0:T(8,128)(2,1)S(1)}, bf1...) custom-call(s32[1]{0:T(128)} %bitcast.1.me_ref, ...), custom_call_target="tpu_custom_call" | custom-call | flops 2000000000 | bytes 10000000 | tf_op jit(solution)/shard_map/early_rows/pallas_call | solution.py:67
  46.0 2.4 %collective-permute-start.8 = (bf16[80,768]{1,0:T(8,128)(2,1)S(1)}, bf16[80,768]{1,0:T(8,128)(2,1)S(1)}, u32[]{:S(2)}, u32[]{:S(2)}) collective-permute-start(bf16[80,768]{1,0:T(8,128)(2,1)S(1)} %get-tuple-element.46), channel_id=1, source_target_pairs={{0,12},{4,8},{8,4},{12,0},{16,28},{20,24},{24,20},{28,16},{1,13},{... | collective-permute-start | bytes 368648 | tf_op jit(solution)/shard_map/ppermute | solution.py:571
  48.5 1.4 %collective-permute-start.10 = (bf16[80,768]{1,0:T(8,128)(2,1)S(1)}, bf16[80,768]{1,0:T(8,128)(2,1)S(1)}, u32[]{:S(2)}, u32[]{:S(2)}) collective-permute-start(bf16[80,768]{1,0:T(8,128)(2,1)S(1)} %get-tuple-element.48), channel_id=1, source_target_pairs={{0,4},{4,0},{8,12},{12,8},{16,20},{20,16},{24,28},{28,24},{1,5},{5... | collective-permute-start | bytes 368648 | tf_op jit(solution)/shard_map/ppermute | solution.py:571
  51.4 11.2 %collective-permute-done.5.rest_1_ = bf16[80,2048]{1,0:T(8,128)(2,1)S(1)} collective-permute-done((bf16[80,2048]{1,0:T(8,128)(2,1)}, bf16[80,2048]{1,0:T(8,128)(2,1)S(1)}, u32[]{:S(2)}, u32[]{:S(2)}) %collective-permute-start.5) | collective-permute-done | bytes 327712 | tf_op jit(solution)/shard_map/ppermute | solution.py:571
  62.5 6.1 %collective-permute-done.6.rest_2_ = bf16[80,2048]{1,0:T(8,128)(2,1)S(1)} collective-permute-done((bf16[80,2048]{1,0:T(8,128)(2,1)}, bf16[80,2048]{1,0:T(8,128)(2,1)S(1)}, u32[]{:S(2)}, u32[]{:S(2)}) %collective-permute-start.6) | collective-permute-done | bytes 327712 | tf_op jit(solution)/shard_map/ppermute | solution.py:571
  70.9 1.6 %collective-permute-start.11 = (f32[64,768]{1,0:T(8,128)S(1)}, f32[64,768]{1,0:T(8,128)S(1)}, u32[]{:S(2)}, u32[]{:S(2)}) collective-permute-start(f32[64,768]{1,0:T(8,128)S(1)} %add.2.pa_ref), channel_id=1, source_target_pairs={{0,2},{1,3},{2,0},{3,1},{4,6},{5,7},{6,4},{7,5},{8,10},{9,11},{10,... | collective-permute-start | bytes 589832 | tf_op jit(solution)/shard_map/ppermute | solution.py:598
  72.5 1.9 %collective-permute-start.15 = (bf16[80,768]{1,0:T(8,128)(2,1)S(1)}, bf16[80,768]{1,0:T(8,128)(2,1)S(1)}, u32[]{:S(2)}, u32[]{:S(2)}) collective-permute-start(bf16[80,768]{1,0:T(8,128)(2,1)S(1)} %get-tuple-element.63), channel_id=1, source_target_pairs={{0,28},{4,24},{8,20},{12,16},{16,12},{20,8},{24,4},{28,0},{1,29},{... | collective-permute-start | bytes 368648 | tf_op jit(solution)/shard_map/ppermute | solution.py:571
  74.4 1.8 %collective-permute-start.16 = (bf16[80,768]{1,0:T(8,128)(2,1)S(1)}, bf16[80,768]{1,0:T(8,128)(2,1)S(1)}, u32[]{:S(2)}, u32[]{:S(2)}) collective-permute-start(bf16[80,768]{1,0:T(8,128)(2,1)S(1)} %get-tuple-element.50.rest_0_), channel_id=1, source_target_pairs={{0,24},{4,28},{8,16},{12,20},{16,8},{20,12},{24,0},{28,4},{1,25},{... | collective-permute-start | bytes 368648 | tf_op jit(solution)/shard_map/ppermute | solution.py:571
  76.1 1.8 %collective-permute-done.11.pb_ref = f32[64,768]{1,0:T(8,128)S(1)} collective-permute-done((f32[64,768]{1,0:T(8,128)S(1)}, f32[64,768]{1,0:T(8,128)S(1)}, u32[]{:S(2)}, u32[]{:S(2)}) %collective-permute-start.11) | collective-permute-done | bytes 196640 | tf_op jit(solution)/shard_map/ppermute | solution.py:598
  77.9 1.7 %s_partial.1 = (f32[64,768]{1,0:T(8,128)S(1)}, f32[64,1024]{1,0:T(8,128)S(1)}, f32[64,1024]{1,0:T(8,128)S(1)}, f32[8,128]{1,0:T(8,128)S(1)}) custom-call(s32[1]{0:T(128)} %bitcast.core_ref, f32[64,768]{1,0:T(8,128)S(1)} %add.2.pa_ref, f32[64,768]{1,0:T(8,128)S(1)} %collective-permute-done.11.pb_ref, bf16[768,2048]{1,0:T(8,128)(2,1)S(1)} %bitcast.20, ...), custom_call_target="tpu_custom_call" | custom-call | flops 1000000000 | bytes 7000000 | tf_op jit(solution)/shard_map/s_partial/pallas_call | solution.py:67
  81.3 1.6 %collective-permute-start.13 = (f32[64,1024]{1,0:T(8,128)S(1)}, f32[64,1024]{1,0:T(8,128)S(1)}, u32[]{:S(2)}, u32[]{:S(2)}) collective-permute-start(f32[64,1024]{1,0:T(8,128)S(1)} %add.3.before_ref.mine_ref), channel_id=1, source_target_pairs={{0,2},{1,3},{2,0},{3,1},{4,6},{5,7},{6,4},{7,5},{8,10},{9,11},{10,... | collective-permute-start | bytes 786440 | tf_op jit(solution)/shard_map/ppermute | solution.py:608
  85.2 4.2 %basis.1 = (f32[64,768]{1,0:T(8,128)}, f32[64,64]{1,0:T(8,128)S(1)}, bf16[768,384]{1,0:T(8,128)(2,1)S(1)}) custom-call(f32[64,768]{1,0:T(8,128)S(1)} %get-tuple-element.56.p_ref, f32[768,2048]{1,0:T(8,128)S(1)} %moment_add.1.before_ref.moment_ref), custom_call_target="tpu_custom_call" | custom-call | flops 10000000000 | bytes 1000000 | tf_op jit(solution)/shard_map/basis/pallas_call | solution.py:67
  91.7 2.0 %new_error_second.1 = (f32[64,2048]{1,0:T(8,128)}, bf16[768,2048]{1,0:T(8,128)(2,1)}, f32[8,128]{1,0:T(8,128)S(1)}) custom-call(s32[1]{0:T(128)} %bitcast.core_ref, f32[64,1024]{1,0:T(8,128)S(1)} %q_half.1.q_ref.mine_ref, f32[64,1024]{1,0:T(8,128)S(1)} %collective-permute-done.14.other_ref, bf16[768,384]{1,0:T(8,128)(2,1)S(1)} %get-tuple-element.60.left_ref, ...), custom_call_target="tpu_custom_call" | custom-call | flops 10000000000 | bytes 1000000 | tf_op jit(solution)/shard_map/new_error_second/pallas_call | solution.py:67
  94.6 1.3 %unpack_rows.1 = bf16[512,768]{1,0:T(8,128)(2,1)} custom-call(f32[8,128]{1,0:T(8,128)S(1)} %get-tuple-element.61.token_ref, bf16[512,320]{1,0:T(8,128)(2,1)S(1)} %pick_rows.3.rest_1_.pick_ref, bf16[512,768]{1,0:T(8,128)(2,1)S(1)} %get-tuple-element.62.first_ref, bf16[80,768]{1,0:T(8,128)(2,1)S(1)} %collective-permute-done.15.rest_0_, ...), custom_call_target="tpu_custom_call" | custom-call | flops 1000000 | bytes 10000 | tf_op jit(solution)/shard_map/unpack_rows/pallas_call | solution.py:500
  (50 shorter events, 12.1 us)
Async XLA Ops:
  0.6 35.6 %copy-start.5 = (bf16[1,2048,64]{1,2,0:T(8,128)(2,1)S(1)}, bf16[1,2048,64]{1,2,0:T(8,128)(2,1)}, u32[]{:S(2)}) copy-start(bf16[1,2048,64]{1,2,0:T(8,128)(2,1)} %param.13) | copy-start | bytes 786436
  0.6 35.6 %copy-start.2 = (bf16[1,1,640,768]{3,2,1,0:T(8,128)(2,1)S(1)}, bf16[1,1,640,768]{3,2,1,0:T(8,128)(2,1)}, u32[]{:S(2)}) copy-start(bf16[1,1,640,768]{3,2,1,0:T(8,128)(2,1)} %param.10) | copy-start | bytes 2949124
  3.3 14.9 %collective-permute-start = (bf16[80,2048]{1,0:T(8,128)(2,1)}, bf16[80,2048]{1,0:T(8,128)(2,1)S(1)}, u32[]{:S(2)}, u32[]{:S(2)}) collective-permute-start(bf16[80,2048]{1,0:T(8,128)(2,1)} %pack_rows.2), channel_id=1, source_target_pairs={{0,28},{4,24},{8,20},{12,16},{16,12},{20,8},{24,4},{28,0},{1,29},{... | collective-permute-start | bytes 983048 | tf_op jit(solution)/shard_map/ppermute | solution.py:571
  12.7 17.8 %collective-permute-start.1 = (bf16[80,2048]{1,0:T(8,128)(2,1)}, bf16[80,2048]{1,0:T(8,128)(2,1)S(1)}, u32[]{:S(2)}, u32[]{:S(2)}) collective-permute-start(bf16[80,2048]{1,0:T(8,128)(2,1)} %get-tuple-element.36), channel_id=1, source_target_pairs={{0,12},{4,8},{8,4},{12,0},{16,28},{20,24},{24,20},{28,16},{1,13},{... | collective-permute-start | bytes 983048 | tf_op jit(solution)/shard_map/ppermute | solution.py:571
  12.8 23.5 %collective-permute-start.2 = (bf16[80,2048]{1,0:T(8,128)(2,1)}, bf16[80,2048]{1,0:T(8,128)(2,1)S(1)}, u32[]{:S(2)}, u32[]{:S(2)}) collective-permute-start(bf16[80,2048]{1,0:T(8,128)(2,1)} %get-tuple-element.37), channel_id=1, source_target_pairs={{0,8},{4,12},{8,0},{12,4},{16,24},{20,28},{24,16},{28,20},{1,9},{5... | collective-permute-start | bytes 983048 | tf_op jit(solution)/shard_map/ppermute | solution.py:571
  14.7 21.5 %collective-permute-start.3 = (bf16[80,2048]{1,0:T(8,128)(2,1)}, bf16[80,2048]{1,0:T(8,128)(2,1)S(1)}, u32[]{:S(2)}, u32[]{:S(2)}) collective-permute-start(bf16[80,2048]{1,0:T(8,128)(2,1)} %get-tuple-element.38), channel_id=1, source_target_pairs={{0,4},{4,0},{8,12},{12,8},{16,20},{20,16},{24,28},{28,24},{1,5},{5... | collective-permute-start | bytes 983048 | tf_op jit(solution)/shard_map/ppermute | solution.py:571
  16.2 32.3 %collective-permute-start.4 = (bf16[80,2048]{1,0:T(8,128)(2,1)}, bf16[80,2048]{1,0:T(8,128)(2,1)S(1)}, u32[]{:S(2)}, u32[]{:S(2)}) collective-permute-start(bf16[80,2048]{1,0:T(8,128)(2,1)} %get-tuple-element.41), channel_id=1, source_target_pairs={{0,24},{4,28},{8,16},{12,20},{16,8},{20,12},{24,0},{28,4},{1,25},{... | collective-permute-start | bytes 983048 | tf_op jit(solution)/shard_map/ppermute | solution.py:571
  18.3 44.3 %collective-permute-start.5 = (bf16[80,2048]{1,0:T(8,128)(2,1)}, bf16[80,2048]{1,0:T(8,128)(2,1)S(1)}, u32[]{:S(2)}, u32[]{:S(2)}) collective-permute-start(bf16[80,2048]{1,0:T(8,128)(2,1)} %get-tuple-element.42), channel_id=1, source_target_pairs={{0,20},{4,16},{8,28},{12,24},{16,4},{20,0},{24,12},{28,8},{1,21},{... | collective-permute-start | bytes 983048 | tf_op jit(solution)/shard_map/ppermute | solution.py:571
  30.5 38.1 %collective-permute-start.6 = (bf16[80,2048]{1,0:T(8,128)(2,1)}, bf16[80,2048]{1,0:T(8,128)(2,1)S(1)}, u32[]{:S(2)}, u32[]{:S(2)}) collective-permute-start(bf16[80,2048]{1,0:T(8,128)(2,1)} %get-tuple-element.43), channel_id=1, source_target_pairs={{0,16},{4,20},{8,24},{12,28},{16,0},{20,4},{24,8},{28,12},{1,17},{... | collective-permute-start | bytes 983048 | tf_op jit(solution)/shard_map/ppermute | solution.py:571
  41.0 8.9 %copy-start.7 = (s32[1,512]{1,0:T(1,128)S(1)}, s32[1,512]{1,0:T(1,128)}, u32[]{:S(2)}) copy-start(s32[1,512]{1,0:T(1,128)} %order_ref.3) | copy-start | bytes 6148
  41.0 8.9 %copy-start.8 = (s32[1,1,8]{2,1,0:T(1,128)S(1)}, s32[1,1,8]{2,1,0:T(1,128)}, u32[]{:S(2)}) copy-start(s32[1,1,8]{2,1,0:T(1,128)} %param.8) | copy-start | bytes 100
  46.0 23.5 %copy-start.4 = (bf16[1,768,2048]{2,1,0:T(8,128)(2,1)S(1)}, bf16[1,768,2048]{2,1,0:T(8,128)(2,1)}, u32[]{:S(2)}) copy-start(bf16[1,768,2048]{2,1,0:T(8,128)(2,1)} %param.11) | copy-start | bytes 9437188
  46.0 23.4 %collective-permute-start.8 = (bf16[80,768]{1,0:T(8,128)(2,1)S(1)}, bf16[80,768]{1,0:T(8,128)(2,1)S(1)}, u32[]{:S(2)}, u32[]{:S(2)}) collective-permute-start(bf16[80,768]{1,0:T(8,128)(2,1)S(1)} %get-tuple-element.46), channel_id=1, source_target_pairs={{0,12},{4,8},{8,4},{12,0},{16,28},{20,24},{24,20},{28,16},{1,13},{... | collective-permute-start | bytes 368648 | tf_op jit(solution)/shard_map/ppermute | solution.py:571
  48.4 21.0 %collective-permute-start.9 = (bf16[80,768]{1,0:T(8,128)(2,1)S(1)}, bf16[80,768]{1,0:T(8,128)(2,1)S(1)}, u32[]{:S(2)}, u32[]{:S(2)}) collective-permute-start(bf16[80,768]{1,0:T(8,128)(2,1)S(1)} %get-tuple-element.47), channel_id=1, source_target_pairs={{0,8},{4,12},{8,0},{12,4},{16,24},{20,28},{24,16},{28,20},{1,9},{5... | collective-permute-start | bytes 368648 | tf_op jit(solution)/shard_map/ppermute | solution.py:571
  48.5 20.9 %collective-permute-start.10 = (bf16[80,768]{1,0:T(8,128)(2,1)S(1)}, bf16[80,768]{1,0:T(8,128)(2,1)S(1)}, u32[]{:S(2)}, u32[]{:S(2)}) collective-permute-start(bf16[80,768]{1,0:T(8,128)(2,1)S(1)} %get-tuple-element.48), channel_id=1, source_target_pairs={{0,4},{4,0},{8,12},{12,8},{16,20},{20,16},{24,28},{28,24},{1,5},{5... | collective-permute-start | bytes 368648 | tf_op jit(solution)/shard_map/ppermute | solution.py:571
  69.4 1.5 %collective-permute-start.7 = (f32[64,768]{1,0:T(8,128)S(1)}, f32[64,768]{1,0:T(8,128)S(1)}, u32[]{:S(2)}, u32[]{:S(2)}) collective-permute-start(f32[64,768]{1,0:T(8,128)S(1)} %get-tuple-element.44.a_ref), channel_id=1, source_target_pairs={{0,1},{1,0},{2,3},{3,2},{4,5},{5,4},{6,7},{7,6},{8,9},{9,8},{10,11... | collective-permute-start | bytes 589832 | tf_op jit(solution)/shard_map/ppermute | solution.py:597
  70.9 7.0 %collective-permute-start.11 = (f32[64,768]{1,0:T(8,128)S(1)}, f32[64,768]{1,0:T(8,128)S(1)}, u32[]{:S(2)}, u32[]{:S(2)}) collective-permute-start(f32[64,768]{1,0:T(8,128)S(1)} %add.2.pa_ref), channel_id=1, source_target_pairs={{0,2},{1,3},{2,0},{3,1},{4,6},{5,7},{6,4},{7,5},{8,10},{9,11},{10,... | collective-permute-start | bytes 589832 | tf_op jit(solution)/shard_map/ppermute | solution.py:598
  72.5 21.3 %collective-permute-start.15 = (bf16[80,768]{1,0:T(8,128)(2,1)S(1)}, bf16[80,768]{1,0:T(8,128)(2,1)S(1)}, u32[]{:S(2)}, u32[]{:S(2)}) collective-permute-start(bf16[80,768]{1,0:T(8,128)(2,1)S(1)} %get-tuple-element.63), channel_id=1, source_target_pairs={{0,28},{4,24},{8,20},{12,16},{16,12},{20,8},{24,4},{28,0},{1,29},{... | collective-permute-start | bytes 368648 | tf_op jit(solution)/shard_map/ppermute | solution.py:571
  74.4 19.7 %collective-permute-start.16 = (bf16[80,768]{1,0:T(8,128)(2,1)S(1)}, bf16[80,768]{1,0:T(8,128)(2,1)S(1)}, u32[]{:S(2)}, u32[]{:S(2)}) collective-permute-start(bf16[80,768]{1,0:T(8,128)(2,1)S(1)} %get-tuple-element.50.rest_0_), channel_id=1, source_target_pairs={{0,24},{4,28},{8,16},{12,20},{16,8},{20,12},{24,0},{28,4},{1,25},{... | collective-permute-start | bytes 368648 | tf_op jit(solution)/shard_map/ppermute | solution.py:571
  76.1 17.9 %collective-permute-start.17 = (bf16[80,768]{1,0:T(8,128)(2,1)S(1)}, bf16[80,768]{1,0:T(8,128)(2,1)S(1)}, u32[]{:S(2)}, u32[]{:S(2)}) collective-permute-start(bf16[80,768]{1,0:T(8,128)(2,1)S(1)} %get-tuple-element.64), channel_id=1, source_target_pairs={{0,20},{4,16},{8,28},{12,24},{16,4},{20,0},{24,12},{28,8},{1,21},{... | collective-permute-start | bytes 368648 | tf_op jit(solution)/shard_map/ppermute | solution.py:571
  79.7 1.6 %collective-permute-start.12 = (f32[64,1024]{1,0:T(8,128)S(1)}, f32[64,1024]{1,0:T(8,128)S(1)}, u32[]{:S(2)}, u32[]{:S(2)}) collective-permute-start(f32[64,1024]{1,0:T(8,128)S(1)} %get-tuple-element.53), channel_id=1, source_target_pairs={{0,1},{1,0},{2,3},{3,2},{4,5},{5,4},{6,7},{7,6},{8,9},{9,8},{10,11... | collective-permute-start | bytes 786440 | tf_op jit(solution)/shard_map/ppermute | solution.py:602
  81.3 8.4 %collective-permute-start.13 = (f32[64,1024]{1,0:T(8,128)S(1)}, f32[64,1024]{1,0:T(8,128)S(1)}, u32[]{:S(2)}, u32[]{:S(2)}) collective-permute-start(f32[64,1024]{1,0:T(8,128)S(1)} %add.3.before_ref.mine_ref), channel_id=1, source_target_pairs={{0,2},{1,3},{2,0},{3,1},{4,6},{5,7},{6,4},{7,5},{8,10},{9,11},{10,... | collective-permute-start | bytes 786440 | tf_op jit(solution)/shard_map/ppermute | solution.py:608
  82.9 11.7 %collective-permute-start.18 = (bf16[80,768]{1,0:T(8,128)(2,1)S(1)}, bf16[80,768]{1,0:T(8,128)(2,1)S(1)}, u32[]{:S(2)}, u32[]{:S(2)}) collective-permute-start(bf16[80,768]{1,0:T(8,128)(2,1)S(1)} %pass_on.1.before_ref), channel_id=1, source_target_pairs={{0,16},{4,20},{8,24},{12,28},{16,0},{20,4},{24,8},{28,12},{1,17},{... | collective-permute-start | bytes 368648 | tf_op jit(solution)/shard_map/ppermute | solution.py:571
  90.1 1.6 %collective-permute-start.14 = (f32[64,1024]{1,0:T(8,128)S(1)}, f32[64,1024]{1,0:T(8,128)S(1)}, u32[]{:S(2)}, u32[]{:S(2)}) collective-permute-start(f32[64,1024]{1,0:T(8,128)S(1)} %q_half.1.q_ref.mine_ref), channel_id=1, source_target_pairs={{0,1},{1,0},{2,3},{3,2},{4,5},{5,4},{6,7},{7,6},{8,9},{9,8},{10,11... | collective-permute-start | bytes 786440 | tf_op jit(solution)/shard_map/ppermute | solution.py:609
  (4 other events, 13.2 us)

commit v2 on v1

--- a/solution.py
+++ b/solution.py
@@ -230,33 +230,56 @@
     )
 
 
-def s_kernel(core_ref, pa_ref, pb_ref, error_ref, *rest):
-    *groups, p_out, send_ref, keep_ref, token_ref = rest
-    set_token(token_ref)
+def s_columns(part, p3, ys, error_ref, groups, out_ref):
+    half = out_ref.shape[1]
+    for j in range(0, half, COLS):
+        cols = pl.ds(pl.multiple_of(part * half + j, COLS), COLS)
+        res = dot_nn(p3, error_ref[:, cols])
+        for y, group in zip(ys, groups):
+            res = res + dot_nn(y, group[:, cols])
+        out_ref[:, j : j + COLS] = fold3(res)
+
+
+def s_send_kernel(count, core_ref, pa_ref, pb_ref, error_ref, *rest):
+    groups = rest[:count]
+    p_out, send_ref, p3_ref, *y_refs = rest[count:]
     total = pa_ref[...] + pb_ref[...]
     p_out[...] = total
-    p3 = stack3(total)
+    p3_ref[...] = stack3(total)
     width = error_ref.shape[1]
-    half = width // 2
-    ys = [stack3(fold3(dot_nt(p3, group[:, width:]))) for group in groups]
-    for out, part in ((send_ref, 1 - core_ref[0]), (keep_ref, core_ref[0])):
-        for j in range(0, half, COLS):
-            cols = pl.ds(pl.multiple_of(part * half + j, COLS), COLS)
-            res = dot_nn(p3, error_ref[:, cols])
-            for y, group in zip(ys, groups):
-                res = res + dot_nn(y, group[:, cols])
-            out[:, j : j + COLS] = fold3(res)
-
-
-def s_partial(core, pa, pb, error, groups):
+    for y_ref, group in zip(y_refs, groups):
+        y_ref[...] = stack3(fold3(dot_nt(p3_ref[...], group[:, width:])))
+    s_columns(1 - core_ref[0], p3_ref[...], [y[...] for y in y_refs], error_ref, groups, send_ref)
+
+
+def s_send(core, pa, pb, error, groups):
     rank, ff = pa.shape
     width = error.shape[1]
     return call(
-        s_kernel,
-        "s_partial",
+        functools.partial(s_send_kernel, len(groups)),
+        "s_send",
         (core,),
         (pa, pb, error, *groups),
-        [((rank, ff), F32), ((rank, width // 2), F32), ((rank, width // 2), F32), TOKEN],
+        [((rank, ff), F32), ((rank, width // 2), F32), ((3 * rank, ff), BF16)]
+        + [((3 * rank, group.shape[0]), BF16) for group in groups],
+        nbytes=7 * 10**6,
+    )
+
+
+def s_keep_kernel(count, core_ref, p3_ref, error_ref, *rest):
+    ys, groups, (keep_ref, token_ref) = rest[:count], rest[count : 2 * count], rest[2 * count :]
+    set_token(token_ref)
+    s_columns(core_ref[0], p3_ref[...], [y[...] for y in ys], error_ref, groups, keep_ref)
+
+
+def s_keep(core, p3, ys, error, groups):
+    rank = p3.shape[0] // 3
+    return call(
+        functools.partial(s_keep_kernel, len(groups)),
+        "s_keep",
+        (core,),
+        (p3, error, *ys, *groups),
+        [((rank, error.shape[1] // 2), F32), TOKEN],
         nbytes=7 * 10**6,
     )
 
@@ -342,7 +365,7 @@
         (),
         (before, moment, both),
         [(moment.shape, F32)],
-        nbytes=10**7,
+        flops=10**10,
     )[0]
 
 
@@ -383,9 +406,13 @@
     )[0]
 
 
-def error_second_kernel(block, core_ref, mine_ref, other_ref, left_ref, moment_ref, first_ref, *rest):
-    q_hbm, out_hbm, token_ref, right, held, sems = rest
-    set_token(token_ref)
+def last_kernel(block, parts, core_ref, mine_ref, other_ref, left_ref, moment_ref, first_ref, *rest):
+    count = len(rest) - (10 if parts else 5)
+    chunks = rest[2 : 2 + count] if parts else ()
+    near_ref, pick_ref = rest[:2] if parts else (None, None)
+    outs = rest[2 + count :] if parts else rest
+    q_hbm, out_hbm = outs[:2]
+    right, held, sems = outs[-3:]
     half = mine_ref.shape[1]
     part = 1 - core_ref[0]
     at_mine = pl.ds(pl.multiple_of(core_ref[0] * half, half), half)
@@ -397,32 +424,53 @@
     ]
     for copy in copies:
         copy.start()
-    for k in range(half // block):
+    steps = half // block
+    for k in range(steps):
         here = pl.ds(k * block, block)
         cols = pl.ds(pl.multiple_of(part * half + k * block, block), block)
         held[:, here] = error_block(part, k, block, other_ref, left_ref, moment_ref, right)
         copies.append(pltpu.make_async_copy(held.at[:, here], out_hbm.at[:, cols], sems.at[3 + k]))
         copies[-1].start()
+    if parts:
+        grad_hbm, cat, grad_ref = outs[2:5]
+        cap = chunks[0].shape[0]
+        for k in range(count):
+            cat[k * cap : (k + 1) * cap, :] = chunks[k][...]
+        rows = grad_ref.shape[0] // parts
+        for k in range(parts):
+            at = pl.ds(k * rows, rows)
+            grad_ref[at, :] = near_ref[at, :] + dot_nn(pick_ref[at, :], cat[...]).astype(BF16)
+            copies.append(pltpu.make_async_copy(grad_ref.at[at, :], grad_hbm.at[at, :], sems.at[3 + steps + k]))
+            copies[-1].start()
     for copy in copies:
         copy.wait()
 
 
-def error_second(core, mine, other, left, moment, first):
+def last_part(core, mine, other, left, moment, first, near=None, pick=None, chunks=()):
     ff, width = moment.shape
     rank, half = mine.shape
     block = 256
-    return call(
-        functools.partial(error_second_kernel, block),
-        "new_error_second",
+    parts = 2 if chunks else 0
+    operands = [mine, other, left, moment, first]
+    outs = [((rank, width), F32), ((ff, width), BF16)]
+    scratch = []
+    if chunks:
+        operands += [near, pick, *chunks]
+        outs.append((near.shape, BF16))
+        scratch = [pltpu.VMEM((pick.shape[1], ff), BF16), pltpu.VMEM(near.shape, BF16)]
+    scratch += [
+        pltpu.VMEM((left.shape[1], half), BF16),
+        pltpu.VMEM((ff, half), BF16),
+        pltpu.SemaphoreType.DMA((3 + half // block + parts,)),
+    ]
+    return call(
+        functools.partial(last_kernel, block, parts),
+        "new_error_last",
         (core,),
-        (mine, other, left, moment, first),
-        [((rank, width), F32), ((ff, width), BF16), TOKEN],
-        [
-            pltpu.VMEM((left.shape[1], half), BF16),
-            pltpu.VMEM((ff, half), BF16),
-            pltpu.SemaphoreType.DMA((3 + half // block,)),
-        ],
-        out_specs=[in_hbm(), in_hbm(), whole_vmem()],
+        operands,
+        outs,
+        scratch,
+        out_specs=[in_hbm()] * len(outs),
         flops=10**10,
     )
 
@@ -475,42 +523,6 @@
         [pltpu.VMEM((len(chunks) * cap, ff), BF16)],
         flops=10**10,
     )
-
-
-def unpack_kernel(count, parts, token_ref, pick_ref, first_ref, *rest):
-    chunks, (out_hbm, cat, out_ref, sems) = rest[:count], rest[count:]
-    cap = chunks[0].shape[0]
-    for k in range(count):
-        cat[k * cap : (k + 1) * cap, :] = chunks[k][...]
-    rows = out_ref.shape[0] // parts
-    copies = []
-    for k in range(parts):
-        at = pl.ds(k * rows, rows)
-        out_ref[at, :] = first_ref[at, :] + dot_nn(pick_ref[at, :], cat[...]).astype(BF16)
-        copies.append(pltpu.make_async_copy(out_ref.at[at, :], out_hbm.at[at, :], sems.at[k]))
-        copies[k].start()
-    for copy in copies:
-        copy.wait()
-
-
-def unpack(token, pick, first, chunks):
-    cap, ff = chunks[0].shape
-    tokens, slots = pick.shape
-    parts = 2
-    return pl.pallas_call(
-        functools.partial(unpack_kernel, len(chunks), parts),
-        in_specs=[whole_vmem()] * (3 + len(chunks)),
-        out_specs=in_hbm(),
-        out_shape=jax.ShapeDtypeStruct((tokens, ff), BF16),
-        scratch_shapes=[
-            pltpu.VMEM((slots, ff), BF16),
-            pltpu.VMEM((tokens, ff), BF16),
-            pltpu.SemaphoreType.DMA((parts,)),
-        ],
-        compiler_params=pltpu.CompilerParams(vmem_limit_bytes=8 * MIB),
-        cost_estimate=cost(10**6, 10**4),
-        name="unpack_rows",
-    )(token, pick, first, *chunks)
 
 
 def pack_plain(route_count, local_rows, experts, capacity):
@@ -584,6 +596,7 @@
         back_next = slot_grads(
             both_last, weight, (pick_near, pick_far, *back_near), 0, capacity, len(last), 10**10
         )
+        back_soon = pass_on(back[0], back_next[0])
         before, groups = back_next[:1], [both_first, both_last]
     else:
         outgoing = pack_plain(count, rows, n_expert, capacity)
@@ -596,22 +609,28 @@
         returned = returned.reshape(n_expert * capacity, ff)
     p_chip = add(p_mine, lax.ppermute(p_mine, "dp", core_pairs), *before)
     p_far = lax.ppermute(p_chip, "dp", chip_pairs)
-    p_total, s_send, s_keep, token = s_partial(core, p_chip, p_far, error, groups)
+    if by_pairs:
+        back_sent = [pass_on(x, p_chip) for x in back_next[:-1]]
+        moment = moment_add(back_sent[-1], moment, both_last)
+    p_total, s_sent, p3, *ys = s_send(core, p_chip, p_far, error, groups)
+    s_swapped = lax.ppermute(s_sent, "dp", core_pairs)
+    s_kept, token = s_keep(core, p3, ys, error, groups)
     if by_pairs:
         grad_near, token = unpack_first(token, pick_near, back_near)
-    s_half = add(s_keep, lax.ppermute(s_send, "dp", core_pairs), token)
+    s_half = add(s_kept, s_swapped, token)
     if by_pairs:
         back_last = pass_on(back_next[-1], s_half)
-        back_far = [swap(x, m) for x, m in zip([back[0], *back_next[:-1], back_last], far)]
-        moment = moment_add(back_last, moment, both_last)
-    basis, linv, left = basis_of(p_total, moment)
+        back_far = [swap(x, m) for x, m in zip([back_soon, *back_sent, back_last], far)]
+    basis, linv, left = basis_of(p_total, back_last if by_pairs else p_total)
     q_mine = q_half(s_half, lax.ppermute(s_half, "dp", chip_pairs), linv, n_dp)
     q_other = lax.ppermute(q_mine, "dp", core_pairs)
     first_half = error_first(core, q_mine, left, moment)
-    q_factor, error_out, token = error_second(core, q_mine, q_other, left, moment, first_half)
     if by_pairs:
-        input_grad = unpack(token, pick_far, grad_near, back_far)
+        q_factor, error_out, input_grad = last_part(
+            core, q_mine, q_other, left, moment, first_half, grad_near, pick_far, back_far
+        )
     else:
+        q_factor, error_out = last_part(core, q_mine, q_other, left, moment, first_half)
         input_grad = unpack_plain(count, order[0], returned, n_expert, capacity)
     return (input_grad[None], basis.T[None], q_factor.T[None], error_out[None, None])
 

time: 96.2 us -> 96.7 us (level)
  waiting for transfers between devices: 29.5 us -> 31.4 us
  starting transfers between devices: 34.3 us -> 33.2 us
    ppermute x1, waiting for transfers between devices: 0.23 us -> 2.57 us  [shards(): q_mine = q_half(s_half, lax.ppermute(s_half, 'dp', chip_pairs), linv, n_dp)]
    pallas_call x1 -> x0, Pallas kernels: 1.33 us -> none  [unpack(): pl.pallas_call(functools.partial(unpack_kernel, len(chunks), parts), in_s...]
    ppermute x14, starting transfers between devices: 30.9 us -> 29.9 us  [swap(): return lax.ppermute(x, 'expert', [(e, e ^ mask) for e in range(n_expert)])]
    pallas_call x17 -> x21, Pallas kernels: 25.2 us -> 26 us  [call(): pl.pallas_call(kernel, grid_spec=pltpu.PrefetchScalarGridSpec(num_scalar_...]
  transfers between devices with their start and end apart: 19 -> 19, of which waited for: 11 -> 8; matrix products, arithmetic and copies ran while one was open for 0% -> 0% of each run, Pallas kernels for 23% -> 22%
where the time goes in v2:
time: 96.7 us; the launch traced here: 96.4 us
  starting transfers between devices  33.2 us (34%)
  waiting for transfers between devices  31.4 us (32%)
  Pallas kernels  26 us (27%)
  local copies, waits for them, and re-layouts  4.78 us (5%)
  between operations  1.08 us (1%)
    ppermute x14, starting transfers between devices, swap(): return lax.ppermute(x, 'expert', [(e, e ^ mask) for e in range(n_expert)])  29.9 us
    ppermute x14, waiting for transfers between devices, swap(): return lax.ppermute(x, 'expert', [(e, e ^ mask) for e in range(n_expert)])  26.1 us
    pallas_call x21, Pallas kernels, call(): pl.pallas_call(kernel, grid_spec=pltpu.PrefetchScalarGridSpec(num_scalar_...  26 us
    unnamed x18, local copies, waits for them, and re-layouts  4.78 us
    ppermute x1, waiting for transfers between devices, shards(): q_mine = q_half(s_half, lax.ppermute(s_half, 'dp', chip_pairs), linv, n_dp)  2.57 us
    ppermute x1, waiting for transfers between devices, shards(): p_far = lax.ppermute(p_chip, 'dp', chip_pairs)  2.52 us
  transfers between devices with their start and end apart: 19, of which 8 were waited for; matrix products, arithmetic and copies ran while one was open for 0% of the time, Pallas kernels for 22%

profile of v2, /device:TPU:0, one launch (start us, length us, event | category | flops | bytes accessed | tf_op | source)
XLA Modules:
  0.0 96.4 jit_solution(13892725188403809121)
XLA Ops:
  0.7 2.7 %pack_rows.2 = bf16[80,2048]{1,0:T(8,128)(2,1)} custom-call(s32[1]{0:T(128)} %bitcast.1.me_ref, s32[1]{0:T(128)} %bitcast.core_ref, s32[1,8]{1,0:T(1,128)} %bitcast.28, bf16[512,2048]{1,0:T(8,128)(2,1)} %bitcast.32), custom_call_target="tpu_custom_call" | custom-call | flops 1000000 | bytes 4000000 | tf_op jit(solution)/shard_map/pack_rows/pallas_call | solution.py:67
  3.3 6.1 %collective-permute-start = (bf16[80,2048]{1,0:T(8,128)(2,1)}, bf16[80,2048]{1,0:T(8,128)(2,1)S(1)}, u32[]{:S(2)}, u32[]{:S(2)}) collective-permute-start(bf16[80,2048]{1,0:T(8,128)(2,1)} %pack_rows.2), channel_id=1, source_target_pairs={{0,28},{4,24},{8,20},{12,16},{16,12},{20,8},{24,4},{28,0},{1,29},{... | collective-permute-start | bytes 983048 | tf_op jit(solution)/shard_map/ppermute | solution.py:583
  9.4 3.3 %pack_rows.3 = (bf16[80,2048]{1,0:T(8,128)(2,1)}, bf16[80,2048]{1,0:T(8,128)(2,1)}, bf16[80,2048]{1,0:T(8,128)(2,1)}, bf16[80,2048]{1,0:T(8,128)(2,1)}, bf16[80,...) custom-call(s32[1]{0:T(128)} %bitcast.1.me_ref, s32[1]{0:T(128)} %bitcast.core_ref, ...), custom_call_target="tpu_custom_call" | custom-call | flops 1000000 | bytes 10000 | tf_op jit(solution)/shard_map/pack_rows/pallas_call | solution.py:67
  12.8 2.0 %collective-permute-start.2 = (bf16[80,2048]{1,0:T(8,128)(2,1)}, bf16[80,2048]{1,0:T(8,128)(2,1)S(1)}, u32[]{:S(2)}, u32[]{:S(2)}) collective-permute-start(bf16[80,2048]{1,0:T(8,128)(2,1)} %get-tuple-element.40), channel_id=1, source_target_pairs={{0,8},{4,12},{8,0},{12,4},{16,24},{20,28},{24,16},{28,20},{1,9},{5... | collective-permute-start | bytes 983048 | tf_op jit(solution)/shard_map/ppermute | solution.py:583
  14.7 1.5 %collective-permute-start.3 = (bf16[80,2048]{1,0:T(8,128)(2,1)}, bf16[80,2048]{1,0:T(8,128)(2,1)S(1)}, u32[]{:S(2)}, u32[]{:S(2)}) collective-permute-start(bf16[80,2048]{1,0:T(8,128)(2,1)} %get-tuple-element.41), channel_id=1, source_target_pairs={{0,4},{4,0},{8,12},{12,8},{16,20},{20,16},{24,28},{28,24},{1,5},{5... | collective-permute-start | bytes 983048 | tf_op jit(solution)/shard_map/ppermute | solution.py:583
  16.5 1.8 %collective-permute-done.rest_0_ = bf16[80,2048]{1,0:T(8,128)(2,1)S(1)} collective-permute-done((bf16[80,2048]{1,0:T(8,128)(2,1)}, bf16[80,2048]{1,0:T(8,128)(2,1)S(1)}, u32[]{:S(2)}, u32[]{:S(2)}) %collective-permute-start) | collective-permute-done | bytes 327712 | tf_op jit(solution)/shard_map/ppermute | solution.py:583
  18.3 12.2 %collective-permute-start.5 = (bf16[80,2048]{1,0:T(8,128)(2,1)}, bf16[80,2048]{1,0:T(8,128)(2,1)S(1)}, u32[]{:S(2)}, u32[]{:S(2)}) collective-permute-start(bf16[80,2048]{1,0:T(8,128)(2,1)} %get-tuple-element.45), channel_id=1, source_target_pairs={{0,20},{4,16},{8,28},{12,24},{16,4},{20,0},{24,12},{28,8},{1,21},{... | collective-permute-start | bytes 983048 | tf_op jit(solution)/shard_map/ppermute | solution.py:583
  30.5 5.7 %collective-permute-done.2.rest_2_ = bf16[80,2048]{1,0:T(8,128)(2,1)S(1)} collective-permute-done((bf16[80,2048]{1,0:T(8,128)(2,1)}, bf16[80,2048]{1,0:T(8,128)(2,1)S(1)}, u32[]{:S(2)}, u32[]{:S(2)}) %collective-permute-start.2) | collective-permute-done | bytes 327712 | tf_op jit(solution)/shard_map/ppermute | solution.py:583
  36.2 1.9 %copy-done = bf16[1,1,768,2048]{3,2,1,0:T(8,128)(2,1)S(1)} copy-done((bf16[1,1,768,2048]{3,2,1,0:T(8,128)(2,1)S(1)}, bf16[1,1,768,2048]{3,2,1,0:T(8,128)(2,1)}, u32[]{:S(2)}) %copy-start) | copy-done | bytes 3145752
  38.1 1.9 %copy-done.3 = bf16[1,768,2048]{2,1,0:T(8,128)(2,1)S(1)} copy-done((bf16[1,768,2048]{2,1,0:T(8,128)(2,1)S(1)}, bf16[1,768,2048]{2,1,0:T(8,128)(2,1)}, u32[]{:S(2)}) %copy-start.3) | copy-done | bytes 3145752
  41.0 5.0 %early_rows.1 = (f32[64,768]{1,0:T(8,128)S(1)}, bf16[400,2816]{1,0:T(8,128)(2,1)S(1)}, f32[768,2048]{1,0:T(8,128)S(1)}, bf16[80,768]{1,0:T(8,128)(2,1)S(1)}, bf1...) custom-call(s32[1]{0:T(128)} %bitcast.1.me_ref, ...), custom_call_target="tpu_custom_call" | custom-call | flops 2000000000 | bytes 10000000 | tf_op jit(solution)/shard_map/early_rows/pallas_call | solution.py:67
  46.0 2.4 %collective-permute-start.8 = (bf16[80,768]{1,0:T(8,128)(2,1)S(1)}, bf16[80,768]{1,0:T(8,128)(2,1)S(1)}, u32[]{:S(2)}, u32[]{:S(2)}) collective-permute-start(bf16[80,768]{1,0:T(8,128)(2,1)S(1)} %get-tuple-element.49), channel_id=1, source_target_pairs={{0,12},{4,8},{8,4},{12,0},{16,28},{20,24},{24,20},{28,16},{1,13},{... | collective-permute-start | bytes 368648 | tf_op jit(solution)/shard_map/ppermute | solution.py:583
  48.5 1.4 %collective-permute-start.10 = (bf16[80,768]{1,0:T(8,128)(2,1)S(1)}, bf16[80,768]{1,0:T(8,128)(2,1)S(1)}, u32[]{:S(2)}, u32[]{:S(2)}) collective-permute-start(bf16[80,768]{1,0:T(8,128)(2,1)S(1)} %get-tuple-element.51), channel_id=1, source_target_pairs={{0,4},{4,0},{8,12},{12,8},{16,20},{20,16},{24,28},{28,24},{1,5},{5... | collective-permute-start | bytes 368648 | tf_op jit(solution)/shard_map/ppermute | solution.py:583
  51.4 11.2 %collective-permute-done.5.rest_1_ = bf16[80,2048]{1,0:T(8,128)(2,1)S(1)} collective-permute-done((bf16[80,2048]{1,0:T(8,128)(2,1)}, bf16[80,2048]{1,0:T(8,128)(2,1)S(1)}, u32[]{:S(2)}, u32[]{:S(2)}) %collective-permute-start.5) | collective-permute-done | bytes 327712 | tf_op jit(solution)/shard_map/ppermute | solution.py:583
  62.5 6.1 %collective-permute-done.6.rest_2_ = bf16[80,2048]{1,0:T(8,128)(2,1)S(1)} collective-permute-done((bf16[80,2048]{1,0:T(8,128)(2,1)}, bf16[80,2048]{1,0:T(8,128)(2,1)S(1)}, u32[]{:S(2)}, u32[]{:S(2)}) %collective-permute-start.6) | collective-permute-done | bytes 327712 | tf_op jit(solution)/shard_map/ppermute | solution.py:583
  70.6 2.0 %collective-permute-start.15 = (bf16[80,768]{1,0:T(8,128)(2,1)S(1)}, bf16[80,768]{1,0:T(8,128)(2,1)S(1)}, u32[]{:S(2)}, u32[]{:S(2)}) collective-permute-start(bf16[80,768]{1,0:T(8,128)(2,1)S(1)} %pass_on.6), channel_id=1, source_target_pairs={{0,28},{4,24},{8,20},{12,16},{16,12},{20,8},{24,4},{28,0},{1,29},{... | collective-permute-start | bytes 368648 | tf_op jit(solution)/shard_map/ppermute | solution.py:583
  72.6 1.6 %collective-permute-start.11 = (f32[64,768]{1,0:T(8,128)S(1)}, f32[64,768]{1,0:T(8,128)S(1)}, u32[]{:S(2)}, u32[]{:S(2)}) collective-permute-start(f32[64,768]{1,0:T(8,128)S(1)} %add.2.pa_ref.before_ref), channel_id=1, source_target_pairs={{0,2},{1,3},{2,0},{3,1},{4,6},{5,7},{6,4},{7,5},{8,10},{9,11},{10,... | collective-permute-start | bytes 589832 | tf_op jit(solution)/shard_map/ppermute | solution.py:611
  75.3 1.8 %collective-permute-start.16 = (bf16[80,768]{1,0:T(8,128)(2,1)S(1)}, bf16[80,768]{1,0:T(8,128)(2,1)S(1)}, u32[]{:S(2)}, u32[]{:S(2)}) collective-permute-start(bf16[80,768]{1,0:T(8,128)(2,1)S(1)} %pass_on.7), channel_id=1, source_target_pairs={{0,24},{4,28},{8,16},{12,20},{16,8},{20,12},{24,0},{28,4},{1,25},{... | collective-permute-start | bytes 368648 | tf_op jit(solution)/shard_map/ppermute | solution.py:583
  77.1 2.5 %collective-permute-done.11.pb_ref = f32[64,768]{1,0:T(8,128)S(1)} collective-permute-done((f32[64,768]{1,0:T(8,128)S(1)}, f32[64,768]{1,0:T(8,128)S(1)}, u32[]{:S(2)}, u32[]{:S(2)}) %collective-permute-start.11) | collective-permute-done | bytes 196640 | tf_op jit(solution)/shard_map/ppermute | solution.py:611
  82.4 1.6 %collective-permute-start.13 = (f32[64,1024]{1,0:T(8,128)S(1)}, f32[64,1024]{1,0:T(8,128)S(1)}, u32[]{:S(2)}, u32[]{:S(2)}) collective-permute-start(f32[64,1024]{1,0:T(8,128)S(1)} %add.3.before_ref.mine_ref), channel_id=1, source_target_pairs={{0,2},{1,3},{2,0},{3,1},{4,6},{5,7},{6,4},{7,5},{8,10},{9,11},{10,... | collective-permute-start | bytes 786440 | tf_op jit(solution)/shard_map/ppermute | solution.py:625
  84.1 4.4 %basis.1 = (f32[64,768]{1,0:T(8,128)}, f32[64,64]{1,0:T(8,128)S(1)}, bf16[768,384]{1,0:T(8,128)(2,1)S(1)}) custom-call(f32[64,768]{1,0:T(8,128)S(1)} %get-tuple-element.62.p_ref, bf16[80,768]{1,0:T(8,128)(2,1)S(1)} %pass_on.4.before_ref), custom_call_target="tpu_custom_call" | custom-call | flops 10000000000 | bytes 1000000 | tf_op jit(solution)/shard_map/basis/pallas_call | solution.py:67
  88.5 2.6 %collective-permute-done.13.far_ref = f32[64,1024]{1,0:T(8,128)S(1)} collective-permute-done((f32[64,1024]{1,0:T(8,128)S(1)}, f32[64,1024]{1,0:T(8,128)S(1)}, u32[]{:S(2)}, u32[]{:S(2)}) %collective-permute-start.13) | collective-permute-done | bytes 262176 | tf_op jit(solution)/shard_map/ppermute | solution.py:625
  92.5 1.3 %collective-permute-done.18.rest_5_ = bf16[80,768]{1,0:T(8,128)(2,1)S(1)} collective-permute-done((bf16[80,768]{1,0:T(8,128)(2,1)S(1)}, bf16[80,768]{1,0:T(8,128)(2,1)S(1)}, u32[]{:S(2)}, u32[]{:S(2)}) %collective-permute-start.18) | collective-permute-done | bytes 122912 | tf_op jit(solution)/shard_map/ppermute | solution.py:583
  93.9 2.4 %new_error_last.1 = (f32[64,2048]{1,0:T(8,128)}, bf16[768,2048]{1,0:T(8,128)(2,1)}, bf16[512,768]{1,0:T(8,128)(2,1)}) custom-call(s32[1]{0:T(128)} %bitcast.core_ref, f32[64,1024]{1,0:T(8,128)S(1)} %q_half.1.q_ref.mine_ref, f32[64,1024]{1,0:T(8,128)S(1)} %collective-permute-done.14.other_ref, bf16[768,384]{1,0:T(8,128)(2,1)S(1)} %get-tuple-element.65.left_ref, ...), custom_call_target="tpu_custom_call" | custom-call | flops 10000000000 | bytes 1000000 | tf_op jit(solution)/shard_map/new_error_last/pallas_call | solution.py:67
  (53 shorter events, 10.2 us)
Async XLA Ops:
  0.6 35.6 %copy-start.5 = (bf16[1,2048,64]{1,2,0:T(8,128)(2,1)S(1)}, bf16[1,2048,64]{1,2,0:T(8,128)(2,1)}, u32[]{:S(2)}) copy-start(bf16[1,2048,64]{1,2,0:T(8,128)(2,1)} %param.13) | copy-start | bytes 786436
  0.6 35.6 %copy-start.2 = (bf16[1,1,640,768]{3,2,1,0:T(8,128)(2,1)S(1)}, bf16[1,1,640,768]{3,2,1,0:T(8,128)(2,1)}, u32[]{:S(2)}) copy-start(bf16[1,1,640,768]{3,2,1,0:T(8,128)(2,1)} %param.10) | copy-start | bytes 2949124
  3.3 15.0 %collective-permute-start = (bf16[80,2048]{1,0:T(8,128)(2,1)}, bf16[80,2048]{1,0:T(8,128)(2,1)S(1)}, u32[]{:S(2)}, u32[]{:S(2)}) collective-permute-start(bf16[80,2048]{1,0:T(8,128)(2,1)} %pack_rows.2), channel_id=1, source_target_pairs={{0,28},{4,24},{8,20},{12,16},{16,12},{20,8},{24,4},{28,0},{1,29},{... | collective-permute-start | bytes 983048 | tf_op jit(solution)/shard_map/ppermute | solution.py:583
  12.7 17.8 %collective-permute-start.1 = (bf16[80,2048]{1,0:T(8,128)(2,1)}, bf16[80,2048]{1,0:T(8,128)(2,1)S(1)}, u32[]{:S(2)}, u32[]{:S(2)}) collective-permute-start(bf16[80,2048]{1,0:T(8,128)(2,1)} %get-tuple-element.39), channel_id=1, source_target_pairs={{0,12},{4,8},{8,4},{12,0},{16,28},{20,24},{24,20},{28,16},{1,13},{... | collective-permute-start | bytes 983048 | tf_op jit(solution)/shard_map/ppermute | solution.py:583
  12.8 23.4 %collective-permute-start.2 = (bf16[80,2048]{1,0:T(8,128)(2,1)}, bf16[80,2048]{1,0:T(8,128)(2,1)S(1)}, u32[]{:S(2)}, u32[]{:S(2)}) collective-permute-start(bf16[80,2048]{1,0:T(8,128)(2,1)} %get-tuple-element.40), channel_id=1, source_target_pairs={{0,8},{4,12},{8,0},{12,4},{16,24},{20,28},{24,16},{28,20},{1,9},{5... | collective-permute-start | bytes 983048 | tf_op jit(solution)/shard_map/ppermute | solution.py:583
  14.7 21.5 %collective-permute-start.3 = (bf16[80,2048]{1,0:T(8,128)(2,1)}, bf16[80,2048]{1,0:T(8,128)(2,1)S(1)}, u32[]{:S(2)}, u32[]{:S(2)}) collective-permute-start(bf16[80,2048]{1,0:T(8,128)(2,1)} %get-tuple-element.41), channel_id=1, source_target_pairs={{0,4},{4,0},{8,12},{12,8},{16,20},{20,16},{24,28},{28,24},{1,5},{5... | collective-permute-start | bytes 983048 | tf_op jit(solution)/shard_map/ppermute | solution.py:583
  16.3 32.3 %collective-permute-start.4 = (bf16[80,2048]{1,0:T(8,128)(2,1)}, bf16[80,2048]{1,0:T(8,128)(2,1)S(1)}, u32[]{:S(2)}, u32[]{:S(2)}) collective-permute-start(bf16[80,2048]{1,0:T(8,128)(2,1)} %get-tuple-element.44), channel_id=1, source_target_pairs={{0,24},{4,28},{8,16},{12,20},{16,8},{20,12},{24,0},{28,4},{1,25},{... | collective-permute-start | bytes 983048 | tf_op jit(solution)/shard_map/ppermute | solution.py:583
  18.3 44.3 %collective-permute-start.5 = (bf16[80,2048]{1,0:T(8,128)(2,1)}, bf16[80,2048]{1,0:T(8,128)(2,1)S(1)}, u32[]{:S(2)}, u32[]{:S(2)}) collective-permute-start(bf16[80,2048]{1,0:T(8,128)(2,1)} %get-tuple-element.45), channel_id=1, source_target_pairs={{0,20},{4,16},{8,28},{12,24},{16,4},{20,0},{24,12},{28,8},{1,21},{... | collective-permute-start | bytes 983048 | tf_op jit(solution)/shard_map/ppermute | solution.py:583
  30.5 38.1 %collective-permute-start.6 = (bf16[80,2048]{1,0:T(8,128)(2,1)}, bf16[80,2048]{1,0:T(8,128)(2,1)S(1)}, u32[]{:S(2)}, u32[]{:S(2)}) collective-permute-start(bf16[80,2048]{1,0:T(8,128)(2,1)} %get-tuple-element.46), channel_id=1, source_target_pairs={{0,16},{4,20},{8,24},{12,28},{16,0},{20,4},{24,8},{28,12},{1,17},{... | collective-permute-start | bytes 983048 | tf_op jit(solution)/shard_map/ppermute | solution.py:583
  41.0 8.9 %copy-start.7 = (s32[1,512]{1,0:T(1,128)S(1)}, s32[1,512]{1,0:T(1,128)}, u32[]{:S(2)}) copy-start(s32[1,512]{1,0:T(1,128)} %order_ref.3) | copy-start | bytes 6148
  41.0 8.9 %copy-start.8 = (s32[1,1,8]{2,1,0:T(1,128)S(1)}, s32[1,1,8]{2,1,0:T(1,128)}, u32[]{:S(2)}) copy-start(s32[1,1,8]{2,1,0:T(1,128)} %param.8) | copy-start | bytes 100
  46.0 23.5 %copy-start.4 = (bf16[1,768,2048]{2,1,0:T(8,128)(2,1)S(1)}, bf16[1,768,2048]{2,1,0:T(8,128)(2,1)}, u32[]{:S(2)}) copy-start(bf16[1,768,2048]{2,1,0:T(8,128)(2,1)} %param.11) | copy-start | bytes 9437188
  46.0 23.5 %collective-permute-start.8 = (bf16[80,768]{1,0:T(8,128)(2,1)S(1)}, bf16[80,768]{1,0:T(8,128)(2,1)S(1)}, u32[]{:S(2)}, u32[]{:S(2)}) collective-permute-start(bf16[80,768]{1,0:T(8,128)(2,1)S(1)} %get-tuple-element.49), channel_id=1, source_target_pairs={{0,12},{4,8},{8,4},{12,0},{16,28},{20,24},{24,20},{28,16},{1,13},{... | collective-permute-start | bytes 368648 | tf_op jit(solution)/shard_map/ppermute | solution.py:583
  48.4 21.1 %collective-permute-start.9 = (bf16[80,768]{1,0:T(8,128)(2,1)S(1)}, bf16[80,768]{1,0:T(8,128)(2,1)S(1)}, u32[]{:S(2)}, u32[]{:S(2)}) collective-permute-start(bf16[80,768]{1,0:T(8,128)(2,1)S(1)} %get-tuple-element.50), channel_id=1, source_target_pairs={{0,8},{4,12},{8,0},{12,4},{16,24},{20,28},{24,16},{28,20},{1,9},{5... | collective-permute-start | bytes 368648 | tf_op jit(solution)/shard_map/ppermute | solution.py:583
  48.5 21.0 %collective-permute-start.10 = (bf16[80,768]{1,0:T(8,128)(2,1)S(1)}, bf16[80,768]{1,0:T(8,128)(2,1)S(1)}, u32[]{:S(2)}, u32[]{:S(2)}) collective-permute-start(bf16[80,768]{1,0:T(8,128)(2,1)S(1)} %get-tuple-element.51), channel_id=1, source_target_pairs={{0,4},{4,0},{8,12},{12,8},{16,20},{20,16},{24,28},{28,24},{1,5},{5... | collective-permute-start | bytes 368648 | tf_op jit(solution)/shard_map/ppermute | solution.py:583
  69.4 3.2 %collective-permute-start.7 = (f32[64,768]{1,0:T(8,128)S(1)}, f32[64,768]{1,0:T(8,128)S(1)}, u32[]{:S(2)}, u32[]{:S(2)}) collective-permute-start(f32[64,768]{1,0:T(8,128)S(1)} %get-tuple-element.47.a_ref), channel_id=1, source_target_pairs={{0,1},{1,0},{2,3},{3,2},{4,5},{5,4},{6,7},{7,6},{8,9},{9,8},{10,11... | collective-permute-start | bytes 589832 | tf_op jit(solution)/shard_map/ppermute | solution.py:610
  70.6 21.9 %collective-permute-start.15 = (bf16[80,768]{1,0:T(8,128)(2,1)S(1)}, bf16[80,768]{1,0:T(8,128)(2,1)S(1)}, u32[]{:S(2)}, u32[]{:S(2)}) collective-permute-start(bf16[80,768]{1,0:T(8,128)(2,1)S(1)} %pass_on.6), channel_id=1, source_target_pairs={{0,28},{4,24},{8,20},{12,16},{16,12},{20,8},{24,4},{28,0},{1,29},{... | collective-permute-start | bytes 368648 | tf_op jit(solution)/shard_map/ppermute | solution.py:583
  72.6 7.1 %collective-permute-start.11 = (f32[64,768]{1,0:T(8,128)S(1)}, f32[64,768]{1,0:T(8,128)S(1)}, u32[]{:S(2)}, u32[]{:S(2)}) collective-permute-start(f32[64,768]{1,0:T(8,128)S(1)} %add.2.pa_ref.before_ref), channel_id=1, source_target_pairs={{0,2},{1,3},{2,0},{3,1},{4,6},{5,7},{6,4},{7,5},{8,10},{9,11},{10,... | collective-permute-start | bytes 589832 | tf_op jit(solution)/shard_map/ppermute | solution.py:611
  74.1 18.4 %collective-permute-start.17 = (bf16[80,768]{1,0:T(8,128)(2,1)S(1)}, bf16[80,768]{1,0:T(8,128)(2,1)S(1)}, u32[]{:S(2)}, u32[]{:S(2)}) collective-permute-start(bf16[80,768]{1,0:T(8,128)(2,1)S(1)} %pass_on.5.before_ref), channel_id=1, source_target_pairs={{0,20},{4,16},{8,28},{12,24},{16,4},{20,0},{24,12},{28,8},{1,21},{... | collective-permute-start | bytes 368648 | tf_op jit(solution)/shard_map/ppermute | solution.py:583
  75.3 17.2 %collective-permute-start.16 = (bf16[80,768]{1,0:T(8,128)(2,1)S(1)}, bf16[80,768]{1,0:T(8,128)(2,1)S(1)}, u32[]{:S(2)}, u32[]{:S(2)}) collective-permute-start(bf16[80,768]{1,0:T(8,128)(2,1)S(1)} %pass_on.7), channel_id=1, source_target_pairs={{0,24},{4,28},{8,16},{12,20},{16,8},{20,12},{24,0},{28,4},{1,25},{... | collective-permute-start | bytes 368648 | tf_op jit(solution)/shard_map/ppermute | solution.py:583
  80.8 1.6 %collective-permute-start.12 = (f32[64,1024]{1,0:T(8,128)S(1)}, f32[64,1024]{1,0:T(8,128)S(1)}, u32[]{:S(2)}, u32[]{:S(2)}) collective-permute-start(f32[64,1024]{1,0:T(8,128)S(1)} %get-tuple-element.59), channel_id=1, source_target_pairs={{0,1},{1,0},{2,3},{3,2},{4,5},{5,4},{6,7},{7,6},{8,9},{9,8},{10,11... | collective-permute-start | bytes 786440 | tf_op jit(solution)/shard_map/ppermute | solution.py:616
  82.4 8.6 %collective-permute-start.13 = (f32[64,1024]{1,0:T(8,128)S(1)}, f32[64,1024]{1,0:T(8,128)S(1)}, u32[]{:S(2)}, u32[]{:S(2)}) collective-permute-start(f32[64,1024]{1,0:T(8,128)S(1)} %add.3.before_ref.mine_ref), channel_id=1, source_target_pairs={{0,2},{1,3},{2,0},{3,1},{4,6},{5,7},{6,4},{7,5},{8,10},{9,11},{10,... | collective-permute-start | bytes 786440 | tf_op jit(solution)/shard_map/ppermute | solution.py:625
  84.0 9.9 %collective-permute-start.18 = (bf16[80,768]{1,0:T(8,128)(2,1)S(1)}, bf16[80,768]{1,0:T(8,128)(2,1)S(1)}, u32[]{:S(2)}, u32[]{:S(2)}) collective-permute-start(bf16[80,768]{1,0:T(8,128)(2,1)S(1)} %pass_on.4.before_ref), channel_id=1, source_target_pairs={{0,16},{4,20},{8,24},{12,28},{16,0},{20,4},{24,8},{28,12},{1,17},{... | collective-permute-start | bytes 368648 | tf_op jit(solution)/shard_map/ppermute | solution.py:583
  91.4 2.5 %collective-permute-start.14 = (f32[64,1024]{1,0:T(8,128)S(1)}, f32[64,1024]{1,0:T(8,128)S(1)}, u32[]{:S(2)}, u32[]{:S(2)}) collective-permute-start(f32[64,1024]{1,0:T(8,128)S(1)} %q_half.1.q_ref.mine_ref), channel_id=1, source_target_pairs={{0,1},{1,0},{2,3},{3,2},{4,5},{5,4},{6,7},{7,6},{8,9},{9,8},{10,11... | collective-permute-start | bytes 786440 | tf_op jit(solution)/shard_map/ppermute | solution.py:626
  (4 other events, 10.2 us)

commit v3 on v1

--- a/solution.py
+++ b/solution.py
@@ -80,7 +80,50 @@
     )(*scalars, *operands)
 
 
-def pack_kernel(n, cap, masks, me_ref, core_ref, counts_hbm, rows_hbm, *rest):
+def start_of(counts_ref, expert, n):
+    start = jnp.int32(0)
+    for e in range(n):
+        start = start + jnp.where(e < expert, counts_ref[0, e], 0)
+    return start
+
+
+def pack_first_kernel(n, mask, me_ref, core_ref, counts_hbm, rows_hbm, out_ref, counts_ref, rows_ref, sems):
+    cap = out_ref.shape[0]
+    total, window = rows_hbm.shape[0], rows_ref.shape[0]
+    dest = me_ref[0] ^ mask
+    base = jnp.clip(total - cap * (n - dest), 0, total - window)
+    base = pl.multiple_of(base, ROW_TILE)
+    copy_counts = pltpu.make_async_copy(counts_hbm, counts_ref, sems.at[0])
+    copy_rows = pltpu.make_async_copy(rows_hbm.at[pl.ds(base, window), :], rows_ref, sems.at[1])
+    copy_counts.start()
+    copy_rows.start()
+    copy_counts.wait()
+    j = lax.broadcasted_iota(jnp.int32, (cap, window), 0)
+    w = lax.broadcasted_iota(jnp.int32, (cap, window), 1)
+    hit = (w == j + (start_of(counts_ref, dest, n) - base)) & (j < counts_ref[0, dest])
+    pick = jnp.where(hit, 1.0, 0.0).astype(BF16)
+    copy_rows.wait()
+    out_ref[...] = dot_nn(pick, rows_ref[...]).astype(BF16)
+
+
+def pack_first(me, core, counts, rows, n, cap, mask):
+    total, width = rows.shape
+    window = min(total, cap * (n + 1) - total)
+    return call(
+        functools.partial(pack_first_kernel, n, mask),
+        "pack_first",
+        (me, core),
+        (counts, rows),
+        [((cap, width), BF16)],
+        [pltpu.SMEM(counts.shape, jnp.int32), pltpu.VMEM((window, width), BF16), pltpu.SemaphoreType.DMA((2,))],
+        specs=[in_hbm()] * 2,
+        limit=62,
+        flops=10**6,
+        nbytes=4 * 10**6,
+    )[0]
+
+
+def pack_kernel(n, cap, masks, me_ref, counts_hbm, rows_hbm, *rest):
     outs = rest[: len(masks)]
     counts_ref, rows_ref, held, sems, out_sems = rest[len(masks) :]
     total = rows_ref.shape[0]
@@ -95,17 +138,12 @@
     bases, picks = [], []
     for mask in masks:
         dest = me_ref[0] ^ mask
-        start = jnp.int32(0)
-        for e in range(n):
-            start = start + jnp.where(e < dest, counts_ref[0, e], 0)
+        start = start_of(counts_ref, dest, n)
         base = jnp.minimum((start // ROW_TILE) * ROW_TILE, total - window)
         bases.append(pl.multiple_of(base, ROW_TILE))
         hit = (w == j + (start - base)) & (j < counts_ref[0, dest])
         picks.append(jnp.where(hit, 1.0, 0.0).astype(BF16))
     copy_rows.wait()
-    if len(masks) == 1:
-        outs[0][...] = dot_nn(picks[0], rows_ref[pl.ds(bases[0], window), :]).astype(BF16)
-        return
     copies = []
     for k, (base, pick) in enumerate(zip(bases, picks)):
         held[k] = dot_nn(pick, rows_ref[pl.ds(base, window), :]).astype(BF16)
@@ -115,12 +153,12 @@
         copy.wait()
 
 
-def pack(me, core, counts, rows, n, cap, masks, nbytes, out_spec, limit):
+def pack(me, counts, rows, n, cap, masks):
     count, width = len(masks), rows.shape[1]
     return call(
         functools.partial(pack_kernel, n, cap, masks),
         "pack_rows",
-        (me, core),
+        (me,),
         (counts, rows),
         [((cap, width), BF16)] * count,
         [
@@ -131,10 +169,10 @@
             pltpu.SemaphoreType.DMA((count,)),
         ],
         specs=[in_hbm()] * 2,
-        out_specs=[out_spec] * count,
-        limit=limit,
+        out_specs=[in_hbm()] * count,
+        limit=FULL,
         flops=10**6,
-        nbytes=nbytes,
+        nbytes=10**4,
     )
 
 
@@ -230,33 +268,56 @@
     )
 
 
-def s_kernel(core_ref, pa_ref, pb_ref, error_ref, *rest):
-    *groups, p_out, send_ref, keep_ref, token_ref = rest
-    set_token(token_ref)
+def s_columns(part, p3, ys, error_ref, groups, out_ref):
+    half = out_ref.shape[1]
+    for j in range(0, half, COLS):
+        cols = pl.ds(pl.multiple_of(part * half + j, COLS), COLS)
+        res = dot_nn(p3, error_ref[:, cols])
+        for y, group in zip(ys, groups):
+            res = res + dot_nn(y, group[:, cols])
+        out_ref[:, j : j + COLS] = fold3(res)
+
+
+def s_send_kernel(count, core_ref, pa_ref, pb_ref, error_ref, *rest):
+    groups = rest[:count]
+    p_out, send_ref, p3_ref, *y_refs = rest[count:]
     total = pa_ref[...] + pb_ref[...]
     p_out[...] = total
-    p3 = stack3(total)
+    p3_ref[...] = stack3(total)
     width = error_ref.shape[1]
-    half = width // 2
-    ys = [stack3(fold3(dot_nt(p3, group[:, width:]))) for group in groups]
-    for out, part in ((send_ref, 1 - core_ref[0]), (keep_ref, core_ref[0])):
-        for j in range(0, half, COLS):
-            cols = pl.ds(pl.multiple_of(part * half + j, COLS), COLS)
-            res = dot_nn(p3, error_ref[:, cols])
-            for y, group in zip(ys, groups):
-                res = res + dot_nn(y, group[:, cols])
-            out[:, j : j + COLS] = fold3(res)
-
-
-def s_partial(core, pa, pb, error, groups):
+    for y_ref, group in zip(y_refs, groups):
+        y_ref[...] = stack3(fold3(dot_nt(p3_ref[...], group[:, width:])))
+    s_columns(1 - core_ref[0], p3_ref[...], [y[...] for y in y_refs], error_ref, groups, send_ref)
+
+
+def s_send(core, pa, pb, error, groups):
     rank, ff = pa.shape
     width = error.shape[1]
     return call(
-        s_kernel,
-        "s_partial",
+        functools.partial(s_send_kernel, len(groups)),
+        "s_send",
         (core,),
         (pa, pb, error, *groups),
-        [((rank, ff), F32), ((rank, width // 2), F32), ((rank, width // 2), F32), TOKEN],
+        [((rank, ff), F32), ((rank, width // 2), F32), ((3 * rank, ff), BF16)]
+        + [((3 * rank, group.shape[0]), BF16) for group in groups],
+        nbytes=7 * 10**6,
+    )
+
+
+def s_keep_kernel(count, core_ref, p3_ref, error_ref, *rest):
+    ys, groups, (keep_ref, token_ref) = rest[:count], rest[count : 2 * count], rest[2 * count :]
+    set_token(token_ref)
+    s_columns(core_ref[0], p3_ref[...], [y[...] for y in ys], error_ref, groups, keep_ref)
+
+
+def s_keep(core, p3, ys, error, groups):
+    rank = p3.shape[0] // 3
+    return call(
+        functools.partial(s_keep_kernel, len(groups)),
+        "s_keep",
+        (core,),
+        (p3, error, *ys, *groups),
+        [((rank, error.shape[1] // 2), F32), TOKEN],
         nbytes=7 * 10**6,
     )
 
@@ -560,7 +621,7 @@
     core = (lax.axis_index("dp").astype(jnp.int32) & 1)[None]
     core_pairs = [(d, d ^ 1) for d in range(n_dp)]
     chip_pairs = [(d, d ^ 2) for d in range(n_dp)]
-    by_pairs = n_expert == 8 and capacity % ROW_TILE == 0
+    by_pairs = n_expert == 8 and capacity % ROW_TILE == 0 and rows.shape[0] % ROW_TILE == 0
 
     if by_pairs:
         far = tuple(reversed(range(n_expert // 2, n_expert)))
@@ -571,8 +632,8 @@
             return lax.ppermute(x, "expert", [(e, e ^ mask) for e in range(n_expert)])
 
         others = far[1:] + near
-        packed = {far[0]: pack(me, core, counts[0], rows, n_expert, capacity, far[:1], 4 * 10**6, whole_vmem(), 62)[0]}
-        packed.update(zip(others, pack(me, core, counts[0], rows, n_expert, capacity, others, 10**4, in_hbm(), FULL)))
+        packed = {far[0]: pack_first(me, core, counts[0], rows, n_expert, capacity, far[0])}
+        packed.update(zip(others, pack(me, counts[0], rows, n_expert, capacity, others)))
         arrived = {m: swap(packed[m], m) if m else packed[m] for m in far + near}
         pick_near = pick_of(me, count, order, n_expert, capacity, near)
         pick_far = pick_of(me, count, order, n_expert, capacity, far)
@@ -596,10 +657,12 @@
         returned = returned.reshape(n_expert * capacity, ff)
     p_chip = add(p_mine, lax.ppermute(p_mine, "dp", core_pairs), *before)
     p_far = lax.ppermute(p_chip, "dp", chip_pairs)
-    p_total, s_send, s_keep, token = s_partial(core, p_chip, p_far, error, groups)
+    p_total, s_sent, p3, *ys = s_send(core, p_chip, p_far, error, groups)
+    s_swapped = lax.ppermute(s_sent, "dp", core_pairs)
+    s_kept, token = s_keep(core, p3, ys, error, groups)
     if by_pairs:
         grad_near, token = unpack_first(token, pick_near, back_near)
-    s_half = add(s_keep, lax.ppermute(s_send, "dp", core_pairs), token)
+    s_half = add(s_kept, s_swapped, token)
     if by_pairs:
         back_last = pass_on(back_next[-1], s_half)
         back_far = [swap(x, m) for x, m in zip([back[0], *back_next[:-1], back_last], far)]

time: 96.2 us -> 96 us (level)
    pallas_call x17 -> x18, Pallas kernels: 25.2 us -> 25.1 us  [call(): pl.pallas_call(kernel, grid_spec=pltpu.PrefetchScalarGridSpec(num_scalar_...]
  transfers between devices with their start and end apart: 19 -> 19, of which waited for: 11 -> 11; matrix products, arithmetic and copies ran while one was open for 0% -> 0% of each run, Pallas kernels for 23% -> 24%
where the time goes in v3:
time: 96 us; the launch traced here: 95.7 us
  starting transfers between devices  34.3 us (36%)
  waiting for transfers between devices  29.1 us (30%)
  Pallas kernels  26.5 us (28%)
  local copies, waits for them, and re-layouts  4.78 us (5%)
  between operations  1.04 us (1%)
    ppermute x14, starting transfers between devices, swap(): return lax.ppermute(x, 'expert', [(e, e ^ mask) for e in range(n_expert)])  30.9 us
    ppermute x14, waiting for transfers between devices, swap(): return lax.ppermute(x, 'expert', [(e, e ^ mask) for e in range(n_expert)])  26 us
    pallas_call x18, Pallas kernels, call(): pl.pallas_call(kernel, grid_spec=pltpu.PrefetchScalarGridSpec(num_scalar_...  25.1 us
    unnamed x18, local copies, waits for them, and re-layouts  4.78 us
  transfers between devices with their start and end apart: 19, of which 11 were waited for; matrix products, arithmetic and copies ran while one was open for 0% of the time, Pallas kernels for 24%

profile of v3, /device:TPU:0, one launch (start us, length us, event | category | flops | bytes accessed | tf_op | source)
XLA Modules:
  0.0 95.7 jit_solution(1408497241768464046)
XLA Ops:
  0.7 2.3 %pack_first.1 = bf16[80,2048]{1,0:T(8,128)(2,1)} custom-call(s32[1]{0:T(128)} %bitcast.1.me_ref, s32[1]{0:T(128)} %bitcast.core_ref, s32[1,8]{1,0:T(1,128)} %bitcast.28, bf16[512,2048]{1,0:T(8,128)(2,1)} %bitcast.32), custom_call_target="tpu_custom_call" | custom-call | flops 1000000 | bytes 4000000 | tf_op jit(solution)/shard_map/pack_first/pallas_call | solution.py:67
  2.9 6.1 %collective-permute-start = (bf16[80,2048]{1,0:T(8,128)(2,1)}, bf16[80,2048]{1,0:T(8,128)(2,1)S(1)}, u32[]{:S(2)}, u32[]{:S(2)}) collective-permute-start(bf16[80,2048]{1,0:T(8,128)(2,1)} %pack_first.1), channel_id=1, source_target_pairs={{0,28},{4,24},{8,20},{12,16},{16,12},{20,8},{24,4},{28,0},{1,29},{... | collective-permute-start | bytes 983048 | tf_op jit(solution)/shard_map/ppermute | solution.py:632
  9.0 3.3 %pack_rows.1 = (bf16[80,2048]{1,0:T(8,128)(2,1)}, bf16[80,2048]{1,0:T(8,128)(2,1)}, bf16[80,2048]{1,0:T(8,128)(2,1)}, bf16[80,2048]{1,0:T(8,128)(2,1)}, bf16[80,...) custom-call(s32[1]{0:T(128)} %bitcast.1.me_ref, s32[1,8]{1,0:T(1,128)} %bitcast.29, ...), custom_call_target="tpu_custom_call" | custom-call | flops 1000000 | bytes 10000 | tf_op jit(solution)/shard_map/pack_rows/pallas_call | solution.py:67
  12.4 2.0 %collective-permute-start.2 = (bf16[80,2048]{1,0:T(8,128)(2,1)}, bf16[80,2048]{1,0:T(8,128)(2,1)S(1)}, u32[]{:S(2)}, u32[]{:S(2)}) collective-permute-start(bf16[80,2048]{1,0:T(8,128)(2,1)} %get-tuple-element.40), channel_id=1, source_target_pairs={{0,8},{4,12},{8,0},{12,4},{16,24},{20,28},{24,16},{28,20},{1,9},{5... | collective-permute-start | bytes 983048 | tf_op jit(solution)/shard_map/ppermute | solution.py:632
  14.3 1.5 %collective-permute-start.3 = (bf16[80,2048]{1,0:T(8,128)(2,1)}, bf16[80,2048]{1,0:T(8,128)(2,1)S(1)}, u32[]{:S(2)}, u32[]{:S(2)}) collective-permute-start(bf16[80,2048]{1,0:T(8,128)(2,1)} %get-tuple-element.41), channel_id=1, source_target_pairs={{0,4},{4,0},{8,12},{12,8},{16,20},{20,16},{24,28},{28,24},{1,5},{5... | collective-permute-start | bytes 983048 | tf_op jit(solution)/shard_map/ppermute | solution.py:632
  16.1 1.8 %collective-permute-done.rest_0_ = bf16[80,2048]{1,0:T(8,128)(2,1)S(1)} collective-permute-done((bf16[80,2048]{1,0:T(8,128)(2,1)}, bf16[80,2048]{1,0:T(8,128)(2,1)S(1)}, u32[]{:S(2)}, u32[]{:S(2)}) %collective-permute-start) | collective-permute-done | bytes 327712 | tf_op jit(solution)/shard_map/ppermute | solution.py:632
  17.9 12.2 %collective-permute-start.5 = (bf16[80,2048]{1,0:T(8,128)(2,1)}, bf16[80,2048]{1,0:T(8,128)(2,1)S(1)}, u32[]{:S(2)}, u32[]{:S(2)}) collective-permute-start(bf16[80,2048]{1,0:T(8,128)(2,1)} %get-tuple-element.45), channel_id=1, source_target_pairs={{0,20},{4,16},{8,28},{12,24},{16,4},{20,0},{24,12},{28,8},{1,21},{... | collective-permute-start | bytes 983048 | tf_op jit(solution)/shard_map/ppermute | solution.py:632
  30.1 5.7 %collective-permute-done.2.rest_2_ = bf16[80,2048]{1,0:T(8,128)(2,1)S(1)} collective-permute-done((bf16[80,2048]{1,0:T(8,128)(2,1)}, bf16[80,2048]{1,0:T(8,128)(2,1)S(1)}, u32[]{:S(2)}, u32[]{:S(2)}) %collective-permute-start.2) | collective-permute-done | bytes 327712 | tf_op jit(solution)/shard_map/ppermute | solution.py:632
  35.8 1.9 %copy-done = bf16[1,1,768,2048]{3,2,1,0:T(8,128)(2,1)S(1)} copy-done((bf16[1,1,768,2048]{3,2,1,0:T(8,128)(2,1)S(1)}, bf16[1,1,768,2048]{3,2,1,0:T(8,128)(2,1)}, u32[]{:S(2)}) %copy-start) | copy-done | bytes 3145752
  37.7 1.9 %copy-done.3 = bf16[1,768,2048]{2,1,0:T(8,128)(2,1)S(1)} copy-done((bf16[1,768,2048]{2,1,0:T(8,128)(2,1)S(1)}, bf16[1,768,2048]{2,1,0:T(8,128)(2,1)}, u32[]{:S(2)}) %copy-start.3) | copy-done | bytes 3145752
  40.6 5.0 %early_rows.1 = (f32[64,768]{1,0:T(8,128)S(1)}, bf16[400,2816]{1,0:T(8,128)(2,1)S(1)}, f32[768,2048]{1,0:T(8,128)S(1)}, bf16[80,768]{1,0:T(8,128)(2,1)S(1)}, bf1...) custom-call(s32[1]{0:T(128)} %bitcast.1.me_ref, ...), custom_call_target="tpu_custom_call" | custom-call | flops 2000000000 | bytes 10000000 | tf_op jit(solution)/shard_map/early_rows/pallas_call | solution.py:67
  45.6 2.4 %collective-permute-start.8 = (bf16[80,768]{1,0:T(8,128)(2,1)S(1)}, bf16[80,768]{1,0:T(8,128)(2,1)S(1)}, u32[]{:S(2)}, u32[]{:S(2)}) collective-permute-start(bf16[80,768]{1,0:T(8,128)(2,1)S(1)} %get-tuple-element.49), channel_id=1, source_target_pairs={{0,12},{4,8},{8,4},{12,0},{16,28},{20,24},{24,20},{28,16},{1,13},{... | collective-permute-start | bytes 368648 | tf_op jit(solution)/shard_map/ppermute | solution.py:632
  48.1 1.4 %collective-permute-start.10 = (bf16[80,768]{1,0:T(8,128)(2,1)S(1)}, bf16[80,768]{1,0:T(8,128)(2,1)S(1)}, u32[]{:S(2)}, u32[]{:S(2)}) collective-permute-start(bf16[80,768]{1,0:T(8,128)(2,1)S(1)} %get-tuple-element.51), channel_id=1, source_target_pairs={{0,4},{4,0},{8,12},{12,8},{16,20},{20,16},{24,28},{28,24},{1,5},{5... | collective-permute-start | bytes 368648 | tf_op jit(solution)/shard_map/ppermute | solution.py:632
  51.0 11.2 %collective-permute-done.5.rest_1_ = bf16[80,2048]{1,0:T(8,128)(2,1)S(1)} collective-permute-done((bf16[80,2048]{1,0:T(8,128)(2,1)}, bf16[80,2048]{1,0:T(8,128)(2,1)S(1)}, u32[]{:S(2)}, u32[]{:S(2)}) %collective-permute-start.5) | collective-permute-done | bytes 327712 | tf_op jit(solution)/shard_map/ppermute | solution.py:632
  62.1 6.1 %collective-permute-done.6.rest_2_ = bf16[80,2048]{1,0:T(8,128)(2,1)S(1)} collective-permute-done((bf16[80,2048]{1,0:T(8,128)(2,1)}, bf16[80,2048]{1,0:T(8,128)(2,1)S(1)}, u32[]{:S(2)}, u32[]{:S(2)}) %collective-permute-start.6) | collective-permute-done | bytes 327712 | tf_op jit(solution)/shard_map/ppermute | solution.py:632
  70.5 1.6 %collective-permute-start.11 = (f32[64,768]{1,0:T(8,128)S(1)}, f32[64,768]{1,0:T(8,128)S(1)}, u32[]{:S(2)}, u32[]{:S(2)}) collective-permute-start(f32[64,768]{1,0:T(8,128)S(1)} %add.2.pa_ref), channel_id=1, source_target_pairs={{0,2},{1,3},{2,0},{3,1},{4,6},{5,7},{6,4},{7,5},{8,10},{9,11},{10,... | collective-permute-start | bytes 589832 | tf_op jit(solution)/shard_map/ppermute | solution.py:659
  72.1 1.9 %collective-permute-start.15 = (bf16[80,768]{1,0:T(8,128)(2,1)S(1)}, bf16[80,768]{1,0:T(8,128)(2,1)S(1)}, u32[]{:S(2)}, u32[]{:S(2)}) collective-permute-start(bf16[80,768]{1,0:T(8,128)(2,1)S(1)} %get-tuple-element.69), channel_id=1, source_target_pairs={{0,28},{4,24},{8,20},{12,16},{16,12},{20,8},{24,4},{28,0},{1,29},{... | collective-permute-start | bytes 368648 | tf_op jit(solution)/shard_map/ppermute | solution.py:632
  73.9 1.8 %collective-permute-start.16 = (bf16[80,768]{1,0:T(8,128)(2,1)S(1)}, bf16[80,768]{1,0:T(8,128)(2,1)S(1)}, u32[]{:S(2)}, u32[]{:S(2)}) collective-permute-start(bf16[80,768]{1,0:T(8,128)(2,1)S(1)} %get-tuple-element.53.rest_0_), channel_id=1, source_target_pairs={{0,24},{4,28},{8,16},{12,20},{16,8},{20,12},{24,0},{28,4},{1,25},{... | collective-permute-start | bytes 368648 | tf_op jit(solution)/shard_map/ppermute | solution.py:632
  75.7 1.8 %collective-permute-done.11.pb_ref = f32[64,768]{1,0:T(8,128)S(1)} collective-permute-done((f32[64,768]{1,0:T(8,128)S(1)}, f32[64,768]{1,0:T(8,128)S(1)}, u32[]{:S(2)}, u32[]{:S(2)}) %collective-permute-start.11) | collective-permute-done | bytes 196640 | tf_op jit(solution)/shard_map/ppermute | solution.py:659
  80.3 1.6 %collective-permute-start.13 = (f32[64,1024]{1,0:T(8,128)S(1)}, f32[64,1024]{1,0:T(8,128)S(1)}, u32[]{:S(2)}, u32[]{:S(2)}) collective-permute-start(f32[64,1024]{1,0:T(8,128)S(1)} %add.3.before_ref.mine_ref), channel_id=1, source_target_pairs={{0,2},{1,3},{2,0},{3,1},{4,6},{5,7},{6,4},{7,5},{8,10},{9,11},{10,... | collective-permute-start | bytes 786440 | tf_op jit(solution)/shard_map/ppermute | solution.py:671
  81.9 1.3 %collective-permute-start.18 = (bf16[80,768]{1,0:T(8,128)(2,1)S(1)}, bf16[80,768]{1,0:T(8,128)(2,1)S(1)}, u32[]{:S(2)}, u32[]{:S(2)}) collective-permute-start(bf16[80,768]{1,0:T(8,128)(2,1)S(1)} %pass_on.1.before_ref), channel_id=1, source_target_pairs={{0,16},{4,20},{8,24},{12,28},{16,0},{20,4},{24,8},{28,12},{1,17},{... | collective-permute-start | bytes 368648 | tf_op jit(solution)/shard_map/ppermute | solution.py:632
  84.2 4.4 %basis.1 = (f32[64,768]{1,0:T(8,128)}, f32[64,64]{1,0:T(8,128)S(1)}, bf16[768,384]{1,0:T(8,128)(2,1)S(1)}) custom-call(f32[64,768]{1,0:T(8,128)S(1)} %get-tuple-element.62.p_ref, f32[768,2048]{1,0:T(8,128)S(1)} %moment_add.1.before_ref.moment_ref), custom_call_target="tpu_custom_call" | custom-call | flops 10000000000 | bytes 1000000 | tf_op jit(solution)/shard_map/basis/pallas_call | solution.py:67
  90.9 2.0 %new_error_second.1 = (f32[64,2048]{1,0:T(8,128)}, bf16[768,2048]{1,0:T(8,128)(2,1)}, f32[8,128]{1,0:T(8,128)S(1)}) custom-call(s32[1]{0:T(128)} %bitcast.core_ref, f32[64,1024]{1,0:T(8,128)S(1)} %q_half.1.q_ref.mine_ref, f32[64,1024]{1,0:T(8,128)S(1)} %collective-permute-done.14.other_ref, bf16[768,384]{1,0:T(8,128)(2,1)S(1)} %get-tuple-element.66.left_ref, ...), custom_call_target="tpu_custom_call" | custom-call | flops 10000000000 | bytes 1000000 | tf_op jit(solution)/shard_map/new_error_second/pallas_call | solution.py:67
  94.2 1.3 %unpack_rows.1 = bf16[512,768]{1,0:T(8,128)(2,1)} custom-call(f32[8,128]{1,0:T(8,128)S(1)} %get-tuple-element.67.token_ref, bf16[512,320]{1,0:T(8,128)(2,1)S(1)} %pick_rows.3.rest_1_.pick_ref, bf16[512,768]{1,0:T(8,128)(2,1)S(1)} %get-tuple-element.68.first_ref, bf16[80,768]{1,0:T(8,128)(2,1)S(1)} %collective-permute-done.15.rest_0_, ...), custom_call_target="tpu_custom_call" | custom-call | flops 1000000 | bytes 10000 | tf_op jit(solution)/shard_map/unpack_rows/pallas_call | solution.py:561
  (51 shorter events, 12.4 us)
Async XLA Ops:
  0.6 35.2 %copy-start.5 = (bf16[1,2048,64]{1,2,0:T(8,128)(2,1)S(1)}, bf16[1,2048,64]{1,2,0:T(8,128)(2,1)}, u32[]{:S(2)}) copy-start(bf16[1,2048,64]{1,2,0:T(8,128)(2,1)} %param.13) | copy-start | bytes 786436
  0.6 35.2 %copy-start.2 = (bf16[1,1,640,768]{3,2,1,0:T(8,128)(2,1)S(1)}, bf16[1,1,640,768]{3,2,1,0:T(8,128)(2,1)}, u32[]{:S(2)}) copy-start(bf16[1,1,640,768]{3,2,1,0:T(8,128)(2,1)} %param.10) | copy-start | bytes 2949124
  2.9 15.0 %collective-permute-start = (bf16[80,2048]{1,0:T(8,128)(2,1)}, bf16[80,2048]{1,0:T(8,128)(2,1)S(1)}, u32[]{:S(2)}, u32[]{:S(2)}) collective-permute-start(bf16[80,2048]{1,0:T(8,128)(2,1)} %pack_first.1), channel_id=1, source_target_pairs={{0,28},{4,24},{8,20},{12,16},{16,12},{20,8},{24,4},{28,0},{1,29},{... | collective-permute-start | bytes 983048 | tf_op jit(solution)/shard_map/ppermute | solution.py:632
  12.3 17.8 %collective-permute-start.1 = (bf16[80,2048]{1,0:T(8,128)(2,1)}, bf16[80,2048]{1,0:T(8,128)(2,1)S(1)}, u32[]{:S(2)}, u32[]{:S(2)}) collective-permute-start(bf16[80,2048]{1,0:T(8,128)(2,1)} %get-tuple-element.39), channel_id=1, source_target_pairs={{0,12},{4,8},{8,4},{12,0},{16,28},{20,24},{24,20},{28,16},{1,13},{... | collective-permute-start | bytes 983048 | tf_op jit(solution)/shard_map/ppermute | solution.py:632
  12.4 23.4 %collective-permute-start.2 = (bf16[80,2048]{1,0:T(8,128)(2,1)}, bf16[80,2048]{1,0:T(8,128)(2,1)S(1)}, u32[]{:S(2)}, u32[]{:S(2)}) collective-permute-start(bf16[80,2048]{1,0:T(8,128)(2,1)} %get-tuple-element.40), channel_id=1, source_target_pairs={{0,8},{4,12},{8,0},{12,4},{16,24},{20,28},{24,16},{28,20},{1,9},{5... | collective-permute-start | bytes 983048 | tf_op jit(solution)/shard_map/ppermute | solution.py:632
  14.3 21.5 %collective-permute-start.3 = (bf16[80,2048]{1,0:T(8,128)(2,1)}, bf16[80,2048]{1,0:T(8,128)(2,1)S(1)}, u32[]{:S(2)}, u32[]{:S(2)}) collective-permute-start(bf16[80,2048]{1,0:T(8,128)(2,1)} %get-tuple-element.41), channel_id=1, source_target_pairs={{0,4},{4,0},{8,12},{12,8},{16,20},{20,16},{24,28},{28,24},{1,5},{5... | collective-permute-start | bytes 983048 | tf_op jit(solution)/shard_map/ppermute | solution.py:632
  15.8 32.3 %collective-permute-start.4 = (bf16[80,2048]{1,0:T(8,128)(2,1)}, bf16[80,2048]{1,0:T(8,128)(2,1)S(1)}, u32[]{:S(2)}, u32[]{:S(2)}) collective-permute-start(bf16[80,2048]{1,0:T(8,128)(2,1)} %get-tuple-element.44), channel_id=1, source_target_pairs={{0,24},{4,28},{8,16},{12,20},{16,8},{20,12},{24,0},{28,4},{1,25},{... | collective-permute-start | bytes 983048 | tf_op jit(solution)/shard_map/ppermute | solution.py:632
  17.9 44.3 %collective-permute-start.5 = (bf16[80,2048]{1,0:T(8,128)(2,1)}, bf16[80,2048]{1,0:T(8,128)(2,1)S(1)}, u32[]{:S(2)}, u32[]{:S(2)}) collective-permute-start(bf16[80,2048]{1,0:T(8,128)(2,1)} %get-tuple-element.45), channel_id=1, source_target_pairs={{0,20},{4,16},{8,28},{12,24},{16,4},{20,0},{24,12},{28,8},{1,21},{... | collective-permute-start | bytes 983048 | tf_op jit(solution)/shard_map/ppermute | solution.py:632
  30.1 38.1 %collective-permute-start.6 = (bf16[80,2048]{1,0:T(8,128)(2,1)}, bf16[80,2048]{1,0:T(8,128)(2,1)S(1)}, u32[]{:S(2)}, u32[]{:S(2)}) collective-permute-start(bf16[80,2048]{1,0:T(8,128)(2,1)} %get-tuple-element.46), channel_id=1, source_target_pairs={{0,16},{4,20},{8,24},{12,28},{16,0},{20,4},{24,8},{28,12},{1,17},{... | collective-permute-start | bytes 983048 | tf_op jit(solution)/shard_map/ppermute | solution.py:632
  40.6 8.9 %copy-start.7 = (s32[1,512]{1,0:T(1,128)S(1)}, s32[1,512]{1,0:T(1,128)}, u32[]{:S(2)}) copy-start(s32[1,512]{1,0:T(1,128)} %order_ref.3) | copy-start | bytes 6148
  40.6 8.9 %copy-start.8 = (s32[1,1,8]{2,1,0:T(1,128)S(1)}, s32[1,1,8]{2,1,0:T(1,128)}, u32[]{:S(2)}) copy-start(s32[1,1,8]{2,1,0:T(1,128)} %param.8) | copy-start | bytes 100
  45.6 23.5 %copy-start.4 = (bf16[1,768,2048]{2,1,0:T(8,128)(2,1)S(1)}, bf16[1,768,2048]{2,1,0:T(8,128)(2,1)}, u32[]{:S(2)}) copy-start(bf16[1,768,2048]{2,1,0:T(8,128)(2,1)} %param.11) | copy-start | bytes 9437188
  45.6 23.4 %collective-permute-start.8 = (bf16[80,768]{1,0:T(8,128)(2,1)S(1)}, bf16[80,768]{1,0:T(8,128)(2,1)S(1)}, u32[]{:S(2)}, u32[]{:S(2)}) collective-permute-start(bf16[80,768]{1,0:T(8,128)(2,1)S(1)} %get-tuple-element.49), channel_id=1, source_target_pairs={{0,12},{4,8},{8,4},{12,0},{16,28},{20,24},{24,20},{28,16},{1,13},{... | collective-permute-start | bytes 368648 | tf_op jit(solution)/shard_map/ppermute | solution.py:632
  48.0 21.0 %collective-permute-start.9 = (bf16[80,768]{1,0:T(8,128)(2,1)S(1)}, bf16[80,768]{1,0:T(8,128)(2,1)S(1)}, u32[]{:S(2)}, u32[]{:S(2)}) collective-permute-start(bf16[80,768]{1,0:T(8,128)(2,1)S(1)} %get-tuple-element.50), channel_id=1, source_target_pairs={{0,8},{4,12},{8,0},{12,4},{16,24},{20,28},{24,16},{28,20},{1,9},{5... | collective-permute-start | bytes 368648 | tf_op jit(solution)/shard_map/ppermute | solution.py:632
  48.1 20.9 %collective-permute-start.10 = (bf16[80,768]{1,0:T(8,128)(2,1)S(1)}, bf16[80,768]{1,0:T(8,128)(2,1)S(1)}, u32[]{:S(2)}, u32[]{:S(2)}) collective-permute-start(bf16[80,768]{1,0:T(8,128)(2,1)S(1)} %get-tuple-element.51), channel_id=1, source_target_pairs={{0,4},{4,0},{8,12},{12,8},{16,20},{20,16},{24,28},{28,24},{1,5},{5... | collective-permute-start | bytes 368648 | tf_op jit(solution)/shard_map/ppermute | solution.py:632
  69.0 1.5 %collective-permute-start.7 = (f32[64,768]{1,0:T(8,128)S(1)}, f32[64,768]{1,0:T(8,128)S(1)}, u32[]{:S(2)}, u32[]{:S(2)}) collective-permute-start(f32[64,768]{1,0:T(8,128)S(1)} %get-tuple-element.47.a_ref), channel_id=1, source_target_pairs={{0,1},{1,0},{2,3},{3,2},{4,5},{5,4},{6,7},{7,6},{8,9},{9,8},{10,11... | collective-permute-start | bytes 589832 | tf_op jit(solution)/shard_map/ppermute | solution.py:658
  70.5 7.0 %collective-permute-start.11 = (f32[64,768]{1,0:T(8,128)S(1)}, f32[64,768]{1,0:T(8,128)S(1)}, u32[]{:S(2)}, u32[]{:S(2)}) collective-permute-start(f32[64,768]{1,0:T(8,128)S(1)} %add.2.pa_ref), channel_id=1, source_target_pairs={{0,2},{1,3},{2,0},{3,1},{4,6},{5,7},{6,4},{7,5},{8,10},{9,11},{10,... | collective-permute-start | bytes 589832 | tf_op jit(solution)/shard_map/ppermute | solution.py:659
  72.1 20.9 %collective-permute-start.15 = (bf16[80,768]{1,0:T(8,128)(2,1)S(1)}, bf16[80,768]{1,0:T(8,128)(2,1)S(1)}, u32[]{:S(2)}, u32[]{:S(2)}) collective-permute-start(bf16[80,768]{1,0:T(8,128)(2,1)S(1)} %get-tuple-element.69), channel_id=1, source_target_pairs={{0,28},{4,24},{8,20},{12,16},{16,12},{20,8},{24,4},{28,0},{1,29},{... | collective-permute-start | bytes 368648 | tf_op jit(solution)/shard_map/ppermute | solution.py:632
  73.9 19.7 %collective-permute-start.16 = (bf16[80,768]{1,0:T(8,128)(2,1)S(1)}, bf16[80,768]{1,0:T(8,128)(2,1)S(1)}, u32[]{:S(2)}, u32[]{:S(2)}) collective-permute-start(bf16[80,768]{1,0:T(8,128)(2,1)S(1)} %get-tuple-element.53.rest_0_), channel_id=1, source_target_pairs={{0,24},{4,28},{8,16},{12,20},{16,8},{20,12},{24,0},{28,4},{1,25},{... | collective-permute-start | bytes 368648 | tf_op jit(solution)/shard_map/ppermute | solution.py:632
  75.7 17.9 %collective-permute-start.17 = (bf16[80,768]{1,0:T(8,128)(2,1)S(1)}, bf16[80,768]{1,0:T(8,128)(2,1)S(1)}, u32[]{:S(2)}, u32[]{:S(2)}) collective-permute-start(bf16[80,768]{1,0:T(8,128)(2,1)S(1)} %get-tuple-element.70), channel_id=1, source_target_pairs={{0,20},{4,16},{8,28},{12,24},{16,4},{20,0},{24,12},{28,8},{1,21},{... | collective-permute-start | bytes 368648 | tf_op jit(solution)/shard_map/ppermute | solution.py:632
  78.7 1.6 %collective-permute-start.12 = (f32[64,1024]{1,0:T(8,128)S(1)}, f32[64,1024]{1,0:T(8,128)S(1)}, u32[]{:S(2)}, u32[]{:S(2)}) collective-permute-start(f32[64,1024]{1,0:T(8,128)S(1)} %get-tuple-element.59), channel_id=1, source_target_pairs={{0,1},{1,0},{2,3},{3,2},{4,5},{5,4},{6,7},{7,6},{8,9},{9,8},{10,11... | collective-permute-start | bytes 786440 | tf_op jit(solution)/shard_map/ppermute | solution.py:661
  80.3 8.6 %collective-permute-start.13 = (f32[64,1024]{1,0:T(8,128)S(1)}, f32[64,1024]{1,0:T(8,128)S(1)}, u32[]{:S(2)}, u32[]{:S(2)}) collective-permute-start(f32[64,1024]{1,0:T(8,128)S(1)} %add.3.before_ref.mine_ref), channel_id=1, source_target_pairs={{0,2},{1,3},{2,0},{3,1},{4,6},{5,7},{6,4},{7,5},{8,10},{9,11},{10,... | collective-permute-start | bytes 786440 | tf_op jit(solution)/shard_map/ppermute | solution.py:671
  81.9 12.3 %collective-permute-start.18 = (bf16[80,768]{1,0:T(8,128)(2,1)S(1)}, bf16[80,768]{1,0:T(8,128)(2,1)S(1)}, u32[]{:S(2)}, u32[]{:S(2)}) collective-permute-start(bf16[80,768]{1,0:T(8,128)(2,1)S(1)} %pass_on.1.before_ref), channel_id=1, source_target_pairs={{0,16},{4,20},{8,24},{12,28},{16,0},{20,4},{24,8},{28,12},{1,17},{... | collective-permute-start | bytes 368648 | tf_op jit(solution)/shard_map/ppermute | solution.py:632
  89.3 1.6 %collective-permute-start.14 = (f32[64,1024]{1,0:T(8,128)S(1)}, f32[64,1024]{1,0:T(8,128)S(1)}, u32[]{:S(2)}, u32[]{:S(2)}) collective-permute-start(f32[64,1024]{1,0:T(8,128)S(1)} %q_half.1.q_ref.mine_ref), channel_id=1, source_target_pairs={{0,1},{1,0},{2,3},{3,2},{4,5},{5,4},{6,7},{7,6},{8,9},{9,8},{10,11... | collective-permute-start | bytes 786440 | tf_op jit(solution)/shard_map/ppermute | solution.py:672
  (4 other events, 13.2 us)

commit v4 on v2

--- a/solution.py
+++ b/solution.py
@@ -80,7 +80,50 @@
     )(*scalars, *operands)
 
 
-def pack_kernel(n, cap, masks, me_ref, core_ref, counts_hbm, rows_hbm, *rest):
+def start_of(counts_ref, expert, n):
+    start = jnp.int32(0)
+    for e in range(n):
+        start = start + jnp.where(e < expert, counts_ref[0, e], 0)
+    return start
+
+
+def pack_first_kernel(n, mask, me_ref, core_ref, counts_hbm, rows_hbm, out_ref, counts_ref, rows_ref, sems):
+    cap = out_ref.shape[0]
+    total, window = rows_hbm.shape[0], rows_ref.shape[0]
+    dest = me_ref[0] ^ mask
+    base = jnp.clip(total - cap * (n - dest), 0, total - window)
+    base = pl.multiple_of(base, ROW_TILE)
+    copy_counts = pltpu.make_async_copy(counts_hbm, counts_ref, sems.at[0])
+    copy_rows = pltpu.make_async_copy(rows_hbm.at[pl.ds(base, window), :], rows_ref, sems.at[1])
+    copy_counts.start()
+    copy_rows.start()
+    copy_counts.wait()
+    j = lax.broadcasted_iota(jnp.int32, (cap, window), 0)
+    w = lax.broadcasted_iota(jnp.int32, (cap, window), 1)
+    hit = (w == j + (start_of(counts_ref, dest, n) - base)) & (j < counts_ref[0, dest])
+    pick = jnp.where(hit, 1.0, 0.0).astype(BF16)
+    copy_rows.wait()
+    out_ref[...] = dot_nn(pick, rows_ref[...]).astype(BF16)
+
+
+def pack_first(me, core, counts, rows, n, cap, mask):
+    total, width = rows.shape
+    window = min(total, cap * (n + 1) - total)
+    return call(
+        functools.partial(pack_first_kernel, n, mask),
+        "pack_first",
+        (me, core),
+        (counts, rows),
+        [((cap, width), BF16)],
+        [pltpu.SMEM(counts.shape, jnp.int32), pltpu.VMEM((window, width), BF16), pltpu.SemaphoreType.DMA((2,))],
+        specs=[in_hbm()] * 2,
+        limit=62,
+        flops=10**6,
+        nbytes=4 * 10**6,
+    )[0]
+
+
+def pack_kernel(n, cap, masks, me_ref, counts_hbm, rows_hbm, *rest):
     outs = rest[: len(masks)]
     counts_ref, rows_ref, held, sems, out_sems = rest[len(masks) :]
     total = rows_ref.shape[0]
@@ -95,17 +138,12 @@
     bases, picks = [], []
     for mask in masks:
         dest = me_ref[0] ^ mask
-        start = jnp.int32(0)
-        for e in range(n):
-            start = start + jnp.where(e < dest, counts_ref[0, e], 0)
+        start = start_of(counts_ref, dest, n)
         base = jnp.minimum((start // ROW_TILE) * ROW_TILE, total - window)
         bases.append(pl.multiple_of(base, ROW_TILE))
         hit = (w == j + (start - base)) & (j < counts_ref[0, dest])
         picks.append(jnp.where(hit, 1.0, 0.0).astype(BF16))
     copy_rows.wait()
-    if len(masks) == 1:
-        outs[0][...] = dot_nn(picks[0], rows_ref[pl.ds(bases[0], window), :]).astype(BF16)
-        return
     copies = []
     for k, (base, pick) in enumerate(zip(bases, picks)):
         held[k] = dot_nn(pick, rows_ref[pl.ds(base, window), :]).astype(BF16)
@@ -115,12 +153,12 @@
         copy.wait()
 
 
-def pack(me, core, counts, rows, n, cap, masks, nbytes, out_spec, limit):
+def pack(me, counts, rows, n, cap, masks):
     count, width = len(masks), rows.shape[1]
     return call(
         functools.partial(pack_kernel, n, cap, masks),
         "pack_rows",
-        (me, core),
+        (me,),
         (counts, rows),
         [((cap, width), BF16)] * count,
         [
@@ -131,10 +169,10 @@
             pltpu.SemaphoreType.DMA((count,)),
         ],
         specs=[in_hbm()] * 2,
-        out_specs=[out_spec] * count,
-        limit=limit,
+        out_specs=[in_hbm()] * count,
+        limit=FULL,
         flops=10**6,
-        nbytes=nbytes,
+        nbytes=10**4,
     )
 
 
@@ -189,21 +227,21 @@
     )
 
 
-def late_kernel(slots, me_ref, q_ref, hidden_ref, base_ref, *rest):
+def late_kernel(slots, me_ref, weight_ref, q_ref, hidden_ref, base_ref, *rest):
     chunks, (p_ref, both_ref) = rest[: len(slots)], rest[len(slots) :]
     width = chunks[0].shape[1]
     place(chunks, slots, me_ref, hidden_ref, both_ref, 0)
     p_ref[...] = base_ref[...] + p_term(q_ref[...], both_ref[:, :width], both_ref[:, width:])
 
 
-def late_part(me, q, hidden, base, chunks, slots):
+def late_part(me, weight, q, hidden, base, chunks, slots):
     cap, width = chunks[0].shape
     ff = hidden.shape[1]
     return call(
         functools.partial(late_kernel, slots),
         "late_rows",
         (me,),
-        (q, hidden, base, *chunks),
+        (weight, q, hidden, base, *chunks),
         [((q.shape[0], ff), F32), ((cap * len(slots), width + ff), BF16)],
         flops=10**6,
         nbytes=10**4,
@@ -240,7 +278,7 @@
         out_ref[:, j : j + COLS] = fold3(res)
 
 
-def s_send_kernel(count, core_ref, pa_ref, pb_ref, error_ref, *rest):
+def s_send_kernel(count, core_ref, before_ref, pa_ref, pb_ref, error_ref, *rest):
     groups = rest[:count]
     p_out, send_ref, p3_ref, *y_refs = rest[count:]
     total = pa_ref[...] + pb_ref[...]
@@ -252,14 +290,14 @@
     s_columns(1 - core_ref[0], p3_ref[...], [y[...] for y in y_refs], error_ref, groups, send_ref)
 
 
-def s_send(core, pa, pb, error, groups):
+def s_send(core, before, pa, pb, error, groups):
     rank, ff = pa.shape
     width = error.shape[1]
     return call(
         functools.partial(s_send_kernel, len(groups)),
         "s_send",
         (core,),
-        (pa, pb, error, *groups),
+        (before, pa, pb, error, *groups),
         [((rank, ff), F32), ((rank, width // 2), F32), ((3 * rank, ff), BF16)]
         + [((3 * rank, group.shape[0]), BF16) for group in groups],
         nbytes=7 * 10**6,
@@ -543,6 +581,14 @@
     return returned[row_base[expert_of] + order_local]
 
 
+def gap_kernel(*refs):
+    set_token(refs[-1])
+
+
+def gap(*before):
+    return call(gap_kernel, "gap", (), before, [TOKEN], limit=4, flops=10**10)[0]
+
+
 def add_kernel(a_ref, b_ref, *rest):
     rest[-1][...] = a_ref[...] + b_ref[...]
 
@@ -572,7 +618,7 @@
     core = (lax.axis_index("dp").astype(jnp.int32) & 1)[None]
     core_pairs = [(d, d ^ 1) for d in range(n_dp)]
     chip_pairs = [(d, d ^ 2) for d in range(n_dp)]
-    by_pairs = n_expert == 8 and capacity % ROW_TILE == 0
+    by_pairs = n_expert == 8 and capacity % ROW_TILE == 0 and rows.shape[0] % ROW_TILE == 0
 
     if by_pairs:
         far = tuple(reversed(range(n_expert // 2, n_expert)))
@@ -583,8 +629,8 @@
             return lax.ppermute(x, "expert", [(e, e ^ mask) for e in range(n_expert)])
 
         others = far[1:] + near
-        packed = {far[0]: pack(me, core, counts[0], rows, n_expert, capacity, far[:1], 4 * 10**6, whole_vmem(), 62)[0]}
-        packed.update(zip(others, pack(me, core, counts[0], rows, n_expert, capacity, others, 10**4, in_hbm(), FULL)))
+        packed = {far[0]: pack_first(me, core, counts[0], rows, n_expert, capacity, far[0])}
+        packed.update(zip(others, pack(me, counts[0], rows, n_expert, capacity, others)))
         arrived = {m: swap(packed[m], m) if m else packed[m] for m in far + near}
         pick_near = pick_of(me, count, order, n_expert, capacity, near)
         pick_far = pick_of(me, count, order, n_expert, capacity, far)
@@ -592,12 +638,10 @@
             me, q, saved, error, weight, [arrived[m] for m in first], first
         )
         back_near = [swap(x, m) if m else x for x, m in zip(back[1:], near)]
-        p_mine, both_last = late_part(me, q, saved, p_first, [arrived[m] for m in last], last)
-        back_next = slot_grads(
-            both_last, weight, (pick_near, pick_far, *back_near), 0, capacity, len(last), 10**10
-        )
-        back_soon = pass_on(back[0], back_next[0])
-        before, groups = back_next[:1], [both_first, both_last]
+        p_mine, both_last = late_part(me, weight, q, saved, p_first, [arrived[m] for m in last], last)
+        back_soon = pass_on(back[0], p_mine)
+        before = [gap(p_mine, pick_near, pick_far, *back_near)]
+        groups = [both_first, both_last]
     else:
         outgoing = pack_plain(count, rows, n_expert, capacity)
         arrived = lax.all_to_all(outgoing, "expert", split_axis=0, concat_axis=0, tiled=True)
@@ -609,10 +653,12 @@
         returned = returned.reshape(n_expert * capacity, ff)
     p_chip = add(p_mine, lax.ppermute(p_mine, "dp", core_pairs), *before)
     p_far = lax.ppermute(p_chip, "dp", chip_pairs)
+    before = p_chip
     if by_pairs:
-        back_sent = [pass_on(x, p_chip) for x in back_next[:-1]]
-        moment = moment_add(back_sent[-1], moment, both_last)
-    p_total, s_sent, p3, *ys = s_send(core, p_chip, p_far, error, groups)
+        back_next = slot_grads(both_last, weight, (p_chip,), 0, capacity, len(last), 10**6)
+        moment = moment_add(back_next[0], moment, both_last)
+        before = back_next[0]
+    p_total, s_sent, p3, *ys = s_send(core, before, p_chip, p_far, error, groups)
     s_swapped = lax.ppermute(s_sent, "dp", core_pairs)
     s_kept, token = s_keep(core, p3, ys, error, groups)
     if by_pairs:
@@ -620,7 +666,7 @@
     s_half = add(s_kept, s_swapped, token)
     if by_pairs:
         back_last = pass_on(back_next[-1], s_half)
-        back_far = [swap(x, m) for x, m in zip([back_soon, *back_sent, back_last], far)]
+        back_far = [swap(x, m) for x, m in zip([back_soon, *back_next[:-1], back_last], far)]
     basis, linv, left = basis_of(p_total, back_last if by_pairs else p_total)
     q_mine = q_half(s_half, lax.ppermute(s_half, "dp", chip_pairs), linv, n_dp)
     q_other = lax.ppermute(q_mine, "dp", core_pairs)

time: 96.7 us -> 95.2 us (0.984)
  waiting for transfers between devices: 31.4 us -> 29 us
  starting transfers between devices: 33.2 us -> 34.7 us
    ppermute x14, starting transfers between devices: 29.9 us -> 31.4 us  [swap(): return lax.ppermute(x, 'expert', [(e, e ^ mask) for e in range(n_expert)])]
    ppermute x1, waiting for transfers between devices: 2.57 us -> 1.14 us  [shards(): q_mine = q_half(s_half, lax.ppermute(s_half, 'dp', chip_pairs), linv, n_dp)]
    pallas_call x21 -> x20, Pallas kernels: 26 us -> 25.5 us  [call(): pl.pallas_call(kernel, grid_spec=pltpu.PrefetchScalarGridSpec(num_scalar_...]
where the time goes in v4:
time: 95.2 us; the launch traced here: 94.9 us
  starting transfers between devices  34.7 us (36%)
  waiting for transfers between devices  29 us (30%)
  Pallas kernels  25.5 us (27%)
  local copies, waits for them, and re-layouts  4.77 us (5%)
  between operations  1.04 us (1%)
    ppermute x14, starting transfers between devices, swap(): return lax.ppermute(x, 'expert', [(e, e ^ mask) for e in range(n_expert)])  31.4 us
    ppermute x14, waiting for transfers between devices, swap(): return lax.ppermute(x, 'expert', [(e, e ^ mask) for e in range(n_expert)])  26.1 us
    pallas_call x20, Pallas kernels, call(): pl.pallas_call(kernel, grid_spec=pltpu.PrefetchScalarGridSpec(num_scalar_...  25.5 us
    unnamed x18, local copies, waits for them, and re-layouts  4.77 us
  transfers between devices with their start and end apart: 19, of which 8 were waited for; matrix products, arithmetic and copies ran while one was open for 0% of the time, Pallas kernels for 22%

profile of v4, /device:TPU:0, one launch (start us, length us, event | category | flops | bytes accessed | tf_op | source)
XLA Modules:
  0.0 94.9 jit_solution(18108147975678537866)
XLA Ops:
  0.7 2.3 %pack_first.1 = bf16[80,2048]{1,0:T(8,128)(2,1)} custom-call(s32[1]{0:T(128)} %bitcast.1.me_ref, s32[1]{0:T(128)} %bitcast.core_ref, s32[1,8]{1,0:T(1,128)} %bitcast.29, bf16[512,2048]{1,0:T(8,128)(2,1)} %bitcast.33), custom_call_target="tpu_custom_call" | custom-call | flops 1000000 | bytes 4000000 | tf_op jit(solution)/shard_map/pack_first/pallas_call | solution.py:67
  2.9 6.1 %collective-permute-start = (bf16[80,2048]{1,0:T(8,128)(2,1)}, bf16[80,2048]{1,0:T(8,128)(2,1)S(1)}, u32[]{:S(2)}, u32[]{:S(2)}) collective-permute-start(bf16[80,2048]{1,0:T(8,128)(2,1)} %pack_first.1), channel_id=1, source_target_pairs={{0,28},{4,24},{8,20},{12,16},{16,12},{20,8},{24,4},{28,0},{1,29},{... | collective-permute-start | bytes 983048 | tf_op jit(solution)/shard_map/ppermute | solution.py:629
  9.0 3.3 %pack_rows.1 = (bf16[80,2048]{1,0:T(8,128)(2,1)}, bf16[80,2048]{1,0:T(8,128)(2,1)}, bf16[80,2048]{1,0:T(8,128)(2,1)}, bf16[80,2048]{1,0:T(8,128)(2,1)}, bf16[80,...) custom-call(s32[1]{0:T(128)} %bitcast.1.me_ref, s32[1,8]{1,0:T(1,128)} %bitcast.30, ...), custom_call_target="tpu_custom_call" | custom-call | flops 1000000 | bytes 10000 | tf_op jit(solution)/shard_map/pack_rows/pallas_call | solution.py:67
  12.4 2.0 %collective-permute-start.2 = (bf16[80,2048]{1,0:T(8,128)(2,1)}, bf16[80,2048]{1,0:T(8,128)(2,1)S(1)}, u32[]{:S(2)}, u32[]{:S(2)}) collective-permute-start(bf16[80,2048]{1,0:T(8,128)(2,1)} %get-tuple-element.40), channel_id=1, source_target_pairs={{0,8},{4,12},{8,0},{12,4},{16,24},{20,28},{24,16},{28,20},{1,9},{5... | collective-permute-start | bytes 983048 | tf_op jit(solution)/shard_map/ppermute | solution.py:629
  14.3 1.5 %collective-permute-start.3 = (bf16[80,2048]{1,0:T(8,128)(2,1)}, bf16[80,2048]{1,0:T(8,128)(2,1)S(1)}, u32[]{:S(2)}, u32[]{:S(2)}) collective-permute-start(bf16[80,2048]{1,0:T(8,128)(2,1)} %get-tuple-element.41), channel_id=1, source_target_pairs={{0,4},{4,0},{8,12},{12,8},{16,20},{20,16},{24,28},{28,24},{1,5},{5... | collective-permute-start | bytes 983048 | tf_op jit(solution)/shard_map/ppermute | solution.py:629
  16.1 1.8 %collective-permute-done.rest_0_ = bf16[80,2048]{1,0:T(8,128)(2,1)S(1)} collective-permute-done((bf16[80,2048]{1,0:T(8,128)(2,1)}, bf16[80,2048]{1,0:T(8,128)(2,1)S(1)}, u32[]{:S(2)}, u32[]{:S(2)}) %collective-permute-start) | collective-permute-done | bytes 327712 | tf_op jit(solution)/shard_map/ppermute | solution.py:629
  17.9 12.2 %collective-permute-start.5 = (bf16[80,2048]{1,0:T(8,128)(2,1)}, bf16[80,2048]{1,0:T(8,128)(2,1)S(1)}, u32[]{:S(2)}, u32[]{:S(2)}) collective-permute-start(bf16[80,2048]{1,0:T(8,128)(2,1)} %get-tuple-element.45), channel_id=1, source_target_pairs={{0,20},{4,16},{8,28},{12,24},{16,4},{20,0},{24,12},{28,8},{1,21},{... | collective-permute-start | bytes 983048 | tf_op jit(solution)/shard_map/ppermute | solution.py:629
  30.1 5.7 %collective-permute-done.2.rest_2_ = bf16[80,2048]{1,0:T(8,128)(2,1)S(1)} collective-permute-done((bf16[80,2048]{1,0:T(8,128)(2,1)}, bf16[80,2048]{1,0:T(8,128)(2,1)S(1)}, u32[]{:S(2)}, u32[]{:S(2)}) %collective-permute-start.2) | collective-permute-done | bytes 327712 | tf_op jit(solution)/shard_map/ppermute | solution.py:629
  35.8 1.9 %copy-done = bf16[1,768,2048]{2,1,0:T(8,128)(2,1)S(1)} copy-done((bf16[1,768,2048]{2,1,0:T(8,128)(2,1)S(1)}, bf16[1,768,2048]{2,1,0:T(8,128)(2,1)}, u32[]{:S(2)}) %copy-start) | copy-done | bytes 3145752
  37.7 1.9 %copy-done.2 = bf16[1,1,768,2048]{3,2,1,0:T(8,128)(2,1)S(1)} copy-done((bf16[1,1,768,2048]{3,2,1,0:T(8,128)(2,1)S(1)}, bf16[1,1,768,2048]{3,2,1,0:T(8,128)(2,1)}, u32[]{:S(2)}) %copy-start.2) | copy-done | bytes 3145752
  40.6 5.0 %early_rows.1 = (f32[64,768]{1,0:T(8,128)S(1)}, bf16[400,2816]{1,0:T(8,128)(2,1)S(1)}, f32[768,2048]{1,0:T(8,128)S(1)}, bf16[80,768]{1,0:T(8,128)(2,1)S(1)}, bf1...) custom-call(s32[1]{0:T(128)} %bitcast.1.me_ref, ...), custom_call_target="tpu_custom_call" | custom-call | flops 2000000000 | bytes 10000000 | tf_op jit(solution)/shard_map/early_rows/pallas_call | solution.py:67
  45.6 2.4 %collective-permute-start.8 = (bf16[80,768]{1,0:T(8,128)(2,1)S(1)}, bf16[80,768]{1,0:T(8,128)(2,1)S(1)}, u32[]{:S(2)}, u32[]{:S(2)}) collective-permute-start(bf16[80,768]{1,0:T(8,128)(2,1)S(1)} %get-tuple-element.49), channel_id=1, source_target_pairs={{0,12},{4,8},{8,4},{12,0},{16,28},{20,24},{24,20},{28,16},{1,13},{... | collective-permute-start | bytes 368648 | tf_op jit(solution)/shard_map/ppermute | solution.py:629
  48.1 1.4 %collective-permute-start.10 = (bf16[80,768]{1,0:T(8,128)(2,1)S(1)}, bf16[80,768]{1,0:T(8,128)(2,1)S(1)}, u32[]{:S(2)}, u32[]{:S(2)}) collective-permute-start(bf16[80,768]{1,0:T(8,128)(2,1)S(1)} %get-tuple-element.51), channel_id=1, source_target_pairs={{0,4},{4,0},{8,12},{12,8},{16,20},{20,16},{24,28},{28,24},{1,5},{5... | collective-permute-start | bytes 368648 | tf_op jit(solution)/shard_map/ppermute | solution.py:629
  51.0 11.2 %collective-permute-done.5.rest_1_ = bf16[80,2048]{1,0:T(8,128)(2,1)S(1)} collective-permute-done((bf16[80,2048]{1,0:T(8,128)(2,1)}, bf16[80,2048]{1,0:T(8,128)(2,1)S(1)}, u32[]{:S(2)}, u32[]{:S(2)}) %collective-permute-start.5) | collective-permute-done | bytes 327712 | tf_op jit(solution)/shard_map/ppermute | solution.py:629
  62.1 6.1 %collective-permute-done.6.rest_2_ = bf16[80,2048]{1,0:T(8,128)(2,1)S(1)} collective-permute-done((bf16[80,2048]{1,0:T(8,128)(2,1)}, bf16[80,2048]{1,0:T(8,128)(2,1)S(1)}, u32[]{:S(2)}, u32[]{:S(2)}) %collective-permute-start.6) | collective-permute-done | bytes 327712 | tf_op jit(solution)/shard_map/ppermute | solution.py:629
  69.1 2.0 %collective-permute-start.15 = (bf16[80,768]{1,0:T(8,128)(2,1)S(1)}, bf16[80,768]{1,0:T(8,128)(2,1)S(1)}, u32[]{:S(2)}, u32[]{:S(2)}) collective-permute-start(bf16[80,768]{1,0:T(8,128)(2,1)S(1)} %pass_on.3), channel_id=1, source_target_pairs={{0,28},{4,24},{8,20},{12,16},{16,12},{20,8},{24,4},{28,0},{1,29},{... | collective-permute-start | bytes 368648 | tf_op jit(solution)/shard_map/ppermute | solution.py:629
  71.1 1.5 %collective-permute-start.11 = (f32[64,768]{1,0:T(8,128)S(1)}, f32[64,768]{1,0:T(8,128)S(1)}, u32[]{:S(2)}, u32[]{:S(2)}) collective-permute-start(f32[64,768]{1,0:T(8,128)S(1)} %add.2.rest_0_.pa_ref), channel_id=1, source_target_pairs={{0,2},{1,3},{2,0},{3,1},{4,6},{5,7},{6,4},{7,5},{8,10},{9,11},{10,... | collective-permute-start | bytes 589832 | tf_op jit(solution)/shard_map/ppermute | solution.py:655
  73.6 1.8 %collective-permute-start.16 = (bf16[80,768]{1,0:T(8,128)(2,1)S(1)}, bf16[80,768]{1,0:T(8,128)(2,1)S(1)}, u32[]{:S(2)}, u32[]{:S(2)}) collective-permute-start(bf16[80,768]{1,0:T(8,128)(2,1)S(1)} %get-tuple-element.53.before_ref), channel_id=1, source_target_pairs={{0,24},{4,28},{8,16},{12,20},{16,8},{20,12},{24,0},{28,4},{1,25},{... | collective-permute-start | bytes 368648 | tf_op jit(solution)/shard_map/ppermute | solution.py:629
  76.6 1.6 %collective-permute-done.11.pb_ref = f32[64,768]{1,0:T(8,128)S(1)} collective-permute-done((f32[64,768]{1,0:T(8,128)S(1)}, f32[64,768]{1,0:T(8,128)S(1)}, u32[]{:S(2)}, u32[]{:S(2)}) %collective-permute-start.11) | collective-permute-done | bytes 196640 | tf_op jit(solution)/shard_map/ppermute | solution.py:655
  81.0 1.5 %collective-permute-start.13 = (f32[64,1024]{1,0:T(8,128)S(1)}, f32[64,1024]{1,0:T(8,128)S(1)}, u32[]{:S(2)}, u32[]{:S(2)}) collective-permute-start(f32[64,1024]{1,0:T(8,128)S(1)} %add.3.before_ref.mine_ref), channel_id=1, source_target_pairs={{0,2},{1,3},{2,0},{3,1},{4,6},{5,7},{6,4},{7,5},{8,10},{9,11},{10,... | collective-permute-start | bytes 786440 | tf_op jit(solution)/shard_map/ppermute | solution.py:671
  82.5 1.5 %collective-permute-start.18 = (bf16[80,768]{1,0:T(8,128)(2,1)S(1)}, bf16[80,768]{1,0:T(8,128)(2,1)S(1)}, u32[]{:S(2)}, u32[]{:S(2)}) collective-permute-start(bf16[80,768]{1,0:T(8,128)(2,1)S(1)} %pass_on.2.before_ref), channel_id=1, source_target_pairs={{0,16},{4,20},{8,24},{12,28},{16,0},{20,4},{24,8},{28,12},{1,17},{... | collective-permute-start | bytes 368648 | tf_op jit(solution)/shard_map/ppermute | solution.py:629
  84.0 4.4 %basis.1 = (f32[64,768]{1,0:T(8,128)}, f32[64,64]{1,0:T(8,128)S(1)}, bf16[768,384]{1,0:T(8,128)(2,1)S(1)}) custom-call(f32[64,768]{1,0:T(8,128)S(1)} %get-tuple-element.62.p_ref, bf16[80,768]{1,0:T(8,128)(2,1)S(1)} %pass_on.2.before_ref), custom_call_target="tpu_custom_call" | custom-call | flops 10000000000 | bytes 1000000 | tf_op jit(solution)/shard_map/basis/pallas_call | solution.py:67
  91.1 1.3 %collective-permute-done.18.rest_5_ = bf16[80,768]{1,0:T(8,128)(2,1)S(1)} collective-permute-done((bf16[80,768]{1,0:T(8,128)(2,1)S(1)}, bf16[80,768]{1,0:T(8,128)(2,1)S(1)}, u32[]{:S(2)}, u32[]{:S(2)}) %collective-permute-start.18) | collective-permute-done | bytes 122912 | tf_op jit(solution)/shard_map/ppermute | solution.py:629
  92.4 2.4 %new_error_last.1 = (f32[64,2048]{1,0:T(8,128)}, bf16[768,2048]{1,0:T(8,128)(2,1)}, bf16[512,768]{1,0:T(8,128)(2,1)}) custom-call(s32[1]{0:T(128)} %bitcast.core_ref, f32[64,1024]{1,0:T(8,128)S(1)} %q_half.1.q_ref.mine_ref, f32[64,1024]{1,0:T(8,128)S(1)} %collective-permute-done.14.other_ref, bf16[768,384]{1,0:T(8,128)(2,1)S(1)} %get-tuple-element.65.left_ref, ...), custom_call_target="tpu_custom_call" | custom-call | flops 10000000000 | bytes 1000000 | tf_op jit(solution)/shard_map/new_error_last/pallas_call | solution.py:67
  (52 shorter events, 11.2 us)
Async XLA Ops:
  0.6 35.2 %copy-start.5 = (bf16[1,2048,64]{1,2,0:T(8,128)(2,1)S(1)}, bf16[1,2048,64]{1,2,0:T(8,128)(2,1)}, u32[]{:S(2)}) copy-start(bf16[1,2048,64]{1,2,0:T(8,128)(2,1)} %param.13) | copy-start | bytes 786436
  0.6 35.2 %copy-start.4 = (bf16[1,1,640,768]{3,2,1,0:T(8,128)(2,1)S(1)}, bf16[1,1,640,768]{3,2,1,0:T(8,128)(2,1)}, u32[]{:S(2)}) copy-start(bf16[1,1,640,768]{3,2,1,0:T(8,128)(2,1)} %param.10) | copy-start | bytes 2949124
  2.9 15.0 %collective-permute-start = (bf16[80,2048]{1,0:T(8,128)(2,1)}, bf16[80,2048]{1,0:T(8,128)(2,1)S(1)}, u32[]{:S(2)}, u32[]{:S(2)}) collective-permute-start(bf16[80,2048]{1,0:T(8,128)(2,1)} %pack_first.1), channel_id=1, source_target_pairs={{0,28},{4,24},{8,20},{12,16},{16,12},{20,8},{24,4},{28,0},{1,29},{... | collective-permute-start | bytes 983048 | tf_op jit(solution)/shard_map/ppermute | solution.py:629
  12.3 17.8 %collective-permute-start.1 = (bf16[80,2048]{1,0:T(8,128)(2,1)}, bf16[80,2048]{1,0:T(8,128)(2,1)S(1)}, u32[]{:S(2)}, u32[]{:S(2)}) collective-permute-start(bf16[80,2048]{1,0:T(8,128)(2,1)} %get-tuple-element.39), channel_id=1, source_target_pairs={{0,12},{4,8},{8,4},{12,0},{16,28},{20,24},{24,20},{28,16},{1,13},{... | collective-permute-start | bytes 983048 | tf_op jit(solution)/shard_map/ppermute | solution.py:629
  12.4 23.4 %collective-permute-start.2 = (bf16[80,2048]{1,0:T(8,128)(2,1)}, bf16[80,2048]{1,0:T(8,128)(2,1)S(1)}, u32[]{:S(2)}, u32[]{:S(2)}) collective-permute-start(bf16[80,2048]{1,0:T(8,128)(2,1)} %get-tuple-element.40), channel_id=1, source_target_pairs={{0,8},{4,12},{8,0},{12,4},{16,24},{20,28},{24,16},{28,20},{1,9},{5... | collective-permute-start | bytes 983048 | tf_op jit(solution)/shard_map/ppermute | solution.py:629
  14.3 21.5 %collective-permute-start.3 = (bf16[80,2048]{1,0:T(8,128)(2,1)}, bf16[80,2048]{1,0:T(8,128)(2,1)S(1)}, u32[]{:S(2)}, u32[]{:S(2)}) collective-permute-start(bf16[80,2048]{1,0:T(8,128)(2,1)} %get-tuple-element.41), channel_id=1, source_target_pairs={{0,4},{4,0},{8,12},{12,8},{16,20},{20,16},{24,28},{28,24},{1,5},{5... | collective-permute-start | bytes 983048 | tf_op jit(solution)/shard_map/ppermute | solution.py:629
  15.8 32.3 %collective-permute-start.4 = (bf16[80,2048]{1,0:T(8,128)(2,1)}, bf16[80,2048]{1,0:T(8,128)(2,1)S(1)}, u32[]{:S(2)}, u32[]{:S(2)}) collective-permute-start(bf16[80,2048]{1,0:T(8,128)(2,1)} %get-tuple-element.44), channel_id=1, source_target_pairs={{0,24},{4,28},{8,16},{12,20},{16,8},{20,12},{24,0},{28,4},{1,25},{... | collective-permute-start | bytes 983048 | tf_op jit(solution)/shard_map/ppermute | solution.py:629
  17.9 44.3 %collective-permute-start.5 = (bf16[80,2048]{1,0:T(8,128)(2,1)}, bf16[80,2048]{1,0:T(8,128)(2,1)S(1)}, u32[]{:S(2)}, u32[]{:S(2)}) collective-permute-start(bf16[80,2048]{1,0:T(8,128)(2,1)} %get-tuple-element.45), channel_id=1, source_target_pairs={{0,20},{4,16},{8,28},{12,24},{16,4},{20,0},{24,12},{28,8},{1,21},{... | collective-permute-start | bytes 983048 | tf_op jit(solution)/shard_map/ppermute | solution.py:629
  30.1 38.1 %collective-permute-start.6 = (bf16[80,2048]{1,0:T(8,128)(2,1)}, bf16[80,2048]{1,0:T(8,128)(2,1)S(1)}, u32[]{:S(2)}, u32[]{:S(2)}) collective-permute-start(bf16[80,2048]{1,0:T(8,128)(2,1)} %get-tuple-element.46), channel_id=1, source_target_pairs={{0,16},{4,20},{8,24},{12,28},{16,0},{20,4},{24,8},{28,12},{1,17},{... | collective-permute-start | bytes 983048 | tf_op jit(solution)/shard_map/ppermute | solution.py:629
  40.6 8.9 %copy-start.7 = (s32[1,512]{1,0:T(1,128)S(1)}, s32[1,512]{1,0:T(1,128)}, u32[]{:S(2)}) copy-start(s32[1,512]{1,0:T(1,128)} %order_ref.3) | copy-start | bytes 6148
  40.6 8.9 %copy-start.8 = (s32[1,1,8]{2,1,0:T(1,128)S(1)}, s32[1,1,8]{2,1,0:T(1,128)}, u32[]{:S(2)}) copy-start(s32[1,1,8]{2,1,0:T(1,128)} %param.8) | copy-start | bytes 100
  40.6 27.6 %copy-start.1 = (bf16[1,768,2048]{2,1,0:T(8,128)(2,1)S(1)}, bf16[1,768,2048]{2,1,0:T(8,128)(2,1)}, u32[]{:S(2)}) copy-start(bf16[1,768,2048]{2,1,0:T(8,128)(2,1)} %param.11) | copy-start | bytes 9437188
  45.6 25.4 %collective-permute-start.8 = (bf16[80,768]{1,0:T(8,128)(2,1)S(1)}, bf16[80,768]{1,0:T(8,128)(2,1)S(1)}, u32[]{:S(2)}, u32[]{:S(2)}) collective-permute-start(bf16[80,768]{1,0:T(8,128)(2,1)S(1)} %get-tuple-element.49), channel_id=1, source_target_pairs={{0,12},{4,8},{8,4},{12,0},{16,28},{20,24},{24,20},{28,16},{1,13},{... | collective-permute-start | bytes 368648 | tf_op jit(solution)/shard_map/ppermute | solution.py:629
  48.0 23.0 %collective-permute-start.9 = (bf16[80,768]{1,0:T(8,128)(2,1)S(1)}, bf16[80,768]{1,0:T(8,128)(2,1)S(1)}, u32[]{:S(2)}, u32[]{:S(2)}) collective-permute-start(bf16[80,768]{1,0:T(8,128)(2,1)S(1)} %get-tuple-element.50), channel_id=1, source_target_pairs={{0,8},{4,12},{8,0},{12,4},{16,24},{20,28},{24,16},{28,20},{1,9},{5... | collective-permute-start | bytes 368648 | tf_op jit(solution)/shard_map/ppermute | solution.py:629
  48.1 22.9 %collective-permute-start.10 = (bf16[80,768]{1,0:T(8,128)(2,1)S(1)}, bf16[80,768]{1,0:T(8,128)(2,1)S(1)}, u32[]{:S(2)}, u32[]{:S(2)}) collective-permute-start(bf16[80,768]{1,0:T(8,128)(2,1)S(1)} %get-tuple-element.51), channel_id=1, source_target_pairs={{0,4},{4,0},{8,12},{12,8},{16,20},{20,16},{24,28},{28,24},{1,5},{5... | collective-permute-start | bytes 368648 | tf_op jit(solution)/shard_map/ppermute | solution.py:629
  69.0 2.1 %collective-permute-start.7 = (f32[64,768]{1,0:T(8,128)S(1)}, f32[64,768]{1,0:T(8,128)S(1)}, u32[]{:S(2)}, u32[]{:S(2)}) collective-permute-start(f32[64,768]{1,0:T(8,128)S(1)} %get-tuple-element.48.refs_0_.a_ref.before_ref), channel_id=1, source_target_pairs={{0,1},{1,0},{2,3},{3,2},{4,5},{5,4},{6,7},{7,6},{8,9},{9,8},{10,11... | collective-permute-start | bytes 589832 | tf_op jit(solution)/shard_map/ppermute | solution.py:654
  69.1 22.0 %collective-permute-start.15 = (bf16[80,768]{1,0:T(8,128)(2,1)S(1)}, bf16[80,768]{1,0:T(8,128)(2,1)S(1)}, u32[]{:S(2)}, u32[]{:S(2)}) collective-permute-start(bf16[80,768]{1,0:T(8,128)(2,1)S(1)} %pass_on.3), channel_id=1, source_target_pairs={{0,28},{4,24},{8,20},{12,16},{16,12},{20,8},{24,4},{28,0},{1,29},{... | collective-permute-start | bytes 368648 | tf_op jit(solution)/shard_map/ppermute | solution.py:629
  71.1 7.1 %collective-permute-start.11 = (f32[64,768]{1,0:T(8,128)S(1)}, f32[64,768]{1,0:T(8,128)S(1)}, u32[]{:S(2)}, u32[]{:S(2)}) collective-permute-start(f32[64,768]{1,0:T(8,128)S(1)} %add.2.rest_0_.pa_ref), channel_id=1, source_target_pairs={{0,2},{1,3},{2,0},{3,1},{4,6},{5,7},{6,4},{7,5},{8,10},{9,11},{10,... | collective-permute-start | bytes 589832 | tf_op jit(solution)/shard_map/ppermute | solution.py:655
  73.6 17.4 %collective-permute-start.16 = (bf16[80,768]{1,0:T(8,128)(2,1)S(1)}, bf16[80,768]{1,0:T(8,128)(2,1)S(1)}, u32[]{:S(2)}, u32[]{:S(2)}) collective-permute-start(bf16[80,768]{1,0:T(8,128)(2,1)S(1)} %get-tuple-element.53.before_ref), channel_id=1, source_target_pairs={{0,24},{4,28},{8,16},{12,20},{16,8},{20,12},{24,0},{28,4},{1,25},{... | collective-permute-start | bytes 368648 | tf_op jit(solution)/shard_map/ppermute | solution.py:629
  76.5 14.6 %collective-permute-start.17 = (bf16[80,768]{1,0:T(8,128)(2,1)S(1)}, bf16[80,768]{1,0:T(8,128)(2,1)S(1)}, u32[]{:S(2)}, u32[]{:S(2)}) collective-permute-start(bf16[80,768]{1,0:T(8,128)(2,1)S(1)} %get-tuple-element.69), channel_id=1, source_target_pairs={{0,20},{4,16},{8,28},{12,24},{16,4},{20,0},{24,12},{28,8},{1,21},{... | collective-permute-start | bytes 368648 | tf_op jit(solution)/shard_map/ppermute | solution.py:629
  79.3 1.6 %collective-permute-start.12 = (f32[64,1024]{1,0:T(8,128)S(1)}, f32[64,1024]{1,0:T(8,128)S(1)}, u32[]{:S(2)}, u32[]{:S(2)}) collective-permute-start(f32[64,1024]{1,0:T(8,128)S(1)} %get-tuple-element.59), channel_id=1, source_target_pairs={{0,1},{1,0},{2,3},{3,2},{4,5},{5,4},{6,7},{7,6},{8,9},{9,8},{10,11... | collective-permute-start | bytes 786440 | tf_op jit(solution)/shard_map/ppermute | solution.py:662
  81.0 8.6 %collective-permute-start.13 = (f32[64,1024]{1,0:T(8,128)S(1)}, f32[64,1024]{1,0:T(8,128)S(1)}, u32[]{:S(2)}, u32[]{:S(2)}) collective-permute-start(f32[64,1024]{1,0:T(8,128)S(1)} %add.3.before_ref.mine_ref), channel_id=1, source_target_pairs={{0,2},{1,3},{2,0},{3,1},{4,6},{5,7},{6,4},{7,5},{8,10},{9,11},{10,... | collective-permute-start | bytes 786440 | tf_op jit(solution)/shard_map/ppermute | solution.py:671
  82.5 9.9 %collective-permute-start.18 = (bf16[80,768]{1,0:T(8,128)(2,1)S(1)}, bf16[80,768]{1,0:T(8,128)(2,1)S(1)}, u32[]{:S(2)}, u32[]{:S(2)}) collective-permute-start(bf16[80,768]{1,0:T(8,128)(2,1)S(1)} %pass_on.2.before_ref), channel_id=1, source_target_pairs={{0,16},{4,20},{8,24},{12,28},{16,0},{20,4},{24,8},{28,12},{1,17},{... | collective-permute-start | bytes 368648 | tf_op jit(solution)/shard_map/ppermute | solution.py:629
  90.0 2.4 %collective-permute-start.14 = (f32[64,1024]{1,0:T(8,128)S(1)}, f32[64,1024]{1,0:T(8,128)S(1)}, u32[]{:S(2)}, u32[]{:S(2)}) collective-permute-start(f32[64,1024]{1,0:T(8,128)S(1)} %q_half.1.q_ref.mine_ref), channel_id=1, source_target_pairs={{0,1},{1,0},{2,3},{3,2},{4,5},{5,4},{6,7},{7,6},{8,9},{9,8},{10,11... | collective-permute-start | bytes 786440 | tf_op jit(solution)/shard_map/ppermute | solution.py:672
  (4 other events, 7.4 us)

commit v5 on v4

--- a/solution.py
+++ b/solution.py
@@ -434,7 +434,7 @@
 def error_first(core, q, left, moment):
     half = q.shape[1]
     return call(
-        functools.partial(error_first_kernel, 256),
+        functools.partial(error_first_kernel, 512),
         "new_error_first",
         (core,),
         (q, left, moment),
@@ -487,7 +487,7 @@
 def last_part(core, mine, other, left, moment, first, near=None, pick=None, chunks=()):
     ff, width = moment.shape
     rank, half = mine.shape
-    block = 256
+    block = 512
     parts = 2 if chunks else 0
     operands = [mine, other, left, moment, first]
     outs = [((rank, width), F32), ((ff, width), BF16)]

time: 95.2 us -> 95.6 us (level)
  no operation moved by 1% of the time
where the time goes in v5:
time: 95.6 us; the launch traced here: 95.3 us
  starting transfers between devices  34.7 us (36%)
  waiting for transfers between devices  29 us (30%)
  Pallas kernels  25.8 us (27%)
  local copies, waits for them, and re-layouts  4.77 us (5%)
  between operations  1.04 us (1%)
    ppermute x14, starting transfers between devices, swap(): return lax.ppermute(x, 'expert', [(e, e ^ mask) for e in range(n_expert)])  31.4 us
    ppermute x14, waiting for transfers between devices, swap(): return lax.ppermute(x, 'expert', [(e, e ^ mask) for e in range(n_expert)])  26.1 us
    pallas_call x20, Pallas kernels, call(): pl.pallas_call(kernel, grid_spec=pltpu.PrefetchScalarGridSpec(num_scalar_...  25.8 us
    unnamed x18, local copies, waits for them, and re-layouts  4.77 us
  transfers between devices with their start and end apart: 19, of which 8 were waited for; matrix products, arithmetic and copies ran while one was open for 0% of the time, Pallas kernels for 22%

profile of v5, /device:TPU:0, one launch (start us, length us, event | category | flops | bytes accessed | tf_op | source)
XLA Modules:
  0.0 95.3 jit_solution(5093175186906205391)
XLA Ops:
  0.7 2.3 %pack_first.1 = bf16[80,2048]{1,0:T(8,128)(2,1)} custom-call(s32[1]{0:T(128)} %bitcast.1.me_ref, s32[1]{0:T(128)} %bitcast.core_ref, s32[1,8]{1,0:T(1,128)} %bitcast.29, bf16[512,2048]{1,0:T(8,128)(2,1)} %bitcast.33), custom_call_target="tpu_custom_call" | custom-call | flops 1000000 | bytes 4000000 | tf_op jit(solution)/shard_map/pack_first/pallas_call | solution.py:67
  2.9 6.1 %collective-permute-start = (bf16[80,2048]{1,0:T(8,128)(2,1)}, bf16[80,2048]{1,0:T(8,128)(2,1)S(1)}, u32[]{:S(2)}, u32[]{:S(2)}) collective-permute-start(bf16[80,2048]{1,0:T(8,128)(2,1)} %pack_first.1), channel_id=1, source_target_pairs={{0,28},{4,24},{8,20},{12,16},{16,12},{20,8},{24,4},{28,0},{1,29},{... | collective-permute-start | bytes 983048 | tf_op jit(solution)/shard_map/ppermute | solution.py:629
  9.0 3.3 %pack_rows.1 = (bf16[80,2048]{1,0:T(8,128)(2,1)}, bf16[80,2048]{1,0:T(8,128)(2,1)}, bf16[80,2048]{1,0:T(8,128)(2,1)}, bf16[80,2048]{1,0:T(8,128)(2,1)}, bf16[80,...) custom-call(s32[1]{0:T(128)} %bitcast.1.me_ref, s32[1,8]{1,0:T(1,128)} %bitcast.30, ...), custom_call_target="tpu_custom_call" | custom-call | flops 1000000 | bytes 10000 | tf_op jit(solution)/shard_map/pack_rows/pallas_call | solution.py:67
  12.4 2.0 %collective-permute-start.2 = (bf16[80,2048]{1,0:T(8,128)(2,1)}, bf16[80,2048]{1,0:T(8,128)(2,1)S(1)}, u32[]{:S(2)}, u32[]{:S(2)}) collective-permute-start(bf16[80,2048]{1,0:T(8,128)(2,1)} %get-tuple-element.40), channel_id=1, source_target_pairs={{0,8},{4,12},{8,0},{12,4},{16,24},{20,28},{24,16},{28,20},{1,9},{5... | collective-permute-start | bytes 983048 | tf_op jit(solution)/shard_map/ppermute | solution.py:629
  14.3 1.5 %collective-permute-start.3 = (bf16[80,2048]{1,0:T(8,128)(2,1)}, bf16[80,2048]{1,0:T(8,128)(2,1)S(1)}, u32[]{:S(2)}, u32[]{:S(2)}) collective-permute-start(bf16[80,2048]{1,0:T(8,128)(2,1)} %get-tuple-element.41), channel_id=1, source_target_pairs={{0,4},{4,0},{8,12},{12,8},{16,20},{20,16},{24,28},{28,24},{1,5},{5... | collective-permute-start | bytes 983048 | tf_op jit(solution)/shard_map/ppermute | solution.py:629
  16.1 1.8 %collective-permute-done.rest_0_ = bf16[80,2048]{1,0:T(8,128)(2,1)S(1)} collective-permute-done((bf16[80,2048]{1,0:T(8,128)(2,1)}, bf16[80,2048]{1,0:T(8,128)(2,1)S(1)}, u32[]{:S(2)}, u32[]{:S(2)}) %collective-permute-start) | collective-permute-done | bytes 327712 | tf_op jit(solution)/shard_map/ppermute | solution.py:629
  17.9 12.2 %collective-permute-start.5 = (bf16[80,2048]{1,0:T(8,128)(2,1)}, bf16[80,2048]{1,0:T(8,128)(2,1)S(1)}, u32[]{:S(2)}, u32[]{:S(2)}) collective-permute-start(bf16[80,2048]{1,0:T(8,128)(2,1)} %get-tuple-element.45), channel_id=1, source_target_pairs={{0,20},{4,16},{8,28},{12,24},{16,4},{20,0},{24,12},{28,8},{1,21},{... | collective-permute-start | bytes 983048 | tf_op jit(solution)/shard_map/ppermute | solution.py:629
  30.1 5.7 %collective-permute-done.2.rest_2_ = bf16[80,2048]{1,0:T(8,128)(2,1)S(1)} collective-permute-done((bf16[80,2048]{1,0:T(8,128)(2,1)}, bf16[80,2048]{1,0:T(8,128)(2,1)S(1)}, u32[]{:S(2)}, u32[]{:S(2)}) %collective-permute-start.2) | collective-permute-done | bytes 327712 | tf_op jit(solution)/shard_map/ppermute | solution.py:629
  35.8 1.9 %copy-done = bf16[1,768,2048]{2,1,0:T(8,128)(2,1)S(1)} copy-done((bf16[1,768,2048]{2,1,0:T(8,128)(2,1)S(1)}, bf16[1,768,2048]{2,1,0:T(8,128)(2,1)}, u32[]{:S(2)}) %copy-start) | copy-done | bytes 3145752
  37.7 1.9 %copy-done.2 = bf16[1,1,768,2048]{3,2,1,0:T(8,128)(2,1)S(1)} copy-done((bf16[1,1,768,2048]{3,2,1,0:T(8,128)(2,1)S(1)}, bf16[1,1,768,2048]{3,2,1,0:T(8,128)(2,1)}, u32[]{:S(2)}) %copy-start.2) | copy-done | bytes 3145752
  40.6 5.0 %early_rows.1 = (f32[64,768]{1,0:T(8,128)S(1)}, bf16[400,2816]{1,0:T(8,128)(2,1)S(1)}, f32[768,2048]{1,0:T(8,128)S(1)}, bf16[80,768]{1,0:T(8,128)(2,1)S(1)}, bf1...) custom-call(s32[1]{0:T(128)} %bitcast.1.me_ref, ...), custom_call_target="tpu_custom_call" | custom-call | flops 2000000000 | bytes 10000000 | tf_op jit(solution)/shard_map/early_rows/pallas_call | solution.py:67
  45.6 2.4 %collective-permute-start.8 = (bf16[80,768]{1,0:T(8,128)(2,1)S(1)}, bf16[80,768]{1,0:T(8,128)(2,1)S(1)}, u32[]{:S(2)}, u32[]{:S(2)}) collective-permute-start(bf16[80,768]{1,0:T(8,128)(2,1)S(1)} %get-tuple-element.49), channel_id=1, source_target_pairs={{0,12},{4,8},{8,4},{12,0},{16,28},{20,24},{24,20},{28,16},{1,13},{... | collective-permute-start | bytes 368648 | tf_op jit(solution)/shard_map/ppermute | solution.py:629
  48.1 1.4 %collective-permute-start.10 = (bf16[80,768]{1,0:T(8,128)(2,1)S(1)}, bf16[80,768]{1,0:T(8,128)(2,1)S(1)}, u32[]{:S(2)}, u32[]{:S(2)}) collective-permute-start(bf16[80,768]{1,0:T(8,128)(2,1)S(1)} %get-tuple-element.51), channel_id=1, source_target_pairs={{0,4},{4,0},{8,12},{12,8},{16,20},{20,16},{24,28},{28,24},{1,5},{5... | collective-permute-start | bytes 368648 | tf_op jit(solution)/shard_map/ppermute | solution.py:629
  51.0 11.2 %collective-permute-done.5.rest_1_ = bf16[80,2048]{1,0:T(8,128)(2,1)S(1)} collective-permute-done((bf16[80,2048]{1,0:T(8,128)(2,1)}, bf16[80,2048]{1,0:T(8,128)(2,1)S(1)}, u32[]{:S(2)}, u32[]{:S(2)}) %collective-permute-start.5) | collective-permute-done | bytes 327712 | tf_op jit(solution)/shard_map/ppermute | solution.py:629
  62.1 6.1 %collective-permute-done.6.rest_2_ = bf16[80,2048]{1,0:T(8,128)(2,1)S(1)} collective-permute-done((bf16[80,2048]{1,0:T(8,128)(2,1)}, bf16[80,2048]{1,0:T(8,128)(2,1)S(1)}, u32[]{:S(2)}, u32[]{:S(2)}) %collective-permute-start.6) | collective-permute-done | bytes 327712 | tf_op jit(solution)/shard_map/ppermute | solution.py:629
  69.1 2.0 %collective-permute-start.15 = (bf16[80,768]{1,0:T(8,128)(2,1)S(1)}, bf16[80,768]{1,0:T(8,128)(2,1)S(1)}, u32[]{:S(2)}, u32[]{:S(2)}) collective-permute-start(bf16[80,768]{1,0:T(8,128)(2,1)S(1)} %pass_on.3), channel_id=1, source_target_pairs={{0,28},{4,24},{8,20},{12,16},{16,12},{20,8},{24,4},{28,0},{1,29},{... | collective-permute-start | bytes 368648 | tf_op jit(solution)/shard_map/ppermute | solution.py:629
  71.1 1.5 %collective-permute-start.11 = (f32[64,768]{1,0:T(8,128)S(1)}, f32[64,768]{1,0:T(8,128)S(1)}, u32[]{:S(2)}, u32[]{:S(2)}) collective-permute-start(f32[64,768]{1,0:T(8,128)S(1)} %add.2.rest_0_.pa_ref), channel_id=1, source_target_pairs={{0,2},{1,3},{2,0},{3,1},{4,6},{5,7},{6,4},{7,5},{8,10},{9,11},{10,... | collective-permute-start | bytes 589832 | tf_op jit(solution)/shard_map/ppermute | solution.py:655
  73.6 1.8 %collective-permute-start.16 = (bf16[80,768]{1,0:T(8,128)(2,1)S(1)}, bf16[80,768]{1,0:T(8,128)(2,1)S(1)}, u32[]{:S(2)}, u32[]{:S(2)}) collective-permute-start(bf16[80,768]{1,0:T(8,128)(2,1)S(1)} %get-tuple-element.53.before_ref), channel_id=1, source_target_pairs={{0,24},{4,28},{8,16},{12,20},{16,8},{20,12},{24,0},{28,4},{1,25},{... | collective-permute-start | bytes 368648 | tf_op jit(solution)/shard_map/ppermute | solution.py:629
  76.6 1.6 %collective-permute-done.11.pb_ref = f32[64,768]{1,0:T(8,128)S(1)} collective-permute-done((f32[64,768]{1,0:T(8,128)S(1)}, f32[64,768]{1,0:T(8,128)S(1)}, u32[]{:S(2)}, u32[]{:S(2)}) %collective-permute-start.11) | collective-permute-done | bytes 196640 | tf_op jit(solution)/shard_map/ppermute | solution.py:655
  81.0 1.5 %collective-permute-start.13 = (f32[64,1024]{1,0:T(8,128)S(1)}, f32[64,1024]{1,0:T(8,128)S(1)}, u32[]{:S(2)}, u32[]{:S(2)}) collective-permute-start(f32[64,1024]{1,0:T(8,128)S(1)} %add.3.before_ref.mine_ref), channel_id=1, source_target_pairs={{0,2},{1,3},{2,0},{3,1},{4,6},{5,7},{6,4},{7,5},{8,10},{9,11},{10,... | collective-permute-start | bytes 786440 | tf_op jit(solution)/shard_map/ppermute | solution.py:671
  82.5 1.5 %collective-permute-start.18 = (bf16[80,768]{1,0:T(8,128)(2,1)S(1)}, bf16[80,768]{1,0:T(8,128)(2,1)S(1)}, u32[]{:S(2)}, u32[]{:S(2)}) collective-permute-start(bf16[80,768]{1,0:T(8,128)(2,1)S(1)} %pass_on.2.before_ref), channel_id=1, source_target_pairs={{0,16},{4,20},{8,24},{12,28},{16,0},{20,4},{24,8},{28,12},{1,17},{... | collective-permute-start | bytes 368648 | tf_op jit(solution)/shard_map/ppermute | solution.py:629
  84.0 4.4 %basis.1 = (f32[64,768]{1,0:T(8,128)}, f32[64,64]{1,0:T(8,128)S(1)}, bf16[768,384]{1,0:T(8,128)(2,1)S(1)}) custom-call(f32[64,768]{1,0:T(8,128)S(1)} %get-tuple-element.62.p_ref, bf16[80,768]{1,0:T(8,128)(2,1)S(1)} %pass_on.2.before_ref), custom_call_target="tpu_custom_call" | custom-call | flops 10000000000 | bytes 1000000 | tf_op jit(solution)/shard_map/basis/pallas_call | solution.py:67
  91.1 1.3 %collective-permute-done.18.rest_5_ = bf16[80,768]{1,0:T(8,128)(2,1)S(1)} collective-permute-done((bf16[80,768]{1,0:T(8,128)(2,1)S(1)}, bf16[80,768]{1,0:T(8,128)(2,1)S(1)}, u32[]{:S(2)}, u32[]{:S(2)}) %collective-permute-start.18) | collective-permute-done | bytes 122912 | tf_op jit(solution)/shard_map/ppermute | solution.py:629
  92.4 2.7 %new_error_last.1 = (f32[64,2048]{1,0:T(8,128)}, bf16[768,2048]{1,0:T(8,128)(2,1)}, bf16[512,768]{1,0:T(8,128)(2,1)}) custom-call(s32[1]{0:T(128)} %bitcast.core_ref, f32[64,1024]{1,0:T(8,128)S(1)} %q_half.1.q_ref.mine_ref, f32[64,1024]{1,0:T(8,128)S(1)} %collective-permute-done.14.other_ref, bf16[768,384]{1,0:T(8,128)(2,1)S(1)} %get-tuple-element.65.left_ref, ...), custom_call_target="tpu_custom_call" | custom-call | flops 10000000000 | bytes 1000000 | tf_op jit(solution)/shard_map/new_error_last/pallas_call | solution.py:67
  (52 shorter events, 11.2 us)
Async XLA Ops:
  0.6 35.2 %copy-start.5 = (bf16[1,2048,64]{1,2,0:T(8,128)(2,1)S(1)}, bf16[1,2048,64]{1,2,0:T(8,128)(2,1)}, u32[]{:S(2)}) copy-start(bf16[1,2048,64]{1,2,0:T(8,128)(2,1)} %param.13) | copy-start | bytes 786436
  0.6 35.2 %copy-start.4 = (bf16[1,1,640,768]{3,2,1,0:T(8,128)(2,1)S(1)}, bf16[1,1,640,768]{3,2,1,0:T(8,128)(2,1)}, u32[]{:S(2)}) copy-start(bf16[1,1,640,768]{3,2,1,0:T(8,128)(2,1)} %param.10) | copy-start | bytes 2949124
  2.9 15.0 %collective-permute-start = (bf16[80,2048]{1,0:T(8,128)(2,1)}, bf16[80,2048]{1,0:T(8,128)(2,1)S(1)}, u32[]{:S(2)}, u32[]{:S(2)}) collective-permute-start(bf16[80,2048]{1,0:T(8,128)(2,1)} %pack_first.1), channel_id=1, source_target_pairs={{0,28},{4,24},{8,20},{12,16},{16,12},{20,8},{24,4},{28,0},{1,29},{... | collective-permute-start | bytes 983048 | tf_op jit(solution)/shard_map/ppermute | solution.py:629
  12.3 17.8 %collective-permute-start.1 = (bf16[80,2048]{1,0:T(8,128)(2,1)}, bf16[80,2048]{1,0:T(8,128)(2,1)S(1)}, u32[]{:S(2)}, u32[]{:S(2)}) collective-permute-start(bf16[80,2048]{1,0:T(8,128)(2,1)} %get-tuple-element.39), channel_id=1, source_target_pairs={{0,12},{4,8},{8,4},{12,0},{16,28},{20,24},{24,20},{28,16},{1,13},{... | collective-permute-start | bytes 983048 | tf_op jit(solution)/shard_map/ppermute | solution.py:629
  12.4 23.4 %collective-permute-start.2 = (bf16[80,2048]{1,0:T(8,128)(2,1)}, bf16[80,2048]{1,0:T(8,128)(2,1)S(1)}, u32[]{:S(2)}, u32[]{:S(2)}) collective-permute-start(bf16[80,2048]{1,0:T(8,128)(2,1)} %get-tuple-element.40), channel_id=1, source_target_pairs={{0,8},{4,12},{8,0},{12,4},{16,24},{20,28},{24,16},{28,20},{1,9},{5... | collective-permute-start | bytes 983048 | tf_op jit(solution)/shard_map/ppermute | solution.py:629
  14.3 21.5 %collective-permute-start.3 = (bf16[80,2048]{1,0:T(8,128)(2,1)}, bf16[80,2048]{1,0:T(8,128)(2,1)S(1)}, u32[]{:S(2)}, u32[]{:S(2)}) collective-permute-start(bf16[80,2048]{1,0:T(8,128)(2,1)} %get-tuple-element.41), channel_id=1, source_target_pairs={{0,4},{4,0},{8,12},{12,8},{16,20},{20,16},{24,28},{28,24},{1,5},{5... | collective-permute-start | bytes 983048 | tf_op jit(solution)/shard_map/ppermute | solution.py:629
  15.8 32.3 %collective-permute-start.4 = (bf16[80,2048]{1,0:T(8,128)(2,1)}, bf16[80,2048]{1,0:T(8,128)(2,1)S(1)}, u32[]{:S(2)}, u32[]{:S(2)}) collective-permute-start(bf16[80,2048]{1,0:T(8,128)(2,1)} %get-tuple-element.44), channel_id=1, source_target_pairs={{0,24},{4,28},{8,16},{12,20},{16,8},{20,12},{24,0},{28,4},{1,25},{... | collective-permute-start | bytes 983048 | tf_op jit(solution)/shard_map/ppermute | solution.py:629
  17.9 44.3 %collective-permute-start.5 = (bf16[80,2048]{1,0:T(8,128)(2,1)}, bf16[80,2048]{1,0:T(8,128)(2,1)S(1)}, u32[]{:S(2)}, u32[]{:S(2)}) collective-permute-start(bf16[80,2048]{1,0:T(8,128)(2,1)} %get-tuple-element.45), channel_id=1, source_target_pairs={{0,20},{4,16},{8,28},{12,24},{16,4},{20,0},{24,12},{28,8},{1,21},{... | collective-permute-start | bytes 983048 | tf_op jit(solution)/shard_map/ppermute | solution.py:629
  30.1 38.1 %collective-permute-start.6 = (bf16[80,2048]{1,0:T(8,128)(2,1)}, bf16[80,2048]{1,0:T(8,128)(2,1)S(1)}, u32[]{:S(2)}, u32[]{:S(2)}) collective-permute-start(bf16[80,2048]{1,0:T(8,128)(2,1)} %get-tuple-element.46), channel_id=1, source_target_pairs={{0,16},{4,20},{8,24},{12,28},{16,0},{20,4},{24,8},{28,12},{1,17},{... | collective-permute-start | bytes 983048 | tf_op jit(solution)/shard_map/ppermute | solution.py:629
  40.6 8.9 %copy-start.7 = (s32[1,512]{1,0:T(1,128)S(1)}, s32[1,512]{1,0:T(1,128)}, u32[]{:S(2)}) copy-start(s32[1,512]{1,0:T(1,128)} %order_ref.3) | copy-start | bytes 6148
  40.6 8.9 %copy-start.8 = (s32[1,1,8]{2,1,0:T(1,128)S(1)}, s32[1,1,8]{2,1,0:T(1,128)}, u32[]{:S(2)}) copy-start(s32[1,1,8]{2,1,0:T(1,128)} %param.8) | copy-start | bytes 100
  40.6 27.6 %copy-start.1 = (bf16[1,768,2048]{2,1,0:T(8,128)(2,1)S(1)}, bf16[1,768,2048]{2,1,0:T(8,128)(2,1)}, u32[]{:S(2)}) copy-start(bf16[1,768,2048]{2,1,0:T(8,128)(2,1)} %param.11) | copy-start | bytes 9437188
  45.6 25.4 %collective-permute-start.8 = (bf16[80,768]{1,0:T(8,128)(2,1)S(1)}, bf16[80,768]{1,0:T(8,128)(2,1)S(1)}, u32[]{:S(2)}, u32[]{:S(2)}) collective-permute-start(bf16[80,768]{1,0:T(8,128)(2,1)S(1)} %get-tuple-element.49), channel_id=1, source_target_pairs={{0,12},{4,8},{8,4},{12,0},{16,28},{20,24},{24,20},{28,16},{1,13},{... | collective-permute-start | bytes 368648 | tf_op jit(solution)/shard_map/ppermute | solution.py:629
  48.0 23.0 %collective-permute-start.9 = (bf16[80,768]{1,0:T(8,128)(2,1)S(1)}, bf16[80,768]{1,0:T(8,128)(2,1)S(1)}, u32[]{:S(2)}, u32[]{:S(2)}) collective-permute-start(bf16[80,768]{1,0:T(8,128)(2,1)S(1)} %get-tuple-element.50), channel_id=1, source_target_pairs={{0,8},{4,12},{8,0},{12,4},{16,24},{20,28},{24,16},{28,20},{1,9},{5... | collective-permute-start | bytes 368648 | tf_op jit(solution)/shard_map/ppermute | solution.py:629
  48.1 22.9 %collective-permute-start.10 = (bf16[80,768]{1,0:T(8,128)(2,1)S(1)}, bf16[80,768]{1,0:T(8,128)(2,1)S(1)}, u32[]{:S(2)}, u32[]{:S(2)}) collective-permute-start(bf16[80,768]{1,0:T(8,128)(2,1)S(1)} %get-tuple-element.51), channel_id=1, source_target_pairs={{0,4},{4,0},{8,12},{12,8},{16,20},{20,16},{24,28},{28,24},{1,5},{5... | collective-permute-start | bytes 368648 | tf_op jit(solution)/shard_map/ppermute | solution.py:629
  69.0 2.1 %collective-permute-start.7 = (f32[64,768]{1,0:T(8,128)S(1)}, f32[64,768]{1,0:T(8,128)S(1)}, u32[]{:S(2)}, u32[]{:S(2)}) collective-permute-start(f32[64,768]{1,0:T(8,128)S(1)} %get-tuple-element.48.refs_0_.a_ref.before_ref), channel_id=1, source_target_pairs={{0,1},{1,0},{2,3},{3,2},{4,5},{5,4},{6,7},{7,6},{8,9},{9,8},{10,11... | collective-permute-start | bytes 589832 | tf_op jit(solution)/shard_map/ppermute | solution.py:654
  69.1 22.0 %collective-permute-start.15 = (bf16[80,768]{1,0:T(8,128)(2,1)S(1)}, bf16[80,768]{1,0:T(8,128)(2,1)S(1)}, u32[]{:S(2)}, u32[]{:S(2)}) collective-permute-start(bf16[80,768]{1,0:T(8,128)(2,1)S(1)} %pass_on.3), channel_id=1, source_target_pairs={{0,28},{4,24},{8,20},{12,16},{16,12},{20,8},{24,4},{28,0},{1,29},{... | collective-permute-start | bytes 368648 | tf_op jit(solution)/shard_map/ppermute | solution.py:629
  71.1 7.1 %collective-permute-start.11 = (f32[64,768]{1,0:T(8,128)S(1)}, f32[64,768]{1,0:T(8,128)S(1)}, u32[]{:S(2)}, u32[]{:S(2)}) collective-permute-start(f32[64,768]{1,0:T(8,128)S(1)} %add.2.rest_0_.pa_ref), channel_id=1, source_target_pairs={{0,2},{1,3},{2,0},{3,1},{4,6},{5,7},{6,4},{7,5},{8,10},{9,11},{10,... | collective-permute-start | bytes 589832 | tf_op jit(solution)/shard_map/ppermute | solution.py:655
  73.6 17.4 %collective-permute-start.16 = (bf16[80,768]{1,0:T(8,128)(2,1)S(1)}, bf16[80,768]{1,0:T(8,128)(2,1)S(1)}, u32[]{:S(2)}, u32[]{:S(2)}) collective-permute-start(bf16[80,768]{1,0:T(8,128)(2,1)S(1)} %get-tuple-element.53.before_ref), channel_id=1, source_target_pairs={{0,24},{4,28},{8,16},{12,20},{16,8},{20,12},{24,0},{28,4},{1,25},{... | collective-permute-start | bytes 368648 | tf_op jit(solution)/shard_map/ppermute | solution.py:629
  76.5 14.6 %collective-permute-start.17 = (bf16[80,768]{1,0:T(8,128)(2,1)S(1)}, bf16[80,768]{1,0:T(8,128)(2,1)S(1)}, u32[]{:S(2)}, u32[]{:S(2)}) collective-permute-start(bf16[80,768]{1,0:T(8,128)(2,1)S(1)} %get-tuple-element.69), channel_id=1, source_target_pairs={{0,20},{4,16},{8,28},{12,24},{16,4},{20,0},{24,12},{28,8},{1,21},{... | collective-permute-start | bytes 368648 | tf_op jit(solution)/shard_map/ppermute | solution.py:629
  79.3 1.6 %collective-permute-start.12 = (f32[64,1024]{1,0:T(8,128)S(1)}, f32[64,1024]{1,0:T(8,128)S(1)}, u32[]{:S(2)}, u32[]{:S(2)}) collective-permute-start(f32[64,1024]{1,0:T(8,128)S(1)} %get-tuple-element.59), channel_id=1, source_target_pairs={{0,1},{1,0},{2,3},{3,2},{4,5},{5,4},{6,7},{7,6},{8,9},{9,8},{10,11... | collective-permute-start | bytes 786440 | tf_op jit(solution)/shard_map/ppermute | solution.py:662
  81.0 8.6 %collective-permute-start.13 = (f32[64,1024]{1,0:T(8,128)S(1)}, f32[64,1024]{1,0:T(8,128)S(1)}, u32[]{:S(2)}, u32[]{:S(2)}) collective-permute-start(f32[64,1024]{1,0:T(8,128)S(1)} %add.3.before_ref.mine_ref), channel_id=1, source_target_pairs={{0,2},{1,3},{2,0},{3,1},{4,6},{5,7},{6,4},{7,5},{8,10},{9,11},{10,... | collective-permute-start | bytes 786440 | tf_op jit(solution)/shard_map/ppermute | solution.py:671
  82.5 9.9 %collective-permute-start.18 = (bf16[80,768]{1,0:T(8,128)(2,1)S(1)}, bf16[80,768]{1,0:T(8,128)(2,1)S(1)}, u32[]{:S(2)}, u32[]{:S(2)}) collective-permute-start(bf16[80,768]{1,0:T(8,128)(2,1)S(1)} %pass_on.2.before_ref), channel_id=1, source_target_pairs={{0,16},{4,20},{8,24},{12,28},{16,0},{20,4},{24,8},{28,12},{1,17},{... | collective-permute-start | bytes 368648 | tf_op jit(solution)/shard_map/ppermute | solution.py:629
  90.0 2.4 %collective-permute-start.14 = (f32[64,1024]{1,0:T(8,128)S(1)}, f32[64,1024]{1,0:T(8,128)S(1)}, u32[]{:S(2)}, u32[]{:S(2)}) collective-permute-start(f32[64,1024]{1,0:T(8,128)S(1)} %q_half.1.q_ref.mine_ref), channel_id=1, source_target_pairs={{0,1},{1,0},{2,3},{3,2},{4,5},{5,4},{6,7},{7,6},{8,9},{9,8},{10,11... | collective-permute-start | bytes 786440 | tf_op jit(solution)/shard_map/ppermute | solution.py:672
  (4 other events, 7.4 us)
